TPU v7x, 256 devices: a whole 4x4x8 slice. The times are simulated.
256 devices in a mesh: dp: 8 (over y, core), mp: 32 (over x, z).
Axes of the slice: x: 4, y: 4, z: 8, core: 2. Of those that a mesh axis runs over, the one named last changes fastest.
Arguments:
- tokens: bfloat16 [1024, 8192], P('dp', 'mp'), may hold values from -6 to 6
- cotangent: bfloat16 [1024, 28672], P('dp', 'mp'), may hold values from -2 to 2
- tiles: bfloat16 [2, 1344, 128, 128], P(None, 'mp'), may hold values from -0.1875 to 0.1875
- tile_rows: int32 [2, 1344], replicated, may hold values from 0 to 63, as said below
- tile_cols: int32 [2, 1344], replicated, may hold values from 0 to 223, as said below
Outputs:
- hidden: bfloat16 [1024, 28672], P('dp', 'mp')
- input_grad: bfloat16 [1024, 8192], P('dp', 'mp')
- tile_grads: float32 [2, 1344, 128, 128], P(None, 'mp')
Inputs may be any that keep to these rules, and one draw needn't show every extreme that they name: `tile_rows`: row m lists the tiles of matrix m; device k // 42 of mp owns tile k. Within one column panel of one matrix the row blocks are distinct. `tile_cols`: A column panel holds 12 or 4 tiles, the same count for all 7 panels of one holder (panels c with equal c // 7), 12 for a quarter of the holders. An owner's tiles are listed in the order of their panels. At most 3 of one owner's tiles of a matrix lie in one holder's panels, and this bound is reached in every matrix.
All inputs are finite; a program needn't handle non-finite values.
Results may differ from a plain program's by a relative error of at most 0.02.
Values may be sent and summed in bfloat16 or wider, within the bound.
No kernel may reach another device: no remote copies, remote signals or barrier semaphores. Data moves between devices by JAX's collectives and lax.ppermute only.
A program may use at most 128 MiB of HBM per device.

v0:
```python
import jax
import jax.numpy as jnp
from jax import lax
from jax.sharding import PartitionSpec as P

KHEAVY = 12


def per_device(tokens, cotangent, tiles, tile_rows, tile_cols):
    members = lax.axis_size("mp")
    myself = lax.axis_index("mp")
    tile_size = tiles.shape[-1]
    owned_count = tiles.shape[1]
    tok_rows = tokens.shape[0]
    feature_width = tokens.shape[1] * members
    row_blocks = feature_width // tile_size
    panels = cotangent.shape[1] // tile_size
    capacity = (panels * KHEAVY + members - 1) // members
    slot_count = members * capacity
    rows_all = tile_rows.reshape(2, members, owned_count)
    cols_all = tile_cols.reshape(2, members, owned_count)
    holder_all = cols_all // panels
    earlier = jnp.arange(owned_count)[:, None] > jnp.arange(owned_count)[None, :]
    same_holder = holder_all[:, :, :, None] == holder_all[:, :, None, :]
    rank_all = jnp.sum((same_holder & earlier).astype(jnp.int32), axis=3)
    my_holder = lax.dynamic_index_in_dim(holder_all, myself, 1, keepdims=False)
    my_rank = lax.dynamic_index_in_dim(rank_all, myself, 1, keepdims=False)
    slot_ids = my_holder * capacity + my_rank
    matrices = jnp.arange(2)[:, None]
    outgoing = (
        jnp.zeros((2, slot_count, tile_size, tile_size), jnp.bfloat16)
        .at[matrices, slot_ids]
        .set(tiles)
    )
    incoming = lax.all_to_all(
        outgoing.reshape(2, members, capacity, tile_size, tile_size),
        "mp",
        split_axis=1,
        concat_axis=1,
        tiled=True,
    )
    incoming = incoming.reshape(2 * slot_count, tile_size, tile_size)
    matches = (holder_all[:, :, None, :] == myself) & (
        rank_all[:, :, None, :] == jnp.arange(capacity)[None, None, :, None]
    )
    slot_rows = jnp.sum(jnp.where(matches, rows_all[:, :, None, :], 0), axis=3).reshape(
        2, slot_count
    )
    slot_cols = jnp.sum(
        jnp.where(matches, cols_all[:, :, None, :] - myself * panels, 0), axis=3
    ).reshape(2, slot_count)
    all_rows = slot_rows.reshape(-1)
    all_cols = (slot_cols + matrices * panels).reshape(-1)
    gathered = lax.all_gather(tokens, "mp", axis=1, tiled=True)
    grouped = jnp.transpose(gathered.reshape(tok_rows, row_blocks, tile_size), (1, 0, 2))
    picked = jnp.take(grouped, all_rows, axis=0)
    partial_value = jnp.einsum("sni,sij->snj", picked, incoming, preferred_element_type=jnp.float32)
    summed = jax.ops.segment_sum(partial_value, all_cols, num_segments=2 * panels)
    summed = jnp.transpose(summed.reshape(2, panels, tok_rows, tile_size), (0, 2, 1, 3)).reshape(
        2, tok_rows, panels * tile_size
    )
    gate_pre = summed[0]
    up_pre = summed[1]
    sigmoid_gate = jax.nn.sigmoid(gate_pre)
    hidden = (gate_pre * sigmoid_gate * up_pre).astype(jnp.bfloat16)
    upstream = cotangent.astype(jnp.float32)
    gate_grad = (upstream * up_pre * sigmoid_gate * (1.0 + gate_pre * (1.0 - sigmoid_gate))).astype(
        jnp.bfloat16
    )
    up_grad = (upstream * gate_pre * sigmoid_gate).astype(jnp.bfloat16)
    grad_panels = jnp.transpose(
        jnp.stack([gate_grad, up_grad]).reshape(2, tok_rows, panels, tile_size), (0, 2, 1, 3)
    )
    grad_panels = grad_panels.reshape(2 * panels, tok_rows, tile_size)
    columns = jnp.take(grad_panels, all_cols, axis=0)
    grads_slot = jnp.einsum(
        "sni,snj->sij", picked, columns, preferred_element_type=jnp.float32
    ).astype(jnp.bfloat16)
    back_terms = jnp.einsum("snj,sij->sni", columns, incoming, preferred_element_type=jnp.float32)
    input_terms = jax.ops.segment_sum(back_terms, all_rows, num_segments=row_blocks)
    stacked = grads_slot.reshape(2, members, capacity, tile_size, tile_size)
    returned = lax.all_to_all(stacked, "mp", split_axis=1, concat_axis=1, tiled=True).reshape(
        2, slot_count, tile_size, tile_size
    )
    own_grads = returned[matrices, slot_ids]
    input_terms = jnp.transpose(input_terms, (1, 0, 2)).reshape(tok_rows, feature_width)
    input_grad = lax.psum_scatter(
        input_terms.astype(jnp.bfloat16), "mp", scatter_dimension=1, tiled=True
    )
    tile_grads = lax.psum(own_grads.astype(jnp.float32).astype(jnp.bfloat16), "dp").astype(
        jnp.float32
    )
    return (hidden, input_grad, tile_grads)


def solution(mesh):
    in_specs = (P("dp", "mp"), P("dp", "mp"), P(None, "mp", None, None), P(), P())
    out_specs = (P("dp", "mp"), P("dp", "mp"), P(None, "mp", None, None))
    return jax.shard_map(
        per_device, mesh=mesh, in_specs=in_specs, out_specs=out_specs, check_vma=False
    )
```

profile of v0, /device:TPU:1, one launch (start us, length us, event | category | flops | bytes accessed | tf_op | source)
XLA Modules:
  0.0 674.7 jit_solution(216308428799732087)
XLA Ops:
  7.2 0.9 compare_and_fusion
  8.1 0.7 broadcast_subtract_fusion
  9.2 2.1 convert_reduce_fusion
  11.4 4.2 broadcast_in_dim.73
  15.7 14.3 %scatter_fusion = bf16[2,96,128,128]{3,2,1,0:T(8,128)(2,1)} fusion(bf16[2,96,128,128]{3,2,1,0:T(8,128)(2,1)} %broadcast_in_dim.73, s32[84]{0:T(128)S(1)} %reshape.274, bf16[84,128,128]{2,1,0:T(8,128)(2,1)S(1)} %bitcast.67), kind=kCustom, calls=%fused_computation.3 | custom fusion | bytes 8258208 | tf_op jit(solution)/shard_map/scatter | solution.py:33
  30.0 8.1 %copy.141 = bf16[2,32,3,128,128]{4,3,2,0,1:T(8,128)(2,1)} copy(bf16[2,32,3,128,128]{4,3,2,1,0:T(8,128)(2,1)} %bitcast.61) | data formatting | bytes 12582912 | tf_op jit(solution)/shard_map/reshape | solution.py:36
  38.1 12.1 %all-to-all-start = ((bf16[2,32,3,128,128]{4,3,2,0,1:T(8,128)(2,1)}), bf16[2,32,3,128,128]{4,3,2,0,1:T(8,128)(2,1)}, u32[]{:S(2)}, u32[]{:S(2)}) async-start(bf16[2,32,3,128,128]{4,3,2,0,1:T(8,128)(2,1)} %copy.141), calls=%async_computation | async-start | bytes 12582912 | tf_op jit(solution)/shard_map/all_to_all | solution.py:35
  50.4 0.7 copy.137
  52.9 142.2 %all-gather.2.cloned.1.call-done = bf16[128,8192]{0,1:T(8,128)(2,1)} async-done(((bf16[128,256]{0,1:T(8,128)(2,1)}), bf16[128,8192]{0,1:T(8,128)(2,1)}) %all-gather.2.cloned.1.call-update) | async-done | bytes 2097168 | tf_op jit(solution)/shard_map/all_gather | solution.py:54
  195.1 3.2 copy.138
  198.3 8.0 %gather_fusion = bf16[192,128,128]{2,1,0:T(8,128)(2,1)} fusion(bf16[64,128,128]{2,1,0:T(8,128)(2,1)S(1)} %bitcast.62, s32[1024]{0:T(1024)S(1)} %pad_clamp_fusion.1), kind=kCustom, calls=%fused_computation | custom fusion | bytes 12583680 | tf_op jit(solution)/shard_map/jit(_take)/gather | solution.py:56
  206.3 4.3 copy.142
  210.9 6.0 fusion
  217.1 25.3 %scatter_fusion.1 = f32[14,128,128]{2,1,0:T(8,128)S(1)} fusion(f32[14,128,128]{2,1,0:T(8,128)S(1)} %broadcast_in_dim.66, s32[192]{0:T(256)S(1)} %bitcast.71, f32[192,128,128]{2,1,0:T(8,128)} %fusion), kind=kCustom, calls=%fused_computation.4 | custom fusion | flops 3145728 | bytes 37749504 | tf_op jit(solution)/shard_map/scatter-add | solution.py:58
  243.5 8.1 %gather_fusion.1 = bf16[192,128,128]{2,1,0:T(8,128)(2,1)} fusion(bf16[14,128,128]{2,1,0:T(8,128)(2,1)S(1)} %bitcast.58, s32[1024]{0:T(1024)S(1)} %pad_clamp_fusion), kind=kCustom, calls=%fused_computation.1 | custom fusion | bytes 12583680 | tf_op jit(solution)/shard_map/jit(_take)/gather | solution.py:75
  251.6 10.0 %convolution_convert_fusion = bf16[192,128,128]{2,1,0:T(8,128)(2,1)} fusion(bf16[192,128,128]{2,1,0:T(8,128)(2,1)} %gather_fusion, pred[192]{0:T(512)(128)(4,1)S(1)} %get-tuple-element.40, bf16[192,128,128]{2,1,0:T(8,128)(2,1)} %gather_fusion.1, pred[192]{0:T(512)(128)(4,1)S(1)} %get-tuple-element.39), kind=kOutput, calls=%fused_computation.8 | convolution fusion | flops 814743552 | bytes 18874752 | tf_op jit(solution)/shard_map/sni,snj->sij/dot_general | solution.py:76
  261.5 8.1 %copy.150 = bf16[2,32,3,128,128]{4,3,2,0,1:T(8,128)(2,1)} copy(bf16[2,32,3,128,128]{4,3,2,1,0:T(8,128)(2,1)} %bitcast.66) | data formatting | bytes 12582912 | tf_op jit(solution)/shard_map/reshape | solution.py:81
  269.7 5.3 all-to-all-start.1
  275.0 13.7 %fusion.1 = f32[192,128,128]{2,1,0:T(8,128)} fusion(bf16[192,128,128]{2,1,0:T(8,128)(2,1)} %bitcast.60, bf16[192,128,128]{2,1,0:T(8,128)(2,1)} %gather_fusion.1, pred[192]{0:T(512)(128)(4,1)S(1)} %get-tuple-element.39), kind=kOutput, calls=%fused_computation.10 | convolution fusion | flops 808452096 | bytes 25166016 | tf_op jit(solution)/shard_map/snj,sij->sni/dot_general | solution.py:79
  288.7 2.5 broadcast_in_dim.75
  291.2 39.1 %scatter_fusion.2 = f32[64,128,128]{2,1,0:T(8,128)} fusion(f32[64,128,128]{2,1,0:T(8,128)} %broadcast_in_dim.75, s32[192]{0:T(256)S(1)} %reshape_reshape.5, f32[192,128,128]{2,1,0:T(8,128)} %fusion.1), kind=kCustom, calls=%fused_computation.5 | custom fusion | flops 3145728 | bytes 37749504 | tf_op jit(solution)/shard_map/scatter-add | solution.py:80
  330.3 2.6 convert_bitcast_fusion
  332.9 2.9 copy.148
  335.8 0.3 all-reduce.2.cloned.1.call-start
  336.2 81.4 %all-to-all-done.1 = bf16[2,32,3,128,128]{4,3,2,0,1:T(8,128)(2,1)} async-done(((bf16[2,32,3,128,128]{4,3,2,0,1:T(8,128)(2,1)}), bf16[2,32,3,128,128]{4,3,2,0,1:T(8,128)(2,1)}, u32[]{:S(2)}, u32[]{:S(2)}) %all-to-all-start.1) | async-done | bytes 6291488 | tf_op jit(solution)/shard_map/all_to_all | solution.py:82
  417.6 8.1 %copy.151 = bf16[2,32,3,128,128]{4,3,2,1,0:T(8,128)(2,1)} copy(bf16[2,32,3,128,128]{4,3,2,0,1:T(8,128)(2,1)} %all-to-all-done.1) | data formatting | bytes 12582912 | tf_op jit(solution)/shard_map/all_to_all | solution.py:82
  425.7 5.8 gather_fusion.2
  431.5 0.8 copy.152
  432.3 153.0 %reduce-scatter.2.cloned.1.call-done = bf16[128,256]{0,1:T(8,128)(2,1)} async-done(((bf16[128,8192]{0,1:T(8,128)(2,1)}), bf16[128,256]{0,1:T(8,128)(2,1)}) %reduce-scatter.2.cloned.1.call-update) | async-done | bytes 65552 | tf_op jit(solution)/shard_map/reduce_scatter | solution.py:87
  585.3 1.6 copy.153
  586.9 76.4 %all-reduce.2.cloned.1.call-done = bf16[2,42,128,128]{3,2,1,0:T(8,128)(2,1)} async-done(((bf16[2,42,128,128]{3,2,1,0:T(8,128)(2,1)}), bf16[2,42,128,128]{3,2,1,0:T(8,128)(2,1)}) %all-reduce.2.cloned.1.call-update) | async-done | bytes 2752528 | tf_op jit(solution)/shard_map/psum | solution.py:90
  663.2 5.0 convert_element_type.41
  (54 shorter events, 4.1 us)
Async XLA Ops:
  7.2 8.5 %copy-start.2 = (bf16[2,42,128,128]{3,2,1,0:T(8,128)(2,1)S(1)}, bf16[2,42,128,128]{3,2,1,0:T(8,128)(2,1)}, u32[]{:S(2)}) copy-start(bf16[2,42,128,128]{3,2,1,0:T(8,128)(2,1)} %param.7) | copy-start | bytes 8257540
  38.1 12.3 %copy-start.4 = (bf16[128,256]{1,0:T(8,128)(2,1)S(1)}, bf16[128,256]{1,0:T(8,128)(2,1)}, u32[]{:S(2)}) copy-start(bf16[128,256]{1,0:T(8,128)(2,1)} %param.5) | copy-start | bytes 196612
  38.1 13.2 %copy-start.5 = (s32[2,1344]{1,0:T(2,128)S(1)}, s32[2,1344]{1,0:T(2,128)}, u32[]{:S(2)}) copy-start(s32[2,1344]{1,0:T(2,128)} %param.8) | copy-start | bytes 32260
  38.1 14.6 %copy-start.3 = (bf16[128,896]{1,0:T(8,128)(2,1)S(1)}, bf16[128,896]{1,0:T(8,128)(2,1)}, u32[]{:S(2)}) copy-start(bf16[128,896]{1,0:T(8,128)(2,1)} %param.6) | copy-start | bytes 688132
  38.1 168.2 %all-to-all-start = ((bf16[2,32,3,128,128]{4,3,2,0,1:T(8,128)(2,1)}), bf16[2,32,3,128,128]{4,3,2,0,1:T(8,128)(2,1)}, u32[]{:S(2)}, u32[]{:S(2)}) async-start(bf16[2,32,3,128,128]{4,3,2,0,1:T(8,128)(2,1)} %copy.141), calls=%async_computation | async-start | bytes 12582912 | tf_op jit(solution)/shard_map/all_to_all | solution.py:35
  50.1 145.0 %all-gather.2.cloned.1.call-start = ((), (), s32[]{:S(2)}) async-start(), calls=%async_computation.3 | async-start | bytes 2162688 | tf_op jit(solution)/shard_map/all_gather | solution.py:54
  206.3 4.6 copy-start.1
  210.6 6.4 copy-start
  269.7 147.9 %all-to-all-start.1 = ((bf16[2,32,3,128,128]{4,3,2,0,1:T(8,128)(2,1)}), bf16[2,32,3,128,128]{4,3,2,0,1:T(8,128)(2,1)}, u32[]{:S(2)}, u32[]{:S(2)}) async-start(bf16[2,32,3,128,128]{4,3,2,0,1:T(8,128)(2,1)} %copy.150), calls=%async_computation.2 | async-start | bytes 12582912 | tf_op jit(solution)/shard_map/all_to_all | solution.py:82
  274.9 310.4 %reduce-scatter.2.cloned.1.call-start = ((), (), s32[]{:S(2)}) async-start(), calls=%async_computation.4 | async-start | bytes 2162688 | tf_op jit(solution)/shard_map/reduce_scatter | solution.py:87
  335.8 327.4 %all-reduce.2.cloned.1.call-start = ((), (), s32[]{:S(2)}) async-start(), calls=%async_computation.5 | async-start | bytes 5505024 | tf_op jit(solution)/shard_map/psum | solution.py:90
Sparse Core Ops, SparseCore 0:
  54.1 140.9 all-gather.1
  335.9 249.3 reduce-scatter.1
  588.4 74.8 all-reduce.1
where the time goes:
time: 678 us; the launch traced here: 675 us
  waiting for transfers between devices  453 us (67%)
  local copies, waits for them, and re-layouts  83.9 us (12%)
  other arithmetic  76.2 us (11%)
  matrix products  29.7 us (4%)
  starting transfers between devices  17.9 us (3%)
  between operations  14 us (2%)
    reduce_scatter x1, waiting for transfers between devices, per_device(): lax.psum_scatter(input_terms.astype(jnp.bfloat16), 'mp', scatter_dimensio...  153 us
    all_gather x1, waiting for transfers between devices, per_device(): gathered = lax.all_gather(tokens, 'mp', axis=1, tiled=True)  142 us
    all_to_all x1, waiting for transfers between devices, per_device(): lax.all_to_all(stacked, 'mp', split_axis=1, concat_axis=1, tiled=True)  81.4 us
    psum x1, waiting for transfers between devices, per_device(): lax.psum(own_grads.astype(jnp.float32).astype(jnp.bfloat16), 'dp')  76.4 us
    scatter-add x1, other arithmetic, per_device(): jax.ops.segment_sum(back_terms, all_rows, num_segments=row_blocks)  39.1 us
    scatter-add x1, other arithmetic, per_device(): jax.ops.segment_sum(partial_value, all_cols, num_segments=2 * panels)  25.3 us
    scatter x1, local copies, waits for them, and re-layouts, per_device(): outgoing = jnp.zeros((2, slot_count, tile_size, tile_size), jnp.bfloat16)...  14.3 us
    dot_general x1, matrix products, per_device(): jnp.einsum('snj,sij->sni', columns, incoming, preferred_element_type=jnp....  13.7 us
  transfers between devices with their start and end apart: 5, of which 4 were waited for; matrix products, arithmetic and copies ran while one was open for 13% of the time, Pallas kernels for 0%

commit v1 on v0

v1 whole, which is shorter than its diff:
```python
import jax
import jax.numpy as jnp
from jax import lax
from jax.experimental import pallas as pl
from jax.experimental.pallas import tpu as pltpu
from jax.sharding import PartitionSpec as P

BLOCK = 128
MOST = 12
PAIR = 3
GROUP = 4
F32 = jnp.float32
BF16 = jnp.bfloat16


def nt(a, b):
    return lax.dot_general(a, b, (((1,), (1,)), ((), ())), preferred_element_type=F32)


def nn(a, b):
    return lax.dot_general(a, b, (((1,), (0,)), ((), ())), preferred_element_type=F32)


def slot_table(tile_rows, tile_cols, me, members, panels):
    owned = tile_cols.shape[1] // members
    cols = tile_cols.reshape(2, members, owned)
    rows = tile_rows.reshape(2, members, owned)
    local = cols - me * panels
    holder = cols // panels
    pad = jnp.full((2, members, 2), -1, jnp.int32)

    def run(values):
        one = jnp.concatenate([pad[:, :, :1], values[:, :, :-1]], axis=2)
        two = jnp.concatenate([pad, values[:, :, :-2]], axis=2)
        return (values == one).astype(jnp.int32) + (values == two).astype(jnp.int32)

    rank = run(holder)
    within = run(cols)
    place = (
        jnp.arange(members)[None, :, None] * (2 * PAIR)
        + jnp.arange(2)[:, None, None] * PAIR
        + rank
    )
    value = place * 64 + rows
    mine = local[None] == jnp.arange(panels)[:, None, None, None]
    count = jnp.sum(mine.astype(jnp.int32), axis=3)
    before = jnp.arange(members)[:, None] > jnp.arange(members)[None, :]
    earlier = jnp.sum(jnp.where(before, count[:, :, None, :], 0), axis=3)
    place_in_panel = jnp.where(mine, earlier[..., None] + within[None], -1)
    hit = place_in_panel[:, :, None] == jnp.arange(MOST)[:, None, None]
    table = jnp.sum(jnp.where(hit, value[None, :, None], 0), axis=(3, 4))
    return table.reshape(-1), jnp.sum(count, axis=2).reshape(-1)


def slot_of(cols_ref, me, owned, panels, visit):
    for m in range(2):

        def step(k, carry):
            last, rank = carry
            holder = cols_ref[m, me * owned + k] // panels
            rank = jnp.where(holder == last, rank + 1, 0)
            visit(m, k, holder * (2 * PAIR) + m * PAIR + rank)
            return holder, rank

        lax.fori_loop(0, owned, step, (jnp.int32(-1), jnp.int32(0)), unroll=6)


def send_kernel(panels, place_ref, cols_ref, tiles_ref, tokens_ref, out_ref, blocks_ref):
    owned = tiles_ref.shape[1]

    def visit(m, k, slot):
        out_ref[slot] = tiles_ref[m, k]

    slot_of(cols_ref, place_ref[0], owned, panels, visit)
    for b in range(blocks_ref.shape[0]):
        blocks_ref[b] = tokens_ref[:, b * BLOCK : (b + 1) * BLOCK]


def own_kernel(panels, place_ref, cols_ref, back_ref, out_ref):
    owned = out_ref.shape[1]

    def visit(m, k, slot):
        out_ref[m, k] = back_ref[slot]

    slot_of(cols_ref, place_ref[0], owned, panels, visit)


def sort_kernel(table_ref, in_ref, out_ref):
    def step(s, carry):
        out_ref[s] = in_ref[table_ref[s] >> 6]
        return carry

    lax.fori_loop(0, out_ref.shape[0], step, 0, unroll=8)


def unsort_kernel(table_ref, count_ref, in_ref, out_ref):
    for q in range(in_ref.shape[0] // MOST):

        def step(t, carry):
            s = q * MOST + t
            out_ref[table_ref[s] >> 6] = in_ref[s]
            return carry

        lax.fori_loop(0, count_ref[q], step, 0)


def main_kernel(
    sides,
    table_ref,
    count_ref,
    where_ref,
    *refs,
):
    pieces, (tile_ref, cot_ref, hidden_ref, grad_ref) = refs[:sides], refs[sides : sides + 4]
    terms = refs[sides + 4 : 2 * sides + 4]
    tok_ref, tok_t, total, sems = refs[2 * sides + 4 :]
    p = pl.program_id(0)
    blocks = tok_ref.shape[0]
    each = blocks // sides
    side = where_ref[2]

    @pl.when(p == 0)
    def _():
        ring = pieces[0].shape[0]
        copies = [
            pltpu.make_async_copy(
                piece.at[j],
                tok_ref.at[
                    pl.ds(
                        lax.rem(side + sides - s, sides) * each
                        + lax.rem(where_ref[3] + ring - j, ring) * (each // ring),
                        each // ring,
                    )
                ],
                sems.at[s, j],
            )
            for s, piece in enumerate(pieces)
            for j in range(ring)
        ]
        for copy in copies:
            copy.start()
        for copy in copies:
            copy.wait()

        def step(b, carry):
            tok_t[b] = tok_ref[b].T
            total[b] = jnp.zeros_like(total[b])
            return carry

        lax.fori_loop(0, blocks, step, 0)

    def work(counts):
        at = [
            [table_ref[(p * 2 + m) * MOST + t] & 63 for t in range(counts[m])] for m in range(2)
        ]

        def weights(m, first):
            return tile_ref[:, m * MOST + first : m * MOST + first + GROUP]

        def stacked(m, first):
            w = weights(m, first)
            return jnp.concatenate([w[:, i].reshape(BLOCK, BLOCK) for i in range(GROUP)], axis=0)

        pre = []
        for m in range(2):
            acc = None
            for first in range(0, counts[m], GROUP):
                lhs = jnp.concatenate([tok_ref[at[m][first + i]] for i in range(GROUP)], axis=1)
                term = nn(lhs, stacked(m, first))
                acc = term if acc is None else acc + term
            pre.append(acc)
        gate, up = pre
        sig = 1.0 / (1.0 + jnp.exp(-gate))
        hidden_ref[...] = (gate * sig * up).astype(BF16)
        cot = cot_ref[...].astype(F32)
        grads = (
            (cot * up * sig * (1.0 + gate * (1.0 - sig))).astype(BF16),
            (cot * gate * sig).astype(BF16),
        )
        for m in range(2):
            for first in range(0, counts[m], GROUP):
                lhs = jnp.concatenate([tok_t[at[m][first + i]] for i in range(GROUP)], axis=0)
                out = nn(lhs, grads[m]).astype(BF16)
                back = nt(grads[m], stacked(m, first))
                for i in range(GROUP):
                    part = out[i * BLOCK : (i + 1) * BLOCK]
                    grad_ref[:, m * MOST + first + i] = part.reshape(8, BLOCK // 8, BLOCK)
                    total[at[m][first + i]] += back[:, i * BLOCK : (i + 1) * BLOCK]

    many = [count_ref[p * 2 + m] > GROUP for m in range(2)]
    for most in range(4):
        picked = [bool(most & 1), bool(most & 2)]
        same = [many[m] if picked[m] else jnp.logical_not(many[m]) for m in range(2)]

        @pl.when(jnp.logical_and(same[0], same[1]))
        def _():
            work([MOST if picked[m] else GROUP for m in range(2)])

    @pl.when(p == pl.num_programs(0) - 1)
    def _():
        for s in range(sides):
            base = lax.rem(side + s, sides) * each

            def step(b, carry):
                terms[s][b] = total[base + b].astype(BF16)
                return carry

            lax.fori_loop(0, each, step, 0)


def sum_kernel(in_ref, out_ref):
    def step(k, acc):
        return tuple(a + in_ref[k, i].astype(F32) for i, a in enumerate(acc))

    count = in_ref.shape[1]
    acc = lax.fori_loop(
        0, in_ref.shape[0], step, tuple(jnp.zeros(in_ref.shape[2:], F32) for _ in range(count))
    )
    for i in range(count):
        out_ref[:, i * BLOCK : (i + 1) * BLOCK] = acc[i].astype(BF16)


def add_kernel(*refs):
    out_ref = refs[-1]

    def step(b, carry):
        out_ref[b] = sum(r[b].astype(F32) for r in refs[:-1]).astype(BF16)
        return carry

    lax.fori_loop(0, out_ref.shape[0], step, 0)


def widen_kernel(in_ref, out_ref):
    parts, count, part, _ = in_ref.shape

    def step(i, carry):
        out_ref[i] = in_ref[:, i].reshape(parts * part, BLOCK).astype(F32)
        return carry

    lax.fori_loop(0, count, step, 0, unroll=2)


def whole(shape):
    return pl.BlockSpec(shape, lambda *_: (0,) * len(shape))


def per_device(tokens, cotangent, tiles, tile_rows, tile_cols):
    groups = lax.axis_size("dp")
    members = lax.axis_size("mp")
    me = lax.axis_index("mp")
    mygroup = lax.axis_index("dp")
    owned = tiles.shape[1]
    tok_rows, my_features = tokens.shape
    my_blocks = my_features // BLOCK
    row_blocks = my_blocks * members
    panels = cotangent.shape[1] // BLOCK
    part = BLOCK // groups
    slots = members * 2 * PAIR
    used = panels * 2 * MOST
    params = pltpu.CompilerParams(vmem_limit_bytes=48 * 1024 * 1024)
    sides = 4
    ring = members // sides
    each = row_blocks // sides
    where = jnp.stack([me, mygroup, me // ring, me % ring]).astype(jnp.int32)

    outgoing, my_tok = pl.pallas_call(
        lambda *refs: send_kernel(panels, *refs),
        out_shape=(
            jax.ShapeDtypeStruct((slots, part, BLOCK), BF16),
            jax.ShapeDtypeStruct((my_blocks, tok_rows, BLOCK), BF16),
        ),
        grid_spec=pltpu.PrefetchScalarGridSpec(
            num_scalar_prefetch=2,
            grid=(1,),
            in_specs=[
                pl.BlockSpec((2, owned, part, BLOCK), lambda i, w, c: (0, 0, w[1], 0)),
                whole(tokens.shape),
            ],
            out_specs=(whole((slots, part, BLOCK)), whole((my_blocks, tok_rows, BLOCK))),
        ),
        compiler_params=params,
        name="send_pack",
    )(where, tile_cols, tiles, tokens)

    def exchange(values):
        shape = (members, -1) + values.shape[1:]
        return lax.all_to_all(values.reshape(shape), "mp", 0, 0).reshape(values.shape)

    rows = [[x * ring + z for z in range(ring)] for x in range(sides)]

    def turn(value, s):
        pairs = [
            (x * ring + z, (x + s) % sides * ring + z) for x in range(sides) for z in range(ring)
        ]
        return lax.ppermute(value, "mp", pairs)

    def along(value, s):
        pairs = [
            (x * ring + z, x * ring + (z + s) % ring) for x in range(sides) for z in range(ring)
        ]
        return lax.ppermute(value, "mp", pairs)

    row_tok = jnp.stack([my_tok] + [along(my_tok, s) for s in range(1, ring)])
    table, count = slot_table(tile_rows, tile_cols, me, members, panels)
    incoming, row_tok = lax.optimization_barrier((exchange(outgoing), row_tok))
    ordered = pl.pallas_call(
        sort_kernel,
        out_shape=jax.ShapeDtypeStruct((used, part, BLOCK), BF16),
        grid_spec=pltpu.PrefetchScalarGridSpec(
            num_scalar_prefetch=1,
            grid=(1,),
            in_specs=[whole((slots, part, BLOCK))],
            out_specs=whole((used, part, BLOCK)),
        ),
        compiler_params=params,
        name="sort_slots",
    )(table, incoming)
    held = lax.all_gather(ordered, "dp")
    pieces = [row_tok] + [turn(row_tok, s) for s in range(1, sides)]

    per_panel = 2 * MOST
    hidden, grads, *terms = pl.pallas_call(
        lambda *refs: main_kernel(sides, *refs),
        out_shape=(
            jax.ShapeDtypeStruct(cotangent.shape, BF16),
            jax.ShapeDtypeStruct((groups, used, part, BLOCK), BF16),
        )
        + (jax.ShapeDtypeStruct((each, tok_rows, BLOCK), BF16),) * sides,
        grid_spec=pltpu.PrefetchScalarGridSpec(
            num_scalar_prefetch=3,
            grid=(panels,),
            in_specs=[pl.BlockSpec(memory_space=pl.ANY)] * sides
            + [
                pl.BlockSpec((groups, per_panel, part, BLOCK), lambda p, *_: (0, p, 0, 0)),
                pl.BlockSpec((tok_rows, BLOCK), lambda p, *_: (0, p)),
            ],
            out_specs=(
                pl.BlockSpec((tok_rows, BLOCK), lambda p, *_: (0, p)),
                pl.BlockSpec((groups, per_panel, part, BLOCK), lambda p, *_: (0, p, 0, 0)),
            )
            + (whole((each, tok_rows, BLOCK)),) * sides,
            scratch_shapes=[
                pltpu.VMEM((row_blocks, tok_rows, BLOCK), BF16),
                pltpu.VMEM((row_blocks, BLOCK, tok_rows), BF16),
                pltpu.VMEM((row_blocks, tok_rows, BLOCK), F32),
                pltpu.SemaphoreType.DMA((sides, ring)),
            ],
        ),
        compiler_params=params,
        name="gated_pair",
    )(table, count, where, *pieces, held, cotangent)

    my_grads = lax.psum_scatter(grads, "dp", scatter_dimension=0, tiled=False)
    arrived = [terms[0]] + [turn(terms[s], s) for s in range(1, sides)]
    row_terms = pl.pallas_call(
        add_kernel,
        out_shape=jax.ShapeDtypeStruct((each, tok_rows, BLOCK), BF16),
        compiler_params=params,
        name="row_sum",
    )(*arrived)
    my_grads, row_terms = lax.optimization_barrier((my_grads, row_terms))
    returning = pl.pallas_call(
        unsort_kernel,
        out_shape=jax.ShapeDtypeStruct((slots, part, BLOCK), BF16),
        grid_spec=pltpu.PrefetchScalarGridSpec(
            num_scalar_prefetch=2,
            grid=(1,),
            in_specs=[whole((used, part, BLOCK))],
            out_specs=whole((slots, part, BLOCK)),
        ),
        compiler_params=params,
        name="unsort_slots",
    )(table, count, my_grads)
    back = exchange(returning)
    own = pl.pallas_call(
        lambda *refs: own_kernel(panels, *refs),
        out_shape=jax.ShapeDtypeStruct((2, owned, part, BLOCK), BF16),
        grid_spec=pltpu.PrefetchScalarGridSpec(
            num_scalar_prefetch=2,
            grid=(1,),
            in_specs=[whole((slots, part, BLOCK))],
            out_specs=whole((2, owned, part, BLOCK)),
        ),
        compiler_params=params,
        name="own_slots",
    )(where, tile_cols, back)
    own, row_terms = lax.optimization_barrier((own, row_terms))
    full = lax.all_gather(own, "dp").reshape(groups, 2 * owned, part, BLOCK)
    column = lax.all_to_all(
        row_terms.reshape(ring, my_blocks, tok_rows, BLOCK), "mp", 0, 0, axis_index_groups=rows
    )
    input_grad = pl.pallas_call(
        sum_kernel,
        out_shape=jax.ShapeDtypeStruct(tokens.shape, BF16),
        compiler_params=params,
        name="input_sum",
    )(column)
    some = 2 * owned // 6
    tile_grads = pl.pallas_call(
        widen_kernel,
        out_shape=jax.ShapeDtypeStruct((2 * owned, BLOCK, BLOCK), F32),
        grid=(6,),
        in_specs=[pl.BlockSpec((groups, some, part, BLOCK), lambda i: (0, i, 0, 0))],
        out_specs=pl.BlockSpec((some, BLOCK, BLOCK), lambda i: (i, 0, 0)),
        compiler_params=params,
        name="widen",
    )(full).reshape(tiles.shape)
    return hidden, input_grad, tile_grads


def solution(mesh):
    in_specs = (P("dp", "mp"), P("dp", "mp"), P(None, "mp", None, None), P(), P())
    out_specs = (P("dp", "mp"), P("dp", "mp"), P(None, "mp", None, None))
    return jax.shard_map(
        per_device, mesh=mesh, in_specs=in_specs, out_specs=out_specs, check_vma=False
    )
```

time: 678 us -> 243 us (0.36)
  waiting for transfers between devices: 453 us -> 108 us
  local copies, waits for them, and re-layouts: 83.9 us -> 10 us
  other arithmetic: 76.2 us -> 4.5 us
  blocking collectives: 0 us -> 44.1 us
  matrix products: 29.7 us -> 0 us
  Pallas kernels: 0 us -> 29.5 us
  starting transfers between devices: 17.9 us -> 31.5 us
    reduce_scatter x1, waiting for transfers between devices: 153 us -> 13.3 us  [per_device(): my_grads = lax.psum_scatter(grads, 'dp', scatter_dimension=0, tiled=False)]
    all_gather x1 -> x2, waiting for transfers between devices: 142 us -> 29.1 us  [the longest x1 15.3 us: per_device(): held = lax.all_gather(ordered, 'dp')]
    all_to_all x2 -> x1, waiting for transfers between devices: 81.4 us -> 0.01 us  [exchange(): lax.all_to_all(values.reshape(shape), 'mp', 0, 0).reshape(values.shape)]
    psum x1 -> x0, waiting for transfers between devices: 76.4 us -> none  [per_device(): lax.psum(own_grads.astype(jnp.float32).astype(jnp.bfloat16), 'dp')]
    ppermute x0 -> x13, waiting for transfers between devices: none -> 65.9 us  [the longest x6 47.3 us: turn(): return lax.ppermute(value, 'mp', pairs)]
    scatter-add x2 -> x0, other arithmetic: 64.3 us -> none  [the longest x1 39.1 us: per_device(): jax.ops.segment_sum(back_terms, all_rows, num_segments=row_blocks)]
    all_to_all x0 -> x2, blocking collectives: none -> 44.1 us  [the longest x1 25.8 us: exchange(): lax.all_to_all(values.reshape(shape), 'mp', 0, 0).reshape(values.shape)]
    dot_general x3 -> x0, matrix products: 29.7 us -> none  [the longest x1 13.7 us: per_device(): jnp.einsum('snj,sij->sni', columns, incoming, preferred_element_type=jnp....]
  transfers between devices with their start and end apart: 5 -> 17, of which waited for: 4 -> 10; matrix products, arithmetic and copies ran while one was open for 13% -> 2% of each run, Pallas kernels for 0% -> 0%
where the time goes in v1:
time: 243 us; the launch traced here: 242 us
  waiting for transfers between devices  108 us (44%)
  blocking collectives  44.1 us (18%)
  starting transfers between devices  31.5 us (13%)
  Pallas kernels  29.5 us (12%)
  between operations  14 us (6%)
  local copies, waits for them, and re-layouts  10 us (4%)
  other arithmetic  4.5 us (2%)
    ppermute x6, waiting for transfers between devices, turn(): return lax.ppermute(value, 'mp', pairs)  47.3 us
    all_to_all x1, blocking collectives, exchange(): lax.all_to_all(values.reshape(shape), 'mp', 0, 0).reshape(values.shape)  25.8 us
    ppermute x7, waiting for transfers between devices, along(): return lax.ppermute(value, 'mp', pairs)  18.7 us
    all_to_all x1, blocking collectives, per_device(): lax.all_to_all(row_terms.reshape(ring, my_blocks, tok_rows, BLOCK), 'mp',...  18.3 us
    pallas_call x1, Pallas kernels, per_device(): pl.pallas_call(lambda *refs: main_kernel(sides, *refs), out_shape=(jax.Sh...  17.6 us
    ppermute x7, starting transfers between devices, along(): return lax.ppermute(value, 'mp', pairs)  17.5 us
    all_gather x1, waiting for transfers between devices, per_device(): held = lax.all_gather(ordered, 'dp')  15.3 us
    all_gather x1, waiting for transfers between devices, per_device(): full = lax.all_gather(own, 'dp').reshape(groups, 2 * owned, part, BLOCK)  13.8 us
  transfers between devices with their start and end apart: 17, of which 10 were waited for; matrix products, arithmetic and copies ran while one was open for 2% of the time, Pallas kernels for 0%

profile of v1, /device:TPU:1, one launch (start us, length us, event | category | flops | bytes accessed | tf_op | source)
XLA Modules:
  0.0 242.0 jit_solution(10527463045471432145)
XLA Ops:
  7.3 1.8 copy-done
  10.6 2.4 send_pack.1
  13.0 6.4 %collective-permute-start.6 = (bf16[2,128,128]{2,1,0:T(8,128)(2,1)S(1)}, bf16[2,128,128]{2,1,0:T(8,128)(2,1)S(1)}, u32[]{:S(2)}, u32[]{:S(2)}) collective-permute-start(bf16[2,128,128]{2,1,0:T(8,128)(2,1)S(1)} %get-tuple-element.18), channel_id=1, source_target_pairs={{0,7},{1,0},{2,1},{3,2},{4,3},{5,4},{6,5},{7,6},{8,15},{9,8},{10,9... | collective-permute-start | bytes 196616 | tf_op jit(solution)/shard_map/ppermute | solution.py:301
  19.4 1.2 collective-permute-start.5
  21.1 4.5 %collective-permute-start.3 = (bf16[2,128,128]{2,1,0:T(8,128)(2,1)S(1)}, bf16[2,128,128]{2,1,0:T(8,128)(2,1)S(1)}, u32[]{:S(2)}, u32[]{:S(2)}) collective-permute-start(bf16[2,128,128]{2,1,0:T(8,128)(2,1)S(1)} %get-tuple-element.18), channel_id=1, source_target_pairs={{0,4},{1,5},{2,6},{3,7},{4,0},{5,1},{6,2},{7,3},{8,12},{9,13},{10,... | collective-permute-start | bytes 196616 | tf_op jit(solution)/shard_map/ppermute | solution.py:301
  26.3 6.2 %all-to-all-start = ((bf16[32,6,16,128]{3,2,1,0:T(8,128)(2,1)}), bf16[32,6,16,128]{3,2,1,0:T(8,128)(2,1)S(1)}, u32[]{:S(2)}, u32[]{:S(2)}) async-start(bf16[32,6,16,128]{3,2,1,0:T(8,128)(2,1)} %bitcast.4), calls=%async_computation | async-start | bytes 1572864 | tf_op jit(solution)/shard_map/all_to_all | solution.py:287
  34.1 3.2 %select_reduce_fusion = s32[7,2,12]{2,1,0:T(2,128)S(1)} fusion(s32[2,32,42]{2,1,0:T(8,128)S(1)} %get-tuple-element.34, s32[7,2,32,42]{3,2,1,0:T(8,128)S(1)} %add_select_fusion), kind=kLoop, calls=%fused_computation | loop fusion | flops 677208 | bytes 86688 | tf_op jit(solution)/shard_map/reduce_sum | solution.py:51
  37.4 2.2 collective-permute-start.1
  39.6 13.2 %collective-permute-done.1 = bf16[2,128,128]{2,1,0:T(8,128)(2,1)S(1)} collective-permute-done((bf16[2,128,128]{2,1,0:T(8,128)(2,1)S(1)}, bf16[2,128,128]{2,1,0:T(8,128)(2,1)S(1)}, u32[]{:S(2)}, u32[]{:S(2)}) %collective-permute-start.1) | collective-permute-done | bytes 65568 | tf_op jit(solution)/shard_map/ppermute | solution.py:301
  52.8 2.1 collective-permute-start.2
  54.9 5.4 %collective-permute-done.2 = bf16[2,128,128]{2,1,0:T(8,128)(2,1)S(1)} collective-permute-done((bf16[2,128,128]{2,1,0:T(8,128)(2,1)S(1)}, bf16[2,128,128]{2,1,0:T(8,128)(2,1)S(1)}, u32[]{:S(2)}, u32[]{:S(2)}) %collective-permute-start.2) | collective-permute-done | bytes 65568 | tf_op jit(solution)/shard_map/ppermute | solution.py:301
  60.5 1.7 sort_slots.1
  62.3 1.8 collective-permute-start.9
  65.2 6.6 %collective-permute-done.9.refs_6_ = bf16[8,2,128,128]{3,2,1,0:T(8,128)(2,1)S(1)} collective-permute-done((bf16[8,2,128,128]{3,2,1,0:T(8,128)(2,1)S(1)}, bf16[8,2,128,128]{3,2,1,0:T(8,128)(2,1)S(1)}, u32[]{:S(2)}, u32[]{:S(2)}) %collective-permute-start.9) | collective-permute-done | bytes 524320 | tf_op jit(solution)/shard_map/ppermute | solution.py:295
  71.8 2.2 collective-permute-done.8.refs_5_
  73.9 16.7 %collective-permute-done.7.refs_4_ = bf16[8,2,128,128]{3,2,1,0:T(8,128)(2,1)S(1)} collective-permute-done((bf16[8,2,128,128]{3,2,1,0:T(8,128)(2,1)S(1)}, bf16[8,2,128,128]{3,2,1,0:T(8,128)(2,1)S(1)}, u32[]{:S(2)}, u32[]{:S(2)}) %collective-permute-start.7) | collective-permute-done | bytes 524320 | tf_op jit(solution)/shard_map/ppermute | solution.py:295
  90.6 15.3 %all-gather.5.cloned.1.call-done = bf16[1344,16,128]{2,1,0:T(8,128)(2,1)} async-done(((bf16[168,16,128]{2,1,0:T(8,128)(2,1)}), bf16[1344,16,128]{2,1,0:T(8,128)(2,1)}) %all-gather.5.cloned.1.call-update) | async-done | bytes 5505040 | tf_op jit(solution)/shard_map/all_gather | solution.py:318
  105.9 17.6 %gated_pair.1 = (bf16[128,896]{1,0:T(8,128)(2,1)}, bf16[8,168,16,128]{3,2,1,0:T(8,128)(2,1)}, bf16[16,128,128]{2,1,0:T(8,128)(2,1)S(1)}, bf16[16,128,128]{2,1,0:...) custom-call(s32[168]{0:T(256)S(1)} %reshape.97.table_ref.refs_0_, ...), custom_call_target="tpu_custom_call" | custom-call | tf_op jit(solution)/shard_map/gated_pair/pallas_call | solution.py:322
  127.0 2.0 collective-permute-start.10
  129.0 1.6 collective-permute-start.11
  130.6 1.2 collective-permute-start.12
  131.7 9.8 %collective-permute-done.10.refs_1_ = bf16[16,128,128]{2,1,0:T(8,128)(2,1)S(1)} collective-permute-done((bf16[16,128,128]{2,1,0:T(8,128)(2,1)S(1)}, bf16[16,128,128]{2,1,0:T(8,128)(2,1)S(1)}, u32[]{:S(2)}, u32[]{:S(2)}) %collective-permute-start.10) | collective-permute-done | bytes 524320 | tf_op jit(solution)/shard_map/ppermute | solution.py:295
  141.5 12.1 %collective-permute-done.11.refs_2_ = bf16[16,128,128]{2,1,0:T(8,128)(2,1)S(1)} collective-permute-done((bf16[16,128,128]{2,1,0:T(8,128)(2,1)S(1)}, bf16[16,128,128]{2,1,0:T(8,128)(2,1)S(1)}, u32[]{:S(2)}, u32[]{:S(2)}) %collective-permute-start.11) | collective-permute-done | bytes 524320 | tf_op jit(solution)/shard_map/ppermute | solution.py:295
  153.9 13.3 %reduce-scatter.2.cloned.1.call-done = bf16[1,168,16,128]{3,2,1,0:T(8,128)(2,1)} async-done(((bf16[8,168,16,128]{3,2,1,0:T(8,128)(2,1)}), bf16[1,168,16,128]{3,2,1,0:T(8,128)(2,1)}) %reduce-scatter.2.cloned.1.call-update) | async-done | bytes 688144 | tf_op jit(solution)/shard_map/reduce_scatter | solution.py:353
  167.3 1.1 copy-done.2
  168.4 1.0 unsort_slots.1
  169.3 25.8 %all_to_all.15 = bf16[32,6,16,128]{3,2,1,0:T(8,128)(2,1)S(1)} all-to-all(bf16[32,6,16,128]{3,2,1,0:T(8,128)(2,1)S(1)} %bitcast.34), channel_id=1, replica_groups=mesh['dp'=8,'mp'=32] {'mp'}, dimensions={0} | all-to-all | bytes 1572864 | tf_op jit(solution)/shard_map/all_to_all | solution.py:287
  195.1 2.2 own_slots.1
  197.4 18.3 %all_to_all.16.in_ref = bf16[8,2,128,128]{3,2,1,0:T(8,128)(2,1)S(1)} all-to-all(bf16[8,2,128,128]{3,2,1,0:T(8,128)(2,1)S(1)} %bitcast.37), channel_id=1, replica_groups={{0,1,2,3,4,5,6,7},{8,9,10,11,12,13,14,15},{16,17,18,19,20,21,22,23},{24..., dimensions={0} | all-to-all | bytes 1048576 | tf_op jit(solution)/shard_map/all_to_all | solution.py:389
  216.5 13.8 %all-gather.7.cloned.1.call-done = bf16[16,42,16,128]{3,2,1,0:T(8,128)(2,1)} async-done(((bf16[2,42,16,128]{3,2,1,0:T(8,128)(2,1)}), bf16[16,42,16,128]{3,2,1,0:T(8,128)(2,1)}) %all-gather.7.cloned.1.call-update) | async-done | bytes 2752528 | tf_op jit(solution)/shard_map/all_gather | solution.py:388
  230.3 1.8 copy-done.1
  232.1 3.5 %widen.1 = f32[84,128,128]{2,1,0:T(8,128)} custom-call(bf16[8,84,16,128]{3,2,1,0:T(8,128)(2,1)S(1)} %bitcast.36), custom_call_target="tpu_custom_call" | custom-call | tf_op jit(solution)/shard_map/widen/pallas_call | solution.py:399
  (66 shorter events, 10.3 us)
Async XLA Ops:
  7.2 25.4 %copy-start.5 = (s32[2,1344]{1,0:T(2,128)S(1)}, s32[2,1344]{1,0:T(2,128)}, u32[]{:S(2)}) copy-start(s32[2,1344]{1,0:T(2,128)} %refs_1_.3) | copy-start | bytes 32260
  7.2 25.6 %copy-start.13 = (s32[2,1344]{1,0:T(2,128)S(1)}, s32[2,1344]{1,0:T(2,128)}, u32[]{:S(2)}) copy-start(s32[2,1344]{1,0:T(2,128)} %param.8) | copy-start | bytes 32260
  7.3 1.8 copy-start
  9.1 0.7 copy-start.4
  9.8 0.8 copy-start.6
  13.0 47.4 %collective-permute-start.6 = (bf16[2,128,128]{2,1,0:T(8,128)(2,1)S(1)}, bf16[2,128,128]{2,1,0:T(8,128)(2,1)S(1)}, u32[]{:S(2)}, u32[]{:S(2)}) collective-permute-start(bf16[2,128,128]{2,1,0:T(8,128)(2,1)S(1)} %get-tuple-element.18), channel_id=1, source_target_pairs={{0,7},{1,0},{2,1},{3,2},{4,3},{5,4},{6,5},{7,6},{8,15},{9,8},{10,9... | collective-permute-start | bytes 196616 | tf_op jit(solution)/shard_map/ppermute | solution.py:301
  19.4 41.0 %collective-permute-start.5 = (bf16[2,128,128]{2,1,0:T(8,128)(2,1)S(1)}, bf16[2,128,128]{2,1,0:T(8,128)(2,1)S(1)}, u32[]{:S(2)}, u32[]{:S(2)}) collective-permute-start(bf16[2,128,128]{2,1,0:T(8,128)(2,1)S(1)} %get-tuple-element.18), channel_id=1, source_target_pairs={{0,6},{1,7},{2,0},{3,1},{4,2},{5,3},{6,4},{7,5},{8,14},{9,15},{10,... | collective-permute-start | bytes 196616 | tf_op jit(solution)/shard_map/ppermute | solution.py:301
  20.6 39.8 %collective-permute-start.4 = (bf16[2,128,128]{2,1,0:T(8,128)(2,1)S(1)}, bf16[2,128,128]{2,1,0:T(8,128)(2,1)S(1)}, u32[]{:S(2)}, u32[]{:S(2)}) collective-permute-start(bf16[2,128,128]{2,1,0:T(8,128)(2,1)S(1)} %get-tuple-element.18), channel_id=1, source_target_pairs={{0,5},{1,6},{2,7},{3,0},{4,1},{5,2},{6,3},{7,4},{8,13},{9,14},{10,... | collective-permute-start | bytes 196616 | tf_op jit(solution)/shard_map/ppermute | solution.py:301
  21.1 39.3 %collective-permute-start.3 = (bf16[2,128,128]{2,1,0:T(8,128)(2,1)S(1)}, bf16[2,128,128]{2,1,0:T(8,128)(2,1)S(1)}, u32[]{:S(2)}, u32[]{:S(2)}) collective-permute-start(bf16[2,128,128]{2,1,0:T(8,128)(2,1)S(1)} %get-tuple-element.18), channel_id=1, source_target_pairs={{0,4},{1,5},{2,6},{3,7},{4,0},{5,1},{6,2},{7,3},{8,12},{9,13},{10,... | collective-permute-start | bytes 196616 | tf_op jit(solution)/shard_map/ppermute | solution.py:301
  25.5 11.8 %collective-permute-start = (bf16[2,128,128]{2,1,0:T(8,128)(2,1)S(1)}, bf16[2,128,128]{2,1,0:T(8,128)(2,1)S(1)}, u32[]{:S(2)}, u32[]{:S(2)}) collective-permute-start(bf16[2,128,128]{2,1,0:T(8,128)(2,1)S(1)} %get-tuple-element.18), channel_id=1, source_target_pairs={{0,1},{1,2},{2,3},{3,4},{4,5},{5,6},{6,7},{7,0},{8,9},{9,10},{10,1... | collective-permute-start | bytes 196616 | tf_op jit(solution)/shard_map/ppermute | solution.py:301
  26.3 79.7 %copy-start.3 = (bf16[128,896]{1,0:T(8,128)(2,1)S(1)}, bf16[128,896]{1,0:T(8,128)(2,1)}, u32[]{:S(2)}) copy-start(bf16[128,896]{1,0:T(8,128)(2,1)} %refs_8_.1) | copy-start | bytes 688132
  26.3 34.2 %all-to-all-start = ((bf16[32,6,16,128]{3,2,1,0:T(8,128)(2,1)}), bf16[32,6,16,128]{3,2,1,0:T(8,128)(2,1)S(1)}, u32[]{:S(2)}, u32[]{:S(2)}) async-start(bf16[32,6,16,128]{3,2,1,0:T(8,128)(2,1)} %bitcast.4), calls=%async_computation | async-start | bytes 1572864 | tf_op jit(solution)/shard_map/all_to_all | solution.py:287
  32.5 73.5 %all-gather.5.cloned.1.call-start = ((), (), s32[]{:S(2)}) async-start(), calls=%async_computation.5 | async-start | bytes 6193152 | tf_op jit(solution)/shard_map/all_gather | solution.py:318
  37.4 15.4 %collective-permute-start.1 = (bf16[2,128,128]{2,1,0:T(8,128)(2,1)S(1)}, bf16[2,128,128]{2,1,0:T(8,128)(2,1)S(1)}, u32[]{:S(2)}, u32[]{:S(2)}) collective-permute-start(bf16[2,128,128]{2,1,0:T(8,128)(2,1)S(1)} %get-tuple-element.18), channel_id=1, source_target_pairs={{0,2},{1,3},{2,4},{3,5},{4,6},{5,7},{6,0},{7,1},{8,10},{9,11},{10,... | collective-permute-start | bytes 196616 | tf_op jit(solution)/shard_map/ppermute | solution.py:301
  52.8 7.5 %collective-permute-start.2 = (bf16[2,128,128]{2,1,0:T(8,128)(2,1)S(1)}, bf16[2,128,128]{2,1,0:T(8,128)(2,1)S(1)}, u32[]{:S(2)}, u32[]{:S(2)}) collective-permute-start(bf16[2,128,128]{2,1,0:T(8,128)(2,1)S(1)} %get-tuple-element.18), channel_id=1, source_target_pairs={{0,3},{1,4},{2,5},{3,6},{4,7},{5,0},{6,1},{7,2},{8,11},{9,12},{10,... | collective-permute-start | bytes 196616 | tf_op jit(solution)/shard_map/ppermute | solution.py:301
  62.2 105.0 %reduce-scatter.2.cloned.1.call-start = ((), (), s32[]{:S(2)}) async-start(), calls=%async_computation.4 | async-start | bytes 6193152 | tf_op jit(solution)/shard_map/reduce_scatter | solution.py:353
  62.3 9.5 %collective-permute-start.9 = (bf16[8,2,128,128]{3,2,1,0:T(8,128)(2,1)S(1)}, bf16[8,2,128,128]{3,2,1,0:T(8,128)(2,1)S(1)}, u32[]{:S(2)}, u32[]{:S(2)}) collective-permute-start(bf16[8,2,128,128]{3,2,1,0:T(8,128)(2,1)S(1)} %bitcast_dynamic-update-slice_fusion.refs_3_), channel_id=1, source_target_pairs={{0,24},{1,25},{2,26},{3,27},{4,28},{5,29},{6,30},{7,31},{8,0},{9,1... | collective-permute-start | bytes 1572872 | tf_op jit(solution)/shard_map/ppermute | solution.py:295
  64.0 9.9 %collective-permute-start.8 = (bf16[8,2,128,128]{3,2,1,0:T(8,128)(2,1)S(1)}, bf16[8,2,128,128]{3,2,1,0:T(8,128)(2,1)S(1)}, u32[]{:S(2)}, u32[]{:S(2)}) collective-permute-start(bf16[8,2,128,128]{3,2,1,0:T(8,128)(2,1)S(1)} %bitcast_dynamic-update-slice_fusion.refs_3_), channel_id=1, source_target_pairs={{0,16},{1,17},{2,18},{3,19},{4,20},{5,21},{6,22},{7,23},{8,24},{9,... | collective-permute-start | bytes 1572872 | tf_op jit(solution)/shard_map/ppermute | solution.py:295
  64.5 26.1 %collective-permute-start.7 = (bf16[8,2,128,128]{3,2,1,0:T(8,128)(2,1)S(1)}, bf16[8,2,128,128]{3,2,1,0:T(8,128)(2,1)S(1)}, u32[]{:S(2)}, u32[]{:S(2)}) collective-permute-start(bf16[8,2,128,128]{3,2,1,0:T(8,128)(2,1)S(1)} %bitcast_dynamic-update-slice_fusion.refs_3_), channel_id=1, source_target_pairs={{0,8},{1,9},{2,10},{3,11},{4,12},{5,13},{6,14},{7,15},{8,16},{9,17... | collective-permute-start | bytes 1572872 | tf_op jit(solution)/shard_map/ppermute | solution.py:295
  123.5 0.8 copy-start.7
  124.3 0.8 copy-start.9
  125.1 0.8 copy-start.11
  125.9 1.0 copy-start.12
  125.9 3.0 %copy-start.10 = (bf16[16,128,128]{2,1,0:T(8,128)(2,1)S(1)}, bf16[16,128,128]{2,1,0:T(8,128)(2,1)}, u32[]{:S(2)}) copy-start(bf16[16,128,128]{2,1,0:T(8,128)(2,1)} %copy-done.9) | copy-start | bytes 1572868
  125.9 4.6 %copy-start.8 = (bf16[16,128,128]{2,1,0:T(8,128)(2,1)S(1)}, bf16[16,128,128]{2,1,0:T(8,128)(2,1)}, u32[]{:S(2)}) copy-start(bf16[16,128,128]{2,1,0:T(8,128)(2,1)} %copy-done.7) | copy-start | bytes 1572868
  125.9 104.3 %all-gather.7.cloned.1.call-start = ((), (), s32[]{:S(2)}) async-start(), calls=%async_computation.6 | async-start | bytes 3096576 | tf_op jit(solution)/shard_map/all_gather | solution.py:388
  127.0 14.6 %collective-permute-start.10 = (bf16[16,128,128]{2,1,0:T(8,128)(2,1)S(1)}, bf16[16,128,128]{2,1,0:T(8,128)(2,1)S(1)}, u32[]{:S(2)}, u32[]{:S(2)}) collective-permute-start(bf16[16,128,128]{2,1,0:T(8,128)(2,1)S(1)} %copy-done.12), channel_id=1, source_target_pairs={{0,8},{1,9},{2,10},{3,11},{4,12},{5,13},{6,14},{7,15},{8,16},{9,17... | collective-permute-start | bytes 1572872 | tf_op jit(solution)/shard_map/ppermute | solution.py:295
  129.0 24.6 %collective-permute-start.11 = (bf16[16,128,128]{2,1,0:T(8,128)(2,1)S(1)}, bf16[16,128,128]{2,1,0:T(8,128)(2,1)S(1)}, u32[]{:S(2)}, u32[]{:S(2)}) collective-permute-start(bf16[16,128,128]{2,1,0:T(8,128)(2,1)S(1)} %copy-done.10), channel_id=1, source_target_pairs={{0,16},{1,17},{2,18},{3,19},{4,20},{5,21},{6,22},{7,23},{8,24},{9,... | collective-permute-start | bytes 1572872 | tf_op jit(solution)/shard_map/ppermute | solution.py:295
  130.6 23.0 %collective-permute-start.12 = (bf16[16,128,128]{2,1,0:T(8,128)(2,1)S(1)}, bf16[16,128,128]{2,1,0:T(8,128)(2,1)S(1)}, u32[]{:S(2)}, u32[]{:S(2)}) collective-permute-start(bf16[16,128,128]{2,1,0:T(8,128)(2,1)S(1)} %copy-done.8), channel_id=1, source_target_pairs={{0,24},{1,25},{2,26},{3,27},{4,28},{5,29},{6,30},{7,31},{8,0},{9,1... | collective-permute-start | bytes 1572872 | tf_op jit(solution)/shard_map/ppermute | solution.py:295
  167.3 1.1 copy-start.2
  230.3 1.8 copy-start.1
Sparse Core Ops, SparseCore 0:
  62.3 43.5 all-gather.4
  126.1 41.1 reduce-scatter.1
  197.5 32.7 all-gather.6

commit v2 on v1

--- a/solution.py
+++ b/solution.py
@@ -106,14 +106,16 @@
 
 def main_kernel(
     sides,
+    ring,
     table_ref,
     count_ref,
     where_ref,
     *refs,
 ):
-    pieces, (tile_ref, cot_ref, hidden_ref, grad_ref) = refs[:sides], refs[sides : sides + 4]
-    terms = refs[sides + 4 : 2 * sides + 4]
-    tok_ref, tok_t, total, sems = refs[2 * sides + 4 :]
+    pieces, refs = refs[: ring + 1], refs[ring + 1 :]
+    tile_ref, cot_ref, hidden_ref, grad_ref, *refs = refs
+    terms = refs[:sides]
+    tok_ref, tok_t, total, sems = refs[sides:]
     p = pl.program_id(0)
     blocks = tok_ref.shape[0]
     each = blocks // sides
@@ -121,10 +123,16 @@
 
     @pl.when(p == 0)
     def _():
-        ring = pieces[0].shape[0]
+        steps = [j for j in range(ring) if j != ring // 2]
+        held = [(j, s, piece.at[s]) for j, piece in zip(steps, pieces) for s in range(sides)]
+        held += [
+            (ring // 2, k * sides // 2 + s, piece.at[s])
+            for k, piece in enumerate(pieces[-2:])
+            for s in range(sides // 2)
+        ]
         copies = [
             pltpu.make_async_copy(
-                piece.at[j],
+                piece,
                 tok_ref.at[
                     pl.ds(
                         lax.rem(side + sides - s, sides) * each
@@ -134,8 +142,7 @@
                 ],
                 sems.at[s, j],
             )
-            for s, piece in enumerate(pieces)
-            for j in range(ring)
+            for j, s, piece in held
         ]
         for copy in copies:
             copy.start()
@@ -258,6 +265,7 @@
     slots = members * 2 * PAIR
     used = panels * 2 * MOST
     params = pltpu.CompilerParams(vmem_limit_bytes=48 * 1024 * 1024)
+    alone = pltpu.CompilerParams(vmem_limit_bytes=60 * 1024 * 1024)
     sides = 4
     ring = members // sides
     each = row_blocks // sides
@@ -278,7 +286,7 @@
             ],
             out_specs=(whole((slots, part, BLOCK)), whole((my_blocks, tok_rows, BLOCK))),
         ),
-        compiler_params=params,
+        compiler_params=alone,
         name="send_pack",
     )(where, tile_cols, tiles, tokens)
 
@@ -300,9 +308,9 @@
         ]
         return lax.ppermute(value, "mp", pairs)
 
-    row_tok = jnp.stack([my_tok] + [along(my_tok, s) for s in range(1, ring)])
+    line_tok = jnp.stack([my_tok] + [turn(my_tok, s) for s in range(1, sides)])
     table, count = slot_table(tile_rows, tile_cols, me, members, panels)
-    incoming, row_tok = lax.optimization_barrier((exchange(outgoing), row_tok))
+    incoming, line_tok = lax.optimization_barrier((exchange(outgoing), line_tok))
     ordered = pl.pallas_call(
         sort_kernel,
         out_shape=jax.ShapeDtypeStruct((used, part, BLOCK), BF16),
@@ -316,11 +324,16 @@
         name="sort_slots",
     )(table, incoming)
     held = lax.all_gather(ordered, "dp")
-    pieces = [row_tok] + [turn(row_tok, s) for s in range(1, sides)]
+    ups, downs = [line_tok], [line_tok]
+    for _ in range(ring // 2 - 1):
+        ups.append(along(ups[-1], 1))
+        downs.append(along(downs[-1], -1))
+    far = [along(ups[-1][: sides // 2], 1), along(downs[-1][sides // 2 :], -1)]
+    pieces = ups + downs[:0:-1] + far
 
     per_panel = 2 * MOST
     hidden, grads, *terms = pl.pallas_call(
-        lambda *refs: main_kernel(sides, *refs),
+        lambda *refs: main_kernel(sides, ring, *refs),
         out_shape=(
             jax.ShapeDtypeStruct(cotangent.shape, BF16),
             jax.ShapeDtypeStruct((groups, used, part, BLOCK), BF16),
@@ -329,7 +342,7 @@
         grid_spec=pltpu.PrefetchScalarGridSpec(
             num_scalar_prefetch=3,
             grid=(panels,),
-            in_specs=[pl.BlockSpec(memory_space=pl.ANY)] * sides
+            in_specs=[pl.BlockSpec(memory_space=pl.ANY)] * len(pieces)
             + [
                 pl.BlockSpec((groups, per_panel, part, BLOCK), lambda p, *_: (0, p, 0, 0)),
                 pl.BlockSpec((tok_rows, BLOCK), lambda p, *_: (0, p)),
@@ -346,7 +359,7 @@
                 pltpu.SemaphoreType.DMA((sides, ring)),
             ],
         ),
-        compiler_params=params,
+        compiler_params=alone,
         name="gated_pair",
     )(table, count, where, *pieces, held, cotangent)
 

time: 243 us -> 222 us (0.914)
  waiting for transfers between devices: 108 us -> 94.3 us
  local copies, waits for them, and re-layouts: 10 us -> 4.77 us
  starting transfers between devices: 31.5 us -> 28.1 us
    ppermute x6, waiting for transfers between devices: 47.3 us -> 21.3 us  [turn(): return lax.ppermute(value, 'mp', pairs)]
    all_to_all x1, waiting for transfers between devices: 0.01 us -> 13 us  [exchange(): lax.all_to_all(values.reshape(shape), 'mp', 0, 0).reshape(values.shape)]
    ppermute x7 -> x8, starting transfers between devices: 17.5 us -> 8.34 us  [along(): return lax.ppermute(value, 'mp', pairs)]
    unnamed x35 -> x42, local copies, waits for them, and re-layouts: 9.65 us -> 3.86 us
    all_gather x1, waiting for transfers between devices: 15.3 us -> 11 us  [per_device(): held = lax.all_gather(ordered, 'dp')]
    all_to_all x1, starting transfers between devices: 6.2 us -> 10.4 us  [exchange(): lax.all_to_all(values.reshape(shape), 'mp', 0, 0).reshape(values.shape)]
    ppermute x7 -> x8, waiting for transfers between devices: 18.7 us -> 22 us  [along(): return lax.ppermute(value, 'mp', pairs)]
  transfers between devices with their start and end apart: 17 -> 18, of which waited for: 10 -> 14; matrix products, arithmetic and copies ran while one was open for 2% -> 3% of each run, Pallas kernels for 0% -> 1%
where the time goes in v2:
time: 222 us; the launch traced here: 221 us
  waiting for transfers between devices  94.3 us (42%)
  blocking collectives  43.6 us (20%)
  Pallas kernels  30.7 us (14%)
  starting transfers between devices  28.1 us (13%)
  between operations  14.1 us (6%)
  other arithmetic  5.9 us (3%)
  local copies, waits for them, and re-layouts  4.77 us (2%)
    all_to_all x1, blocking collectives, exchange(): lax.all_to_all(values.reshape(shape), 'mp', 0, 0).reshape(values.shape)  25.1 us
    ppermute x8, waiting for transfers between devices, along(): return lax.ppermute(value, 'mp', pairs)  22 us
    ppermute x6, waiting for transfers between devices, turn(): return lax.ppermute(value, 'mp', pairs)  21.3 us
    all_to_all x1, blocking collectives, per_device(): lax.all_to_all(row_terms.reshape(ring, my_blocks, tok_rows, BLOCK), 'mp',...  18.5 us
    pallas_call x1, Pallas kernels, per_device(): pl.pallas_call(lambda *refs: main_kernel(sides, ring, *refs), out_shape=(...  17.5 us
    all_gather x1, waiting for transfers between devices, per_device(): full = lax.all_gather(own, 'dp').reshape(groups, 2 * owned, part, BLOCK)  13.9 us
    reduce_scatter x1, waiting for transfers between devices, per_device(): my_grads = lax.psum_scatter(grads, 'dp', scatter_dimension=0, tiled=False)  13.1 us
    all_to_all x1, waiting for transfers between devices, exchange(): lax.all_to_all(values.reshape(shape), 'mp', 0, 0).reshape(values.shape)  13 us
  transfers between devices with their start and end apart: 18, of which 14 were waited for; matrix products, arithmetic and copies ran while one was open for 3% of the time, Pallas kernels for 1%

profile of v2, /device:TPU:1, one launch (start us, length us, event | category | flops | bytes accessed | tf_op | source)
XLA Modules:
  0.0 221.4 jit_solution(11312115795833909812)
XLA Ops:
  7.8 3.4 %send_pack.1 = (bf16[192,16,128]{2,1,0:T(8,128)(2,1)}, bf16[2,128,128]{2,1,0:T(8,128)(2,1)}) custom-call(s32[4]{0:T(128)} %pad_add_fusion.refs_0_.refs_2_, s32[2,1344]{1,0:T(2,128)} %refs_1_.3, bf16[2,42,128,128]{3,2,1,0:T(8,128)(2,1)} %refs_2_.1, bf16[128,256]{1,0:T(8,128)(2,1)} %refs_3_.1), custom_call_target="tpu_custom_call" | custom-call | tf_op jit(solution)/shard_map/send_pack/pallas_call | solution.py:274
  11.2 3.3 %collective-permute-start.2 = (bf16[2,128,128]{2,1,0:T(8,128)(2,1)}, bf16[2,128,128]{2,1,0:T(8,128)(2,1)S(1)}, u32[]{:S(2)}, u32[]{:S(2)}) collective-permute-start(bf16[2,128,128]{2,1,0:T(8,128)(2,1)} %get-tuple-element.18), channel_id=1, source_target_pairs={{0,24},{1,25},{2,26},{3,27},{4,28},{5,29},{6,30},{7,31},{8,0},{9,1... | collective-permute-start | bytes 196616 | tf_op jit(solution)/shard_map/ppermute | solution.py:303
  15.6 10.4 %all-to-all-start = ((bf16[32,6,16,128]{3,2,1,0:T(8,128)(2,1)}), bf16[32,6,16,128]{3,2,1,0:T(8,128)(2,1)S(1)}, u32[]{:S(2)}, u32[]{:S(2)}) async-start(bf16[32,6,16,128]{3,2,1,0:T(8,128)(2,1)} %bitcast.31), calls=%async_computation | async-start | bytes 1572864 | tf_op jit(solution)/shard_map/all_to_all | solution.py:295
  27.6 3.2 %select_reduce_fusion = s32[7,2,12]{2,1,0:T(2,128)S(1)} fusion(s32[2,32,42]{2,1,0:T(8,128)S(1)} %get-tuple-element.34, s32[7,2,32,42]{3,2,1,0:T(8,128)S(1)} %add_select_fusion), kind=kLoop, calls=%fused_computation | loop fusion | flops 677208 | bytes 86688 | tf_op jit(solution)/shard_map/reduce_sum | solution.py:51
  30.9 0.9 pad_maximum_fusion.refs_3_
  31.8 13.0 %all-to-all-done = bf16[32,6,16,128]{3,2,1,0:T(8,128)(2,1)S(1)} async-done(((bf16[32,6,16,128]{3,2,1,0:T(8,128)(2,1)}), bf16[32,6,16,128]{3,2,1,0:T(8,128)(2,1)S(1)}, u32[]{:S(2)}, u32[]{:S(2)}) %all-to-all-start) | async-done | bytes 786464 | tf_op jit(solution)/shard_map/all_to_all | solution.py:295
  44.8 1.7 sort_slots.1
  46.6 2.5 %collective-permute-start.6 = (bf16[4,2,128,128]{3,2,1,0:T(8,128)(2,1)S(1)}, bf16[4,2,128,128]{3,2,1,0:T(8,128)(2,1)S(1)}, u32[]{:S(2)}, u32[]{:S(2)}) collective-permute-start(bf16[4,2,128,128]{3,2,1,0:T(8,128)(2,1)S(1)} %pad_maximum_fusion.refs_3_), channel_id=1, source_target_pairs={{0,7},{1,0},{2,1},{3,2},{4,3},{5,4},{6,5},{7,6},{8,15},{9,8},{10,9... | collective-permute-start | bytes 786440 | tf_op jit(solution)/shard_map/ppermute | solution.py:309
  49.9 3.7 %collective-permute-done.6.refs_9_ = bf16[4,2,128,128]{3,2,1,0:T(8,128)(2,1)S(1)} collective-permute-done((bf16[4,2,128,128]{3,2,1,0:T(8,128)(2,1)S(1)}, bf16[4,2,128,128]{3,2,1,0:T(8,128)(2,1)S(1)}, u32[]{:S(2)}, u32[]{:S(2)}) %collective-permute-start.6) | collective-permute-done | bytes 262176 | tf_op jit(solution)/shard_map/ppermute | solution.py:309
  53.6 1.9 collective-permute-start.7
  55.5 5.1 %collective-permute-done.7.refs_8_ = bf16[4,2,128,128]{3,2,1,0:T(8,128)(2,1)S(1)} collective-permute-done((bf16[4,2,128,128]{3,2,1,0:T(8,128)(2,1)S(1)}, bf16[4,2,128,128]{3,2,1,0:T(8,128)(2,1)S(1)}, u32[]{:S(2)}, u32[]{:S(2)}) %collective-permute-start.7) | collective-permute-done | bytes 262176 | tf_op jit(solution)/shard_map/ppermute | solution.py:309
  60.6 1.5 collective-permute-start.8
  62.4 6.5 %collective-permute-done.8.refs_7_ = bf16[4,2,128,128]{3,2,1,0:T(8,128)(2,1)S(1)} collective-permute-done((bf16[4,2,128,128]{3,2,1,0:T(8,128)(2,1)S(1)}, bf16[4,2,128,128]{3,2,1,0:T(8,128)(2,1)S(1)}, u32[]{:S(2)}, u32[]{:S(2)}) %collective-permute-start.8) | collective-permute-done | bytes 262176 | tf_op jit(solution)/shard_map/ppermute | solution.py:309
  68.9 1.5 collective-permute-start.10
  71.4 2.8 %collective-permute-done.10.refs_11_ = bf16[2,2,128,128]{3,2,1,0:T(8,128)(2,1)S(1)} collective-permute-done((bf16[2,2,128,128]{3,2,1,0:T(8,128)(2,1)S(1)}, bf16[2,2,128,128]{3,2,1,0:T(8,128)(2,1)S(1)}, u32[]{:S(2)}, u32[]{:S(2)}) %collective-permute-start.10) | collective-permute-done | bytes 131104 | tf_op jit(solution)/shard_map/ppermute | solution.py:309
  74.2 3.4 %collective-permute-done.9.refs_10_ = bf16[2,2,128,128]{3,2,1,0:T(8,128)(2,1)S(1)} collective-permute-done((bf16[2,2,128,128]{3,2,1,0:T(8,128)(2,1)S(1)}, bf16[2,2,128,128]{3,2,1,0:T(8,128)(2,1)S(1)}, u32[]{:S(2)}, u32[]{:S(2)}) %collective-permute-start.9) | collective-permute-done | bytes 131104 | tf_op jit(solution)/shard_map/ppermute | solution.py:309
  77.6 11.0 %all-gather.5.cloned.1.call-done = bf16[1344,16,128]{2,1,0:T(8,128)(2,1)} async-done(((bf16[168,16,128]{2,1,0:T(8,128)(2,1)}), bf16[1344,16,128]{2,1,0:T(8,128)(2,1)}) %all-gather.5.cloned.1.call-update) | async-done | bytes 5505040 | tf_op jit(solution)/shard_map/all_gather | solution.py:326
  88.6 17.5 %gated_pair.1 = (bf16[128,896]{1,0:T(8,128)(2,1)}, bf16[8,168,16,128]{3,2,1,0:T(8,128)(2,1)}, bf16[16,128,128]{2,1,0:T(8,128)(2,1)}, bf16[16,128,128]{2,1,0:T(8,...) custom-call(s32[168]{0:T(256)} %copy-done.4, s32[14]{0:T(128)} %reshape.98.refs_1_.count_ref, ...), custom_call_target="tpu_custom_call" | custom-call | tf_op jit(solution)/shard_map/gated_pair/pallas_call | solution.py:335
  106.2 0.9 copy-done.20
  107.5 2.5 %collective-permute-start.12 = (bf16[16,128,128]{2,1,0:T(8,128)(2,1)S(1)}, bf16[16,128,128]{2,1,0:T(8,128)(2,1)S(1)}, u32[]{:S(2)}, u32[]{:S(2)}) collective-permute-start(bf16[16,128,128]{2,1,0:T(8,128)(2,1)S(1)} %copy-done.19), channel_id=1, source_target_pairs={{0,16},{1,17},{2,18},{3,19},{4,20},{5,21},{6,22},{7,23},{8,24},{9,... | collective-permute-start | bytes 1572872 | tf_op jit(solution)/shard_map/ppermute | solution.py:303
  110.0 1.9 collective-permute-start.13
  111.9 9.8 %collective-permute-done.11.refs_1_ = bf16[16,128,128]{2,1,0:T(8,128)(2,1)S(1)} collective-permute-done((bf16[16,128,128]{2,1,0:T(8,128)(2,1)S(1)}, bf16[16,128,128]{2,1,0:T(8,128)(2,1)S(1)}, u32[]{:S(2)}, u32[]{:S(2)}) %collective-permute-start.11) | collective-permute-done | bytes 524320 | tf_op jit(solution)/shard_map/ppermute | solution.py:303
  121.7 11.2 %collective-permute-done.12.refs_2_ = bf16[16,128,128]{2,1,0:T(8,128)(2,1)S(1)} collective-permute-done((bf16[16,128,128]{2,1,0:T(8,128)(2,1)S(1)}, bf16[16,128,128]{2,1,0:T(8,128)(2,1)S(1)}, u32[]{:S(2)}, u32[]{:S(2)}) %collective-permute-start.12) | collective-permute-done | bytes 524320 | tf_op jit(solution)/shard_map/ppermute | solution.py:303
  133.6 13.1 %reduce-scatter.2.cloned.1.call-done = bf16[1,168,16,128]{3,2,1,0:T(8,128)(2,1)} async-done(((bf16[8,168,16,128]{3,2,1,0:T(8,128)(2,1)}), bf16[1,168,16,128]{3,2,1,0:T(8,128)(2,1)}) %reduce-scatter.2.cloned.1.call-update) | async-done | bytes 688144 | tf_op jit(solution)/shard_map/reduce_scatter | solution.py:366
  146.7 1.1 copy-done.1
  147.8 1.3 unsort_slots.1
  149.1 25.1 %all_to_all.15 = bf16[32,6,16,128]{3,2,1,0:T(8,128)(2,1)S(1)} all-to-all(bf16[32,6,16,128]{3,2,1,0:T(8,128)(2,1)S(1)} %bitcast.22), channel_id=1, replica_groups=mesh['dp'=8,'mp'=32] {'mp'}, dimensions={0} | all-to-all | bytes 1572864 | tf_op jit(solution)/shard_map/all_to_all | solution.py:295
  174.3 2.2 %own_slots.1 = bf16[2,42,16,128]{3,2,1,0:T(8,128)(2,1)} custom-call(s32[4]{0:T(128)S(1)} %copy-done.6, s32[2,1344]{1,0:T(2,128)S(1)} %copy-done.3, bf16[192,16,128]{2,1,0:T(8,128)(2,1)S(1)} %bitcast.23), custom_call_target="tpu_custom_call" | custom-call | tf_op jit(solution)/shard_map/own_slots/pallas_call | solution.py:388
  176.5 18.5 %all_to_all.16.in_ref = bf16[8,2,128,128]{3,2,1,0:T(8,128)(2,1)S(1)} all-to-all(bf16[8,2,128,128]{3,2,1,0:T(8,128)(2,1)S(1)} %bitcast.25), channel_id=1, replica_groups={{0,1,2,3,4,5,6,7},{8,9,10,11,12,13,14,15},{16,17,18,19,20,21,22,23},{24..., dimensions={0} | all-to-all | bytes 1048576 | tf_op jit(solution)/shard_map/all_to_all | solution.py:402
  195.8 13.9 %all-gather.7.cloned.1.call-done = bf16[16,42,16,128]{3,2,1,0:T(8,128)(2,1)} async-done(((bf16[2,42,16,128]{3,2,1,0:T(8,128)(2,1)}), bf16[16,42,16,128]{3,2,1,0:T(8,128)(2,1)}) %all-gather.7.cloned.1.call-update) | async-done | bytes 2752528 | tf_op jit(solution)/shard_map/all_gather | solution.py:401
  209.6 1.8 copy-done
  211.4 3.5 %widen.1 = f32[84,128,128]{2,1,0:T(8,128)} custom-call(bf16[8,84,16,128]{3,2,1,0:T(8,128)(2,1)S(1)} %bitcast.24), custom_call_target="tpu_custom_call" | custom-call | tf_op jit(solution)/shard_map/widen/pallas_call | solution.py:412
  (77 shorter events, 7.5 us)
Async XLA Ops:
  7.2 18.9 %copy-start.3 = (s32[2,1344]{1,0:T(2,128)S(1)}, s32[2,1344]{1,0:T(2,128)}, u32[]{:S(2)}) copy-start(s32[2,1344]{1,0:T(2,128)} %refs_1_.3) | copy-start | bytes 32260
  7.2 19.0 %copy-start.17 = (s32[2,1344]{1,0:T(2,128)S(1)}, s32[2,1344]{1,0:T(2,128)}, u32[]{:S(2)}) copy-start(s32[2,1344]{1,0:T(2,128)} %param.8) | copy-start | bytes 32260
  11.2 19.7 %collective-permute-start.2 = (bf16[2,128,128]{2,1,0:T(8,128)(2,1)}, bf16[2,128,128]{2,1,0:T(8,128)(2,1)S(1)}, u32[]{:S(2)}, u32[]{:S(2)}) collective-permute-start(bf16[2,128,128]{2,1,0:T(8,128)(2,1)} %get-tuple-element.18), channel_id=1, source_target_pairs={{0,24},{1,25},{2,26},{3,27},{4,28},{5,29},{6,30},{7,31},{8,0},{9,1... | collective-permute-start | bytes 196616 | tf_op jit(solution)/shard_map/ppermute | solution.py:303
  14.5 16.4 %collective-permute-start.1 = (bf16[2,128,128]{2,1,0:T(8,128)(2,1)}, bf16[2,128,128]{2,1,0:T(8,128)(2,1)S(1)}, u32[]{:S(2)}, u32[]{:S(2)}) collective-permute-start(bf16[2,128,128]{2,1,0:T(8,128)(2,1)} %get-tuple-element.18), channel_id=1, source_target_pairs={{0,16},{1,17},{2,18},{3,19},{4,20},{5,21},{6,22},{7,23},{8,24},{9,... | collective-permute-start | bytes 196616 | tf_op jit(solution)/shard_map/ppermute | solution.py:303
  15.0 15.9 %collective-permute-start = (bf16[2,128,128]{2,1,0:T(8,128)(2,1)}, bf16[2,128,128]{2,1,0:T(8,128)(2,1)S(1)}, u32[]{:S(2)}, u32[]{:S(2)}) collective-permute-start(bf16[2,128,128]{2,1,0:T(8,128)(2,1)} %get-tuple-element.18), channel_id=1, source_target_pairs={{0,8},{1,9},{2,10},{3,11},{4,12},{5,13},{6,14},{7,15},{8,16},{9,17... | collective-permute-start | bytes 196616 | tf_op jit(solution)/shard_map/ppermute | solution.py:303
  15.6 29.1 %all-to-all-start = ((bf16[32,6,16,128]{3,2,1,0:T(8,128)(2,1)}), bf16[32,6,16,128]{3,2,1,0:T(8,128)(2,1)S(1)}, u32[]{:S(2)}, u32[]{:S(2)}) async-start(bf16[32,6,16,128]{3,2,1,0:T(8,128)(2,1)} %bitcast.31), calls=%async_computation | async-start | bytes 1572864 | tf_op jit(solution)/shard_map/all_to_all | solution.py:295
  26.0 62.5 %all-gather.5.cloned.1.call-start = ((), (), s32[]{:S(2)}) async-start(), calls=%async_computation.5 | async-start | bytes 6193152 | tf_op jit(solution)/shard_map/all_gather | solution.py:326
  30.9 57.7 %copy-start.4 = (s32[168]{0:T(256)}, s32[168]{0:T(256)S(1)}, u32[]{:S(2)}) copy-start(s32[168]{0:T(256)S(1)} %reshape.97.table_ref.refs_0_) | copy-start | bytes 2020
  31.8 56.8 %copy-start.8 = (bf16[4,2,128,128]{3,2,1,0:T(8,128)(2,1)}, bf16[4,2,128,128]{3,2,1,0:T(8,128)(2,1)S(1)}, u32[]{:S(2)}) copy-start(bf16[4,2,128,128]{3,2,1,0:T(8,128)(2,1)S(1)} %pad_maximum_fusion.refs_3_) | copy-start | bytes 786436
  46.5 100.2 %reduce-scatter.2.cloned.1.call-start = ((), (), s32[]{:S(2)}) async-start(), calls=%async_computation.4 | async-start | bytes 6193152 | tf_op jit(solution)/shard_map/reduce_scatter | solution.py:366
  46.6 7.0 %collective-permute-start.6 = (bf16[4,2,128,128]{3,2,1,0:T(8,128)(2,1)S(1)}, bf16[4,2,128,128]{3,2,1,0:T(8,128)(2,1)S(1)}, u32[]{:S(2)}, u32[]{:S(2)}) collective-permute-start(bf16[4,2,128,128]{3,2,1,0:T(8,128)(2,1)S(1)} %pad_maximum_fusion.refs_3_), channel_id=1, source_target_pairs={{0,7},{1,0},{2,1},{3,2},{4,3},{5,4},{6,5},{7,6},{8,15},{9,8},{10,9... | collective-permute-start | bytes 786440 | tf_op jit(solution)/shard_map/ppermute | solution.py:309
  49.0 6.4 %collective-permute-start.3 = (bf16[4,2,128,128]{3,2,1,0:T(8,128)(2,1)S(1)}, bf16[4,2,128,128]{3,2,1,0:T(8,128)(2,1)S(1)}, u32[]{:S(2)}, u32[]{:S(2)}) collective-permute-start(bf16[4,2,128,128]{3,2,1,0:T(8,128)(2,1)S(1)} %pad_maximum_fusion.refs_3_), channel_id=1, source_target_pairs={{0,1},{1,2},{2,3},{3,4},{4,5},{5,6},{6,7},{7,0},{8,9},{9,10},{10,1... | collective-permute-start | bytes 786440 | tf_op jit(solution)/shard_map/ppermute | solution.py:309
  53.6 35.0 %copy-start.11 = (bf16[4,2,128,128]{3,2,1,0:T(8,128)(2,1)}, bf16[4,2,128,128]{3,2,1,0:T(8,128)(2,1)S(1)}, u32[]{:S(2)}) copy-start(bf16[4,2,128,128]{3,2,1,0:T(8,128)(2,1)S(1)} %collective-permute-done.6.refs_9_) | copy-start | bytes 786436
  53.6 7.0 %collective-permute-start.7 = (bf16[4,2,128,128]{3,2,1,0:T(8,128)(2,1)S(1)}, bf16[4,2,128,128]{3,2,1,0:T(8,128)(2,1)S(1)}, u32[]{:S(2)}, u32[]{:S(2)}) collective-permute-start(bf16[4,2,128,128]{3,2,1,0:T(8,128)(2,1)S(1)} %collective-permute-done.6.refs_9_), channel_id=1, source_target_pairs={{0,7},{1,0},{2,1},{3,2},{4,3},{5,4},{6,5},{7,6},{8,15},{9,8},{10,9... | collective-permute-start | bytes 786440 | tf_op jit(solution)/shard_map/ppermute | solution.py:309
  55.5 33.1 %copy-start.12 = (bf16[4,2,128,128]{3,2,1,0:T(8,128)(2,1)}, bf16[4,2,128,128]{3,2,1,0:T(8,128)(2,1)S(1)}, u32[]{:S(2)}) copy-start(bf16[4,2,128,128]{3,2,1,0:T(8,128)(2,1)S(1)} %collective-permute-done.3.refs_4_) | copy-start | bytes 786436
  55.5 6.9 %collective-permute-start.4 = (bf16[4,2,128,128]{3,2,1,0:T(8,128)(2,1)S(1)}, bf16[4,2,128,128]{3,2,1,0:T(8,128)(2,1)S(1)}, u32[]{:S(2)}, u32[]{:S(2)}) collective-permute-start(bf16[4,2,128,128]{3,2,1,0:T(8,128)(2,1)S(1)} %collective-permute-done.3.refs_4_), channel_id=1, source_target_pairs={{0,1},{1,2},{2,3},{3,4},{4,5},{5,6},{6,7},{7,0},{8,9},{9,10},{10,1... | collective-permute-start | bytes 786440 | tf_op jit(solution)/shard_map/ppermute | solution.py:309
  60.6 28.0 %copy-start.13 = (bf16[4,2,128,128]{3,2,1,0:T(8,128)(2,1)}, bf16[4,2,128,128]{3,2,1,0:T(8,128)(2,1)S(1)}, u32[]{:S(2)}) copy-start(bf16[4,2,128,128]{3,2,1,0:T(8,128)(2,1)S(1)} %collective-permute-done.7.refs_8_) | copy-start | bytes 786436
  60.6 8.3 %collective-permute-start.8 = (bf16[4,2,128,128]{3,2,1,0:T(8,128)(2,1)S(1)}, bf16[4,2,128,128]{3,2,1,0:T(8,128)(2,1)S(1)}, u32[]{:S(2)}, u32[]{:S(2)}) collective-permute-start(bf16[4,2,128,128]{3,2,1,0:T(8,128)(2,1)S(1)} %collective-permute-done.7.refs_8_), channel_id=1, source_target_pairs={{0,7},{1,0},{2,1},{3,2},{4,3},{5,4},{6,5},{7,6},{8,15},{9,8},{10,9... | collective-permute-start | bytes 786440 | tf_op jit(solution)/shard_map/ppermute | solution.py:309
  62.4 26.2 %copy-start.14 = (bf16[4,2,128,128]{3,2,1,0:T(8,128)(2,1)}, bf16[4,2,128,128]{3,2,1,0:T(8,128)(2,1)S(1)}, u32[]{:S(2)}) copy-start(bf16[4,2,128,128]{3,2,1,0:T(8,128)(2,1)S(1)} %collective-permute-done.4.refs_5_) | copy-start | bytes 786436
  62.4 8.4 %collective-permute-start.5 = (bf16[4,2,128,128]{3,2,1,0:T(8,128)(2,1)S(1)}, bf16[4,2,128,128]{3,2,1,0:T(8,128)(2,1)S(1)}, u32[]{:S(2)}, u32[]{:S(2)}) collective-permute-start(bf16[4,2,128,128]{3,2,1,0:T(8,128)(2,1)S(1)} %collective-permute-done.4.refs_5_), channel_id=1, source_target_pairs={{0,1},{1,2},{2,3},{3,4},{4,5},{5,6},{6,7},{7,0},{8,9},{9,10},{10,1... | collective-permute-start | bytes 786440 | tf_op jit(solution)/shard_map/ppermute | solution.py:309
  68.9 19.7 %copy-start.9 = (bf16[4,2,128,128]{3,2,1,0:T(8,128)(2,1)}, bf16[4,2,128,128]{3,2,1,0:T(8,128)(2,1)S(1)}, u32[]{:S(2)}) copy-start(bf16[4,2,128,128]{3,2,1,0:T(8,128)(2,1)S(1)} %collective-permute-done.8.refs_7_) | copy-start | bytes 786436
  68.9 5.3 %collective-permute-start.10 = (bf16[2,2,128,128]{3,2,1,0:T(8,128)(2,1)S(1)}, bf16[2,2,128,128]{3,2,1,0:T(8,128)(2,1)S(1)}, u32[]{:S(2)}, u32[]{:S(2)}) collective-permute-start(bf16[2,2,128,128]{3,2,1,0:T(8,128)(2,1)S(1)} %slice.29), channel_id=1, source_target_pairs={{0,7},{1,0},{2,1},{3,2},{4,3},{5,4},{6,5},{7,6},{8,15},{9,8},{10,9... | collective-permute-start | bytes 393224 | tf_op jit(solution)/shard_map/ppermute | solution.py:309
  70.7 17.9 %copy-start.10 = (bf16[4,2,128,128]{3,2,1,0:T(8,128)(2,1)}, bf16[4,2,128,128]{3,2,1,0:T(8,128)(2,1)S(1)}, u32[]{:S(2)}) copy-start(bf16[4,2,128,128]{3,2,1,0:T(8,128)(2,1)S(1)} %collective-permute-done.5.refs_6_) | copy-start | bytes 786436
  70.7 6.9 %collective-permute-start.9 = (bf16[2,2,128,128]{3,2,1,0:T(8,128)(2,1)S(1)}, bf16[2,2,128,128]{3,2,1,0:T(8,128)(2,1)S(1)}, u32[]{:S(2)}, u32[]{:S(2)}) collective-permute-start(bf16[2,2,128,128]{3,2,1,0:T(8,128)(2,1)S(1)} %slice.28), channel_id=1, source_target_pairs={{0,1},{1,2},{2,3},{3,4},{4,5},{5,6},{6,7},{7,0},{8,9},{9,10},{10,1... | collective-permute-start | bytes 393224 | tf_op jit(solution)/shard_map/ppermute | solution.py:309
  106.1 27.1 %copy-start.2 = (bf16[16,128,128]{2,1,0:T(8,128)(2,1)S(1)}, bf16[16,128,128]{2,1,0:T(8,128)(2,1)}, u32[]{:S(2)}) copy-start(bf16[16,128,128]{2,1,0:T(8,128)(2,1)} %get-tuple-element.23.refs_0_) | copy-start | bytes 1572868
  106.1 40.5 %copy-start.5 = (s32[168]{0:T(256)S(1)}, s32[168]{0:T(256)}, u32[]{:S(2)}) copy-start(s32[168]{0:T(256)} %copy-done.4) | copy-start | bytes 2020
  106.1 40.5 %copy-start.7 = (s32[14]{0:T(128)S(1)}, s32[14]{0:T(128)}, u32[]{:S(2)}) copy-start(s32[14]{0:T(128)} %reshape.98.refs_1_.count_ref) | copy-start | bytes 172
  106.2 103.5 %all-gather.7.cloned.1.call-start = ((), (), s32[]{:S(2)}) async-start(), calls=%async_computation.6 | async-start | bytes 3096576 | tf_op jit(solution)/shard_map/all_gather | solution.py:401
  107.1 14.6 %collective-permute-start.11 = (bf16[16,128,128]{2,1,0:T(8,128)(2,1)S(1)}, bf16[16,128,128]{2,1,0:T(8,128)(2,1)S(1)}, u32[]{:S(2)}, u32[]{:S(2)}) collective-permute-start(bf16[16,128,128]{2,1,0:T(8,128)(2,1)S(1)} %copy-done.20), channel_id=1, source_target_pairs={{0,8},{1,9},{2,10},{3,11},{4,12},{5,13},{6,14},{7,15},{8,16},{9,17... | collective-permute-start | bytes 1572872 | tf_op jit(solution)/shard_map/ppermute | solution.py:303
  107.5 25.4 %collective-permute-start.12 = (bf16[16,128,128]{2,1,0:T(8,128)(2,1)S(1)}, bf16[16,128,128]{2,1,0:T(8,128)(2,1)S(1)}, u32[]{:S(2)}, u32[]{:S(2)}) collective-permute-start(bf16[16,128,128]{2,1,0:T(8,128)(2,1)S(1)} %copy-done.19), channel_id=1, source_target_pairs={{0,16},{1,17},{2,18},{3,19},{4,20},{5,21},{6,22},{7,23},{8,24},{9,... | collective-permute-start | bytes 1572872 | tf_op jit(solution)/shard_map/ppermute | solution.py:303
  110.0 23.2 %collective-permute-start.13 = (bf16[16,128,128]{2,1,0:T(8,128)(2,1)S(1)}, bf16[16,128,128]{2,1,0:T(8,128)(2,1)S(1)}, u32[]{:S(2)}, u32[]{:S(2)}) collective-permute-start(bf16[16,128,128]{2,1,0:T(8,128)(2,1)S(1)} %copy-done.18), channel_id=1, source_target_pairs={{0,24},{1,25},{2,26},{3,27},{4,28},{5,29},{6,30},{7,31},{8,0},{9,1... | collective-permute-start | bytes 1572872 | tf_op jit(solution)/shard_map/ppermute | solution.py:303
  133.2 41.0 %copy-start.6 = (s32[4]{0:T(128)S(1)}, s32[4]{0:T(128)}, u32[]{:S(2)}) copy-start(s32[4]{0:T(128)} %pad_add_fusion.refs_0_.refs_2_) | copy-start | bytes 52
  (7 other events, 34.6 us)
Sparse Core Ops, SparseCore 0:
  46.6 41.8 all-gather.4
  106.3 40.3 reduce-scatter.1
  176.6 32.9 all-gather.6

commit v3 on v2

v3 whole, which is shorter than its diff:
```python
import jax
import jax.numpy as jnp
from jax import lax
from jax.experimental import pallas as pl
from jax.experimental.pallas import tpu as pltpu
from jax.sharding import PartitionSpec as P

BLOCK = 128
MOST = 12
PAIR = 3
GROUP = 4
F32 = jnp.float32
BF16 = jnp.bfloat16


def nt(a, b):
    return lax.dot_general(a, b, (((1,), (1,)), ((), ())), preferred_element_type=F32)


def nn(a, b):
    return lax.dot_general(a, b, (((1,), (0,)), ((), ())), preferred_element_type=F32)


def slot_table(tile_rows, tile_cols, me, members, panels):
    owned = tile_cols.shape[1] // members
    cols = tile_cols.reshape(2, members, owned)
    rows = tile_rows.reshape(2, members, owned)
    local = cols - me * panels
    holder = cols // panels
    pad = jnp.full((2, members, 2), -1, jnp.int32)

    def run(values):
        one = jnp.concatenate([pad[:, :, :1], values[:, :, :-1]], axis=2)
        two = jnp.concatenate([pad, values[:, :, :-2]], axis=2)
        return (values == one).astype(jnp.int32) + (values == two).astype(jnp.int32)

    rank = run(holder)
    within = run(cols)
    value = jnp.arange(members)[None, :, None] * 256 + rank * 64 + rows
    mine = local[None] == jnp.arange(panels)[:, None, None, None]
    count = jnp.sum(mine.astype(jnp.int32), axis=3)
    before = jnp.arange(members)[:, None] > jnp.arange(members)[None, :]
    earlier = jnp.sum(jnp.where(before, count[:, :, None, :], 0), axis=3)
    place_in_panel = jnp.where(mine, earlier[..., None] + within[None], -1)
    hit = place_in_panel[:, :, None] == jnp.arange(MOST)[:, None, None]
    table = jnp.sum(jnp.where(hit, value[None, :, None], 0), axis=(3, 4))
    return jnp.swapaxes(table, 0, 1).reshape(-1), jnp.sum(count, axis=2).T.reshape(-1)


def slot_of(cols_ref, me, owned, panels, m, visit):
    def step(k, carry):
        last, rank = carry
        holder = cols_ref[m, me * owned + k] // panels
        rank = jnp.where(holder == last, rank + 1, 0)
        visit(k, holder, rank)
        return holder, rank

    lax.fori_loop(0, owned, step, (jnp.int32(-1), jnp.int32(0)), unroll=6)


def send_kernel(panels, place_ref, cols_ref, tiles_ref, tokens_ref, out_ref, blocks_ref):
    for m in range(2):

        def visit(k, holder, rank):
            out_ref[holder * (2 * PAIR) + m * PAIR + rank] = tiles_ref[m, k]

        slot_of(cols_ref, place_ref[0], tiles_ref.shape[1], panels, m, visit)
    for b in range(blocks_ref.shape[0]):
        blocks_ref[b] = tokens_ref[:, b * BLOCK : (b + 1) * BLOCK]


def own_kernel(panels, place_ref, cols_ref, back_ref, out_ref):
    for m in range(2):

        def visit(k, holder, rank):
            out_ref[m, k] = back_ref[holder * (2 * PAIR) + m * PAIR + rank]

        slot_of(cols_ref, place_ref[0], out_ref.shape[1], panels, m, visit)


def sort_kernel(table_ref, in_ref, out_ref):
    half = out_ref.shape[0] // 2
    for m in range(2):

        def step(s, carry):
            v = table_ref[m * half + s]
            out_ref[m * half + s] = in_ref[(v >> 8) * (2 * PAIR) + m * PAIR + ((v >> 6) & 3)]
            return carry

        lax.fori_loop(0, half, step, 0, unroll=6)


def unsort_kernel(table_ref, count_ref, *refs):
    out_ref = refs[-1]
    each = len(refs) // 2
    half = refs[0].shape[0]
    panels = half // MOST
    for m in range(2):
        in_refs = refs[m * each : (m + 1) * each]
        for q in range(panels):

            def step(g, carry):
                for i in range(GROUP):
                    s = q * MOST + g * GROUP + i
                    v = table_ref[m * half + s]
                    total = sum(r[s].astype(F32) for r in in_refs).astype(BF16)
                    out_ref[(v >> 8) * (2 * PAIR) + m * PAIR + ((v >> 6) & 3)] = total
                return carry

            lax.fori_loop(0, count_ref[m * panels + q] // GROUP, step, 0)


def core_kernel(where_ref, mine_ref, other_ref, *out_refs):
    for k, out_ref in enumerate(out_refs):
        y = lax.rem(where_ref[5] + k, 4)
        out_ref[...] = (mine_ref[y].astype(F32) + other_ref[y].astype(F32)).astype(BF16)


def main_kernel(sides, ring, panels, table_ref, count_ref, where_ref, *refs):
    pieces, refs = refs[: ring + 1], refs[ring + 1 :]
    tile_hbm, cot_ref, hidden_ref, *refs = refs
    grads_hbm, refs = (refs[:2], refs[2:4]), refs[4:]
    terms_ref, tok_ref, tok_t, total, tile_ref, grad_ref, pair_ref, *refs = refs
    tok_sems, in_sems, out_sems = refs
    blocks = tok_ref.shape[0]
    each = blocks // sides
    turned = -(-blocks // panels)
    side = where_ref[2]

    core = where_ref[4]

    def loads(p):
        for m in range(2):
            at = pl.ds((m * panels + p) * MOST, MOST)
            yield pltpu.make_async_copy(tile_hbm.at[:, at], tile_ref.at[:, at], in_sems.at[m, p])

    def stores(p):
        for m in range(2):
            at, to = pl.ds((m * panels + p) * MOST, MOST), pl.ds(p * MOST, MOST)
            for k in range(2):
                yield pltpu.make_async_copy(
                    grad_ref.at[k, :, at], grads_hbm[k][m].at[:, to], out_sems.at[k, m, p]
                )

    steps = [j for j in range(ring) if j != ring // 2]
    held = [(j, s, piece.at[s]) for j, piece in zip(steps, pieces) for s in range(sides)]
    held += [
        (ring // 2, k * sides // 2 + s, piece.at[s])
        for k, piece in enumerate(pieces[-2:])
        for s in range(sides // 2)
    ]
    copies = [
        pltpu.make_async_copy(
            piece,
            tok_ref.at[
                pl.ds(
                    lax.rem(side + sides - s, sides) * each
                    + lax.rem(where_ref[3] + ring - j, ring) * (each // ring),
                    each // ring,
                )
            ],
            tok_sems.at[s, j],
        )
        for j, s, piece in held
    ]
    for copy in copies:
        copy.start()
    for p in range(panels):
        for copy in loads(p):
            copy.start()

    def clear(b, carry):
        total[b] = jnp.zeros_like(total[b])
        return carry

    lax.fori_loop(0, blocks, clear, 0)
    for copy in copies:
        copy.wait()

    def stacked(p, m, first):
        w = tile_ref[:, pl.ds((m * panels + p) * MOST + first, GROUP)]
        return jnp.concatenate([w[:, i].reshape(BLOCK, BLOCK) for i in range(GROUP)], axis=0)

    def by_counts(p, work):
        many = [count_ref[m * panels + p] > GROUP for m in range(2)]
        for most in range(4):
            picked = [bool(most & 1), bool(most & 2)]
            same = [many[m] if picked[m] else jnp.logical_not(many[m]) for m in range(2)]

            @pl.when(jnp.logical_and(same[0], same[1]))
            def _():
                counts = [MOST if picked[m] else GROUP for m in range(2)]
                at = [
                    [table_ref[(m * panels + p) * MOST + t] & 63 for t in range(counts[m])]
                    for m in range(2)
                ]
                work(p, counts, at)

    def forward(p, counts, at):
        for i in range(turned):
            b = jnp.minimum(p * turned + i, blocks - 1)
            tok_t[b] = tok_ref[b].T
        pre = []
        for m in range(2):
            acc = None
            for first in range(0, counts[m], GROUP):
                lhs = jnp.concatenate([tok_ref[at[m][first + i]] for i in range(GROUP)], axis=1)
                term = nn(lhs, stacked(p, m, first))
                acc = term if acc is None else acc + term
            pre.append(acc)
        gate, up = pre
        sig = 1.0 / (1.0 + jnp.exp(-gate))
        columns = pl.ds(pl.multiple_of(p * BLOCK, BLOCK), BLOCK)
        hidden_ref[:, columns] = (gate * sig * up).astype(BF16)
        cot = cot_ref[:, columns].astype(F32)
        pair_ref[p * 2] = (cot * up * sig * (1.0 + gate * (1.0 - sig))).astype(BF16)
        pair_ref[p * 2 + 1] = (cot * gate * sig).astype(BF16)

    def backward(p, counts, at):
        for m in range(2):
            grad = pair_ref[p * 2 + m]
            for first in range(0, counts[m], GROUP):
                lhs = jnp.concatenate([tok_t[at[m][first + i]] for i in range(GROUP)], axis=0)
                out = nn(lhs, grad).astype(BF16)
                back = nt(grad, stacked(p, m, first))
                for i in range(GROUP):
                    part = out[i * BLOCK : (i + 1) * BLOCK].reshape(4, 2, BLOCK // 8, BLOCK)
                    slot = (m * panels + p) * MOST + first + i
                    grad_ref[core, :, slot] = part[:, 0]
                    grad_ref[1 - core, :, slot] = part[:, 1]
                    total[at[m][first + i]] += back[:, i * BLOCK : (i + 1) * BLOCK]

    def first_pass(p, carry):
        for copy in loads(p):
            copy.wait()
        by_counts(p, forward)
        return carry

    def second_pass(p, carry):
        by_counts(p, backward)
        for copy in stores(p):
            copy.start()
        return carry

    lax.fori_loop(0, panels, first_pass, 0)
    lax.fori_loop(0, panels, second_pass, 0)

    def step(b, carry):
        terms_ref[b] = total[b].astype(BF16)
        return carry

    lax.fori_loop(0, blocks, step, 0, unroll=2)
    for p in range(panels):
        for copy in stores(p):
            copy.wait()


def sum_kernel(in_ref, out_ref):
    def step(k, acc):
        return tuple(a + in_ref[k, i].astype(F32) for i, a in enumerate(acc))

    count = in_ref.shape[1]
    acc = lax.fori_loop(
        0, in_ref.shape[0], step, tuple(jnp.zeros(in_ref.shape[2:], F32) for _ in range(count))
    )
    for i in range(count):
        out_ref[:, i * BLOCK : (i + 1) * BLOCK] = acc[i].astype(BF16)


def widen_kernel(in_ref, out_ref):
    parts, count, part, _ = in_ref.shape

    def step(i, carry):
        out_ref[i] = in_ref[:, i].reshape(parts * part, BLOCK).astype(F32)
        return carry

    lax.fori_loop(0, count, step, 0, unroll=2)


def whole(shape):
    return pl.BlockSpec(shape, lambda *_: (0,) * len(shape))


def per_device(tokens, cotangent, tiles, tile_rows, tile_cols):
    groups = lax.axis_size("dp")
    members = lax.axis_size("mp")
    me = lax.axis_index("mp")
    mygroup = lax.axis_index("dp")
    owned = tiles.shape[1]
    tok_rows, my_features = tokens.shape
    my_blocks = my_features // BLOCK
    row_blocks = my_blocks * members
    panels = cotangent.shape[1] // BLOCK
    part = BLOCK // groups
    slots = members * 2 * PAIR
    used = panels * 2 * MOST
    params = pltpu.CompilerParams(vmem_limit_bytes=48 * 1024 * 1024)
    alone = pltpu.CompilerParams(vmem_limit_bytes=60 * 1024 * 1024)
    sides = 4
    ring = members // sides
    each = row_blocks // sides
    where = jnp.stack([me, mygroup, me // ring, me % ring, mygroup % 2, mygroup // 2]).astype(jnp.int32)

    outgoing, my_tok = pl.pallas_call(
        lambda *refs: send_kernel(panels, *refs),
        out_shape=(
            jax.ShapeDtypeStruct((slots, part, BLOCK), BF16),
            jax.ShapeDtypeStruct((my_blocks, tok_rows, BLOCK), BF16),
        ),
        grid_spec=pltpu.PrefetchScalarGridSpec(
            num_scalar_prefetch=2,
            grid=(1,),
            in_specs=[
                pl.BlockSpec((2, owned, part, BLOCK), lambda i, w, c: (0, 0, w[1], 0)),
                whole(tokens.shape),
            ],
            out_specs=(whole((slots, part, BLOCK)), whole((my_blocks, tok_rows, BLOCK))),
        ),
        compiler_params=alone,
        name="send_pack",
    )(where, tile_cols, tiles, tokens)

    def exchange(values):
        shape = (members, -1) + values.shape[1:]
        return lax.all_to_all(values.reshape(shape), "mp", 0, 0).reshape(values.shape)

    rows = [[x * ring + z for z in range(ring)] for x in range(sides)]

    def turn(value, s):
        pairs = [
            (x * ring + z, (x + s) % sides * ring + z) for x in range(sides) for z in range(ring)
        ]
        return lax.ppermute(value, "mp", pairs)

    def along(value, s):
        pairs = [
            (x * ring + z, x * ring + (z + s) % ring) for x in range(sides) for z in range(ring)
        ]
        return lax.ppermute(value, "mp", pairs)

    line_tok = jnp.stack([my_tok] + [turn(my_tok, s) for s in range(1, sides)])
    table, count = slot_table(tile_rows, tile_cols, me, members, panels)
    incoming, line_tok = lax.optimization_barrier((exchange(outgoing), line_tok))
    ordered = pl.pallas_call(
        sort_kernel,
        out_shape=jax.ShapeDtypeStruct((used, part, BLOCK), BF16),
        grid_spec=pltpu.PrefetchScalarGridSpec(
            num_scalar_prefetch=1,
            grid=(1,),
            in_specs=[whole((slots, part, BLOCK))],
            out_specs=whole((used, part, BLOCK)),
        ),
        compiler_params=params,
        name="sort_slots",
    )(table, incoming)
    held = lax.all_gather(ordered, "dp")
    ups, downs = [line_tok], [line_tok]
    for _ in range(ring // 2 - 1):
        ups.append(along(ups[-1], 1))
        downs.append(along(downs[-1], -1))
    far = [along(ups[-1][: sides // 2], 1), along(downs[-1][sides // 2 :], -1)]
    pieces = ups + downs[:0:-1] + far

    anywhere = pl.BlockSpec(memory_space=pl.ANY)
    split = jax.ShapeDtypeStruct((4, used // 2, part, BLOCK), BF16)
    hidden, mine_g, mine_u, other_g, other_u, terms = pl.pallas_call(
        lambda *refs: main_kernel(sides, ring, panels, *refs),
        out_shape=(
            jax.ShapeDtypeStruct(cotangent.shape, BF16),
            *(split,) * 4,
        )
        + (jax.ShapeDtypeStruct((row_blocks, tok_rows, BLOCK), BF16),),
        grid_spec=pltpu.PrefetchScalarGridSpec(
            num_scalar_prefetch=3,
            grid=(1,),
            in_specs=[anywhere] * (len(pieces) + 1) + [whole(cotangent.shape)],
            out_specs=(whole(cotangent.shape), *(anywhere,) * 4)
            + (whole((row_blocks, tok_rows, BLOCK)),),
            scratch_shapes=[
                pltpu.VMEM((row_blocks, tok_rows, BLOCK), BF16),
                pltpu.VMEM((row_blocks, BLOCK, tok_rows), BF16),
                pltpu.VMEM((row_blocks, tok_rows, BLOCK), F32),
                pltpu.VMEM((groups, used, part, BLOCK), BF16),
                pltpu.VMEM((2, 4, used, part, BLOCK), BF16),
                pltpu.VMEM((2 * panels, tok_rows, BLOCK), BF16),
                pltpu.SemaphoreType.DMA((sides, ring)),
                pltpu.SemaphoreType.DMA((2, panels)),
                pltpu.SemaphoreType.DMA((2, 2, panels)),
            ],
        ),
        compiler_params=alone,
        name="gated_pair",
    )(table, count, where, *pieces, held, cotangent)

    def around(value, s):
        pairs = [(y * 2 + c, (y + s) % 4 * 2 + c) for y in range(4) for c in range(2)]
        return lax.ppermute(value, "dp", pairs)

    piece = jax.ShapeDtypeStruct((used // 2, part, BLOCK), BF16)

    def reduced(mine, other):
        block = pl.BlockSpec((4, MOST, part, BLOCK), lambda i, w: (0, i, 0, 0))
        return pl.pallas_call(
            core_kernel,
            out_shape=(piece,) * 4,
            grid_spec=pltpu.PrefetchScalarGridSpec(
                num_scalar_prefetch=1,
                grid=(panels,),
                in_specs=[block] * 2,
                out_specs=(pl.BlockSpec((MOST, part, BLOCK), lambda i, w: (i, 0, 0)),) * 4,
            ),
            compiler_params=params,
            name="core_sum",
        )(where, mine, other)

    mine = [mine_g, mine_u]
    other = [lax.ppermute(v, "dp", [(d, d ^ 1) for d in range(groups)]) for v in (other_g, other_u)]
    sent = [reduced(mine[m], other[m]) for m in range(2)]
    came = [[sent[m][0]] + [around(sent[m][s], s) for s in (1, 2, 3)] for m in range(2)]
    columns = [[x * ring + z for x in range(sides)] for z in range(ring)]
    row_terms = lax.psum_scatter(
        terms, "mp", scatter_dimension=0, axis_index_groups=columns, tiled=True
    )
    returning = pl.pallas_call(
        unsort_kernel,
        out_shape=jax.ShapeDtypeStruct((slots, part, BLOCK), BF16),
        grid_spec=pltpu.PrefetchScalarGridSpec(
            num_scalar_prefetch=2,
            grid=(1,),
            in_specs=[whole(piece.shape)] * 8,
            out_specs=whole((slots, part, BLOCK)),
        ),
        compiler_params=params,
        name="unsort_slots",
    )(table, count, *came[0], *came[1])
    own = pl.pallas_call(
        lambda *refs: own_kernel(panels, *refs),
        out_shape=jax.ShapeDtypeStruct((2, owned, part, BLOCK), BF16),
        grid_spec=pltpu.PrefetchScalarGridSpec(
            num_scalar_prefetch=2,
            grid=(1,),
            in_specs=[whole((slots, part, BLOCK))],
            out_specs=whole((2, owned, part, BLOCK)),
        ),
        compiler_params=params,
        name="own_slots",
    )(where, tile_cols, exchange(returning))
    own, row_terms = lax.optimization_barrier((own, row_terms))
    full = lax.all_gather(own, "dp").reshape(groups, 2 * owned, part, BLOCK)
    column = lax.all_to_all(
        row_terms.reshape(ring, my_blocks, tok_rows, BLOCK), "mp", 0, 0, axis_index_groups=rows
    )
    input_grad = pl.pallas_call(
        sum_kernel,
        out_shape=jax.ShapeDtypeStruct(tokens.shape, BF16),
        compiler_params=params,
        name="input_sum",
    )(column)
    some = 2 * owned // 6
    tile_grads = pl.pallas_call(
        widen_kernel,
        out_shape=jax.ShapeDtypeStruct((2 * owned, BLOCK, BLOCK), F32),
        grid=(6,),
        in_specs=[pl.BlockSpec((groups, some, part, BLOCK), lambda i: (0, i, 0, 0))],
        out_specs=pl.BlockSpec((some, BLOCK, BLOCK), lambda i: (i, 0, 0)),
        compiler_params=params,
        name="widen",
    )(full).reshape(tiles.shape)
    return hidden, input_grad, tile_grads


def solution(mesh):
    in_specs = (P("dp", "mp"), P("dp", "mp"), P(None, "mp", None, None), P(), P())
    out_specs = (P("dp", "mp"), P("dp", "mp"), P(None, "mp", None, None))
    return jax.shard_map(
        per_device, mesh=mesh, in_specs=in_specs, out_specs=out_specs, check_vma=False
    )
```

time: 222 us -> 213 us (0.959)
  waiting for transfers between devices: 94.3 us -> 83.7 us
  blocking collectives: 43.6 us -> 47.2 us
    ppermute x0 -> x8, waiting for transfers between devices: none -> 29.4 us  [the longest x6 26.6 us: around(): return lax.ppermute(value, 'dp', pairs)]
    ppermute x6 -> x3, waiting for transfers between devices: 21.3 us -> 0.05 us  [turn(): return lax.ppermute(value, 'mp', pairs)]
    reduce_scatter x1, waiting for transfers between devices: 13.1 us -> 0.01 us  [per_device(): lax.psum_scatter(terms, 'mp', scatter_dimension=0, axis_index_groups=colu...]
    ppermute x0 -> x8, starting transfers between devices: none -> 5.89 us  [the longest x6 5.29 us: around(): return lax.ppermute(value, 'dp', pairs)]
    ppermute x6 -> x3, starting transfers between devices: 9.23 us -> 3.68 us  [turn(): return lax.ppermute(value, 'mp', pairs)]
    all_to_all x1, blocking collectives: 25.1 us -> 28.9 us  [exchange(): lax.all_to_all(values.reshape(shape), 'mp', 0, 0).reshape(values.shape)]
    all_gather x1, waiting for transfers between devices: 13.9 us -> 11.2 us  [per_device(): full = lax.all_gather(own, 'dp').reshape(groups, 2 * owned, part, BLOCK)]
    all_to_all x1, waiting for transfers between devices: 13 us -> 10.7 us  [exchange(): lax.all_to_all(values.reshape(shape), 'mp', 0, 0).reshape(values.shape)]
  transfers between devices with their start and end apart: 18 -> 23, of which waited for: 14 -> 15; matrix products, arithmetic and copies ran while one was open for 3% -> 3% of each run, Pallas kernels for 1% -> 3%
where the time goes in v3:
time: 213 us
  waiting for transfers between devices  83.7 us (39%)
  blocking collectives  47.2 us (22%)
  starting transfers between devices  30.1 us (14%)
  Pallas kernels  28.5 us (13%)
  between operations  14 us (7%)
  local copies, waits for them, and re-layouts  4.87 us (2%)
  other arithmetic  4.38 us (2%)
    all_to_all x1, blocking collectives, exchange(): lax.all_to_all(values.reshape(shape), 'mp', 0, 0).reshape(values.shape)  28.9 us
    ppermute x6, waiting for transfers between devices, around(): return lax.ppermute(value, 'dp', pairs)  26.6 us
    ppermute x8, waiting for transfers between devices, along(): return lax.ppermute(value, 'mp', pairs)  21.1 us
    all_to_all x1, blocking collectives, per_device(): lax.all_to_all(row_terms.reshape(ring, my_blocks, tok_rows, BLOCK), 'mp',...  18.2 us
    pallas_call x1, Pallas kernels, per_device(): pl.pallas_call(lambda *refs: main_kernel(sides, ring, panels, *refs), out...  13.1 us
    all_to_all x1, starting transfers between devices, exchange(): lax.all_to_all(values.reshape(shape), 'mp', 0, 0).reshape(values.shape)  12 us
    all_gather x1, waiting for transfers between devices, per_device(): held = lax.all_gather(ordered, 'dp')  11.2 us
    all_gather x1, waiting for transfers between devices, per_device(): full = lax.all_gather(own, 'dp').reshape(groups, 2 * owned, part, BLOCK)  11.2 us
  transfers between devices with their start and end apart: 23, of which 15 were waited for; matrix products, arithmetic and copies ran while one was open for 3% of the time, Pallas kernels for 3%

profile of v3, /device:TPU:1, one launch (start us, length us, event | category | flops | bytes accessed | tf_op | source)
XLA Modules:
  0.0 212.8 jit_solution(14845119404773569786)
XLA Ops:
  7.9 3.4 %send_pack.1 = (bf16[192,16,128]{2,1,0:T(8,128)(2,1)}, bf16[2,128,128]{2,1,0:T(8,128)(2,1)}) custom-call(s32[6]{0:T(128)} %stack.42.refs_0_.refs_2_.where_ref, s32[2,1344]{1,0:T(2,128)} %refs_1_.3, bf16[2,42,128,128]{3,2,1,0:T(8,128)(2,1)} %refs_2_.1, bf16[128,256]{1,0:T(8,128)(2,1)} %refs_3_.1), custom_call_target="tpu_custom_call" | custom-call | tf_op jit(solution)/shard_map/send_pack/pallas_call | solution.py:304
  11.3 12.0 %all-to-all-start = ((bf16[32,6,16,128]{3,2,1,0:T(8,128)(2,1)}), bf16[32,6,16,128]{3,2,1,0:T(8,128)(2,1)S(1)}, u32[]{:S(2)}, u32[]{:S(2)}) async-start(bf16[32,6,16,128]{3,2,1,0:T(8,128)(2,1)} %bitcast.32), calls=%async_computation | async-start | bytes 1572864 | tf_op jit(solution)/shard_map/all_to_all | solution.py:325
  23.4 2.6 %collective-permute-start.2 = (bf16[2,128,128]{2,1,0:T(8,128)(2,1)}, bf16[2,128,128]{2,1,0:T(8,128)(2,1)S(1)}, u32[]{:S(2)}, u32[]{:S(2)}) collective-permute-start(bf16[2,128,128]{2,1,0:T(8,128)(2,1)} %get-tuple-element.24), channel_id=1, source_target_pairs={{0,24},{1,25},{2,26},{3,27},{4,28},{5,29},{6,30},{7,31},{8,0},{9,1... | collective-permute-start | bytes 196616 | tf_op jit(solution)/shard_map/ppermute | solution.py:333
  28.5 3.2 %select_reduce_fusion = s32[7,2,12]{2,1,0:T(2,128)S(1)} fusion(s32[2,32,42]{2,1,0:T(8,128)S(1)} %get-tuple-element.46, s32[7,2,32,42]{3,2,1,0:T(8,128)S(1)} %add_select_fusion), kind=kLoop, calls=%fused_computation | loop fusion | flops 677208 | bytes 86688 | tf_op jit(solution)/shard_map/reduce_sum | solution.py:46
  31.9 10.7 %all-to-all-done = bf16[32,6,16,128]{3,2,1,0:T(8,128)(2,1)S(1)} async-done(((bf16[32,6,16,128]{3,2,1,0:T(8,128)(2,1)}), bf16[32,6,16,128]{3,2,1,0:T(8,128)(2,1)S(1)}, u32[]{:S(2)}, u32[]{:S(2)}) %all-to-all-start) | async-done | bytes 786464 | tf_op jit(solution)/shard_map/all_to_all | solution.py:325
  42.6 2.0 sort_slots.1
  44.6 2.1 collective-permute-start.6
  46.7 1.5 collective-permute-start.3
  48.2 3.7 %collective-permute-done.6.refs_9_ = bf16[4,2,128,128]{3,2,1,0:T(8,128)(2,1)S(1)} collective-permute-done((bf16[4,2,128,128]{3,2,1,0:T(8,128)(2,1)S(1)}, bf16[4,2,128,128]{3,2,1,0:T(8,128)(2,1)S(1)}, u32[]{:S(2)}, u32[]{:S(2)}) %collective-permute-start.6) | collective-permute-done | bytes 262176 | tf_op jit(solution)/shard_map/ppermute | solution.py:339
  51.9 1.2 collective-permute-start.7
  53.5 4.8 %collective-permute-done.7.refs_8_ = bf16[4,2,128,128]{3,2,1,0:T(8,128)(2,1)S(1)} collective-permute-done((bf16[4,2,128,128]{3,2,1,0:T(8,128)(2,1)S(1)}, bf16[4,2,128,128]{3,2,1,0:T(8,128)(2,1)S(1)}, u32[]{:S(2)}, u32[]{:S(2)}) %collective-permute-start.7) | collective-permute-done | bytes 262176 | tf_op jit(solution)/shard_map/ppermute | solution.py:339
  58.3 1.3 collective-permute-start.8
  60.0 6.1 %collective-permute-done.8.refs_7_ = bf16[4,2,128,128]{3,2,1,0:T(8,128)(2,1)S(1)} collective-permute-done((bf16[4,2,128,128]{3,2,1,0:T(8,128)(2,1)S(1)}, bf16[4,2,128,128]{3,2,1,0:T(8,128)(2,1)S(1)}, u32[]{:S(2)}, u32[]{:S(2)}) %collective-permute-start.8) | collective-permute-done | bytes 262176 | tf_op jit(solution)/shard_map/ppermute | solution.py:339
  66.1 1.7 collective-permute-start.10
  68.8 3.2 %collective-permute-done.10.refs_11_ = bf16[2,2,128,128]{3,2,1,0:T(8,128)(2,1)S(1)} collective-permute-done((bf16[2,2,128,128]{3,2,1,0:T(8,128)(2,1)S(1)}, bf16[2,2,128,128]{3,2,1,0:T(8,128)(2,1)S(1)}, u32[]{:S(2)}, u32[]{:S(2)}) %collective-permute-start.10) | collective-permute-done | bytes 131104 | tf_op jit(solution)/shard_map/ppermute | solution.py:339
  72.0 2.9 %collective-permute-done.9.refs_10_ = bf16[2,2,128,128]{3,2,1,0:T(8,128)(2,1)S(1)} collective-permute-done((bf16[2,2,128,128]{3,2,1,0:T(8,128)(2,1)S(1)}, bf16[2,2,128,128]{3,2,1,0:T(8,128)(2,1)S(1)}, u32[]{:S(2)}, u32[]{:S(2)}) %collective-permute-start.9) | collective-permute-done | bytes 131104 | tf_op jit(solution)/shard_map/ppermute | solution.py:339
  74.9 11.2 %all-gather.5.cloned.1.call-done = bf16[1344,16,128]{2,1,0:T(8,128)(2,1)} async-done(((bf16[168,16,128]{2,1,0:T(8,128)(2,1)}), bf16[1344,16,128]{2,1,0:T(8,128)(2,1)}) %all-gather.5.cloned.1.call-update) | async-done | bytes 5505040 | tf_op jit(solution)/shard_map/all_gather | solution.py:356
  86.2 13.1 %gated_pair.1 = (bf16[128,896]{1,0:T(8,128)(2,1)}, bf16[4,84,16,128]{3,2,1,0:T(8,128)(2,1)}, bf16[4,84,16,128]{3,2,1,0:T(8,128)(2,1)}, bf16[4,84,16,128]{3,2,1,0...) custom-call(s32[168]{0:T(256)} %copy-done.5, s32[14]{0:T(128)} %reshape.61.refs_1_.count_ref, ...), custom_call_target="tpu_custom_call" | custom-call | tf_op jit(solution)/shard_map/gated_pair/pallas_call | solution.py:366
  99.9 2.8 %collective-permute-done.11.other_ref = bf16[4,84,16,128]{3,2,1,0:T(8,128)(2,1)S(1)} collective-permute-done((bf16[4,84,16,128]{3,2,1,0:T(8,128)(2,1)}, bf16[4,84,16,128]{3,2,1,0:T(8,128)(2,1)S(1)}, u32[]{:S(2)}, u32[]{:S(2)}) %collective-permute-start.11) | collective-permute-done | bytes 1376288 | tf_op jit(solution)/shard_map/ppermute | solution.py:417
  102.8 1.3 copy-done.2
  105.7 1.5 collective-permute-start.13
  107.2 1.9 collective-permute-start.14
  109.1 1.2 core_sum.3
  110.4 1.5 collective-permute-start.17
  111.9 11.2 %collective-permute-done.12.refs_1_ = bf16[84,16,128]{2,1,0:T(8,128)(2,1)S(1)} collective-permute-done((bf16[84,16,128]{2,1,0:T(8,128)(2,1)S(1)}, bf16[84,16,128]{2,1,0:T(8,128)(2,1)S(1)}, u32[]{:S(2)}, u32[]{:S(2)}) %collective-permute-start.12) | collective-permute-done | bytes 344096 | tf_op jit(solution)/shard_map/ppermute | solution.py:397
  123.9 14.3 %collective-permute-done.16.refs_5_ = bf16[84,16,128]{2,1,0:T(8,128)(2,1)S(1)} collective-permute-done((bf16[84,16,128]{2,1,0:T(8,128)(2,1)S(1)}, bf16[84,16,128]{2,1,0:T(8,128)(2,1)S(1)}, u32[]{:S(2)}, u32[]{:S(2)}) %collective-permute-start.16) | collective-permute-done | bytes 344096 | tf_op jit(solution)/shard_map/ppermute | solution.py:397
  139.7 28.9 %all_to_all.15 = bf16[32,6,16,128]{3,2,1,0:T(8,128)(2,1)S(1)} all-to-all(bf16[32,6,16,128]{3,2,1,0:T(8,128)(2,1)S(1)} %bitcast.26), channel_id=1, replica_groups=mesh['dp'=8,'mp'=32] {'mp'}, dimensions={0} | all-to-all | bytes 1572864 | tf_op jit(solution)/shard_map/all_to_all | solution.py:325
  168.6 2.2 %own_slots.1 = bf16[2,42,16,128]{3,2,1,0:T(8,128)(2,1)} custom-call(s32[6]{0:T(128)S(1)} %copy-done.4, s32[2,1344]{1,0:T(2,128)S(1)} %copy-done.3, bf16[192,16,128]{2,1,0:T(8,128)(2,1)S(1)} %bitcast.25), custom_call_target="tpu_custom_call" | custom-call | tf_op jit(solution)/shard_map/own_slots/pallas_call | solution.py:436
  170.9 18.2 %all_to_all.16.in_ref = bf16[8,2,128,128]{3,2,1,0:T(8,128)(2,1)S(1)} all-to-all(bf16[8,2,128,128]{3,2,1,0:T(8,128)(2,1)} %bitcast.33), channel_id=1, replica_groups={{0,1,2,3,4,5,6,7},{8,9,10,11,12,13,14,15},{16,17,18,19,20,21,22,23},{24..., dimensions={0} | all-to-all | bytes 1048576 | tf_op jit(solution)/shard_map/all_to_all | solution.py:450
  189.9 11.2 %all-gather.7.cloned.1.call-done = bf16[16,42,16,128]{3,2,1,0:T(8,128)(2,1)} async-done(((bf16[2,42,16,128]{3,2,1,0:T(8,128)(2,1)}), bf16[16,42,16,128]{3,2,1,0:T(8,128)(2,1)}) %all-gather.7.cloned.1.call-update) | async-done | bytes 2752528 | tf_op jit(solution)/shard_map/all_gather | solution.py:449
  201.1 1.8 copy-done
  202.8 3.5 %widen.1 = f32[84,128,128]{2,1,0:T(8,128)} custom-call(bf16[8,84,16,128]{3,2,1,0:T(8,128)(2,1)S(1)} %bitcast.27), custom_call_target="tpu_custom_call" | custom-call | tf_op jit(solution)/shard_map/widen/pallas_call | solution.py:460
  (84 shorter events, 10.7 us)
Async XLA Ops:
  11.3 20.5 %copy-start.17 = (bf16[2,128,128]{2,1,0:T(8,128)(2,1)S(1)}, bf16[2,128,128]{2,1,0:T(8,128)(2,1)}, u32[]{:S(2)}) copy-start(bf16[2,128,128]{2,1,0:T(8,128)(2,1)} %get-tuple-element.24) | copy-start | bytes 196612
  11.3 31.3 %all-to-all-start = ((bf16[32,6,16,128]{3,2,1,0:T(8,128)(2,1)}), bf16[32,6,16,128]{3,2,1,0:T(8,128)(2,1)S(1)}, u32[]{:S(2)}, u32[]{:S(2)}) async-start(bf16[32,6,16,128]{3,2,1,0:T(8,128)(2,1)} %bitcast.32), calls=%async_computation | async-start | bytes 1572864 | tf_op jit(solution)/shard_map/all_to_all | solution.py:325
  23.3 62.8 %all-gather.5.cloned.1.call-start = ((), (), s32[]{:S(2)}) async-start(), calls=%async_computation.5 | async-start | bytes 6193152 | tf_op jit(solution)/shard_map/all_gather | solution.py:356
  23.4 8.4 %collective-permute-start.2 = (bf16[2,128,128]{2,1,0:T(8,128)(2,1)}, bf16[2,128,128]{2,1,0:T(8,128)(2,1)S(1)}, u32[]{:S(2)}, u32[]{:S(2)}) collective-permute-start(bf16[2,128,128]{2,1,0:T(8,128)(2,1)} %get-tuple-element.24), channel_id=1, source_target_pairs={{0,24},{1,25},{2,26},{3,27},{4,28},{5,29},{6,30},{7,31},{8,0},{9,1... | collective-permute-start | bytes 196616 | tf_op jit(solution)/shard_map/ppermute | solution.py:333
  25.9 5.9 %collective-permute-start.1 = (bf16[2,128,128]{2,1,0:T(8,128)(2,1)}, bf16[2,128,128]{2,1,0:T(8,128)(2,1)S(1)}, u32[]{:S(2)}, u32[]{:S(2)}) collective-permute-start(bf16[2,128,128]{2,1,0:T(8,128)(2,1)} %get-tuple-element.24), channel_id=1, source_target_pairs={{0,16},{1,17},{2,18},{3,19},{4,20},{5,21},{6,22},{7,23},{8,24},{9,... | collective-permute-start | bytes 196616 | tf_op jit(solution)/shard_map/ppermute | solution.py:333
  26.5 5.4 %collective-permute-start = (bf16[2,128,128]{2,1,0:T(8,128)(2,1)}, bf16[2,128,128]{2,1,0:T(8,128)(2,1)S(1)}, u32[]{:S(2)}, u32[]{:S(2)}) collective-permute-start(bf16[2,128,128]{2,1,0:T(8,128)(2,1)} %get-tuple-element.24), channel_id=1, source_target_pairs={{0,8},{1,9},{2,10},{3,11},{4,12},{5,13},{6,14},{7,15},{8,16},{9,17... | collective-permute-start | bytes 196616 | tf_op jit(solution)/shard_map/ppermute | solution.py:333
  31.8 54.3 %copy-start.5 = (s32[168]{0:T(256)}, s32[168]{0:T(256)S(1)}, u32[]{:S(2)}) copy-start(s32[168]{0:T(256)S(1)} %reshape.60.table_ref.refs_0_) | copy-start | bytes 2020
  31.9 54.2 %copy-start.8 = (bf16[4,2,128,128]{3,2,1,0:T(8,128)(2,1)}, bf16[4,2,128,128]{3,2,1,0:T(8,128)(2,1)S(1)}, u32[]{:S(2)}) copy-start(bf16[4,2,128,128]{3,2,1,0:T(8,128)(2,1)S(1)} %pad_maximum_fusion.refs_3_) | copy-start | bytes 786436
  44.6 126.3 %reduce-scatter.2.cloned.1.call-start = ((), (), s32[]{:S(2)}) async-start(), calls=%async_computation.4 | async-start | bytes 2621440 | tf_op jit(solution)/shard_map/reduce_scatter | solution.py:421
  44.6 7.3 %collective-permute-start.6 = (bf16[4,2,128,128]{3,2,1,0:T(8,128)(2,1)S(1)}, bf16[4,2,128,128]{3,2,1,0:T(8,128)(2,1)S(1)}, u32[]{:S(2)}, u32[]{:S(2)}) collective-permute-start(bf16[4,2,128,128]{3,2,1,0:T(8,128)(2,1)S(1)} %pad_maximum_fusion.refs_3_), channel_id=1, source_target_pairs={{0,7},{1,0},{2,1},{3,2},{4,3},{5,4},{6,5},{7,6},{8,15},{9,8},{10,9... | collective-permute-start | bytes 786440 | tf_op jit(solution)/shard_map/ppermute | solution.py:339
  46.7 6.4 %collective-permute-start.3 = (bf16[4,2,128,128]{3,2,1,0:T(8,128)(2,1)S(1)}, bf16[4,2,128,128]{3,2,1,0:T(8,128)(2,1)S(1)}, u32[]{:S(2)}, u32[]{:S(2)}) collective-permute-start(bf16[4,2,128,128]{3,2,1,0:T(8,128)(2,1)S(1)} %pad_maximum_fusion.refs_3_), channel_id=1, source_target_pairs={{0,1},{1,2},{2,3},{3,4},{4,5},{5,6},{6,7},{7,0},{8,9},{9,10},{10,1... | collective-permute-start | bytes 786440 | tf_op jit(solution)/shard_map/ppermute | solution.py:339
  51.9 34.2 %copy-start.11 = (bf16[4,2,128,128]{3,2,1,0:T(8,128)(2,1)}, bf16[4,2,128,128]{3,2,1,0:T(8,128)(2,1)S(1)}, u32[]{:S(2)}) copy-start(bf16[4,2,128,128]{3,2,1,0:T(8,128)(2,1)S(1)} %collective-permute-done.6.refs_9_) | copy-start | bytes 786436
  51.9 6.4 %collective-permute-start.7 = (bf16[4,2,128,128]{3,2,1,0:T(8,128)(2,1)S(1)}, bf16[4,2,128,128]{3,2,1,0:T(8,128)(2,1)S(1)}, u32[]{:S(2)}, u32[]{:S(2)}) collective-permute-start(bf16[4,2,128,128]{3,2,1,0:T(8,128)(2,1)S(1)} %collective-permute-done.6.refs_9_), channel_id=1, source_target_pairs={{0,7},{1,0},{2,1},{3,2},{4,3},{5,4},{6,5},{7,6},{8,15},{9,8},{10,9... | collective-permute-start | bytes 786440 | tf_op jit(solution)/shard_map/ppermute | solution.py:339
  53.1 33.0 %copy-start.12 = (bf16[4,2,128,128]{3,2,1,0:T(8,128)(2,1)}, bf16[4,2,128,128]{3,2,1,0:T(8,128)(2,1)S(1)}, u32[]{:S(2)}) copy-start(bf16[4,2,128,128]{3,2,1,0:T(8,128)(2,1)S(1)} %collective-permute-done.3.refs_4_) | copy-start | bytes 786436
  53.1 6.7 %collective-permute-start.4 = (bf16[4,2,128,128]{3,2,1,0:T(8,128)(2,1)S(1)}, bf16[4,2,128,128]{3,2,1,0:T(8,128)(2,1)S(1)}, u32[]{:S(2)}, u32[]{:S(2)}) collective-permute-start(bf16[4,2,128,128]{3,2,1,0:T(8,128)(2,1)S(1)} %collective-permute-done.3.refs_4_), channel_id=1, source_target_pairs={{0,1},{1,2},{2,3},{3,4},{4,5},{5,6},{6,7},{7,0},{8,9},{9,10},{10,1... | collective-permute-start | bytes 786440 | tf_op jit(solution)/shard_map/ppermute | solution.py:339
  58.3 27.9 %copy-start.13 = (bf16[4,2,128,128]{3,2,1,0:T(8,128)(2,1)}, bf16[4,2,128,128]{3,2,1,0:T(8,128)(2,1)S(1)}, u32[]{:S(2)}) copy-start(bf16[4,2,128,128]{3,2,1,0:T(8,128)(2,1)S(1)} %collective-permute-done.7.refs_8_) | copy-start | bytes 786436
  58.3 7.8 %collective-permute-start.8 = (bf16[4,2,128,128]{3,2,1,0:T(8,128)(2,1)S(1)}, bf16[4,2,128,128]{3,2,1,0:T(8,128)(2,1)S(1)}, u32[]{:S(2)}, u32[]{:S(2)}) collective-permute-start(bf16[4,2,128,128]{3,2,1,0:T(8,128)(2,1)S(1)} %collective-permute-done.7.refs_8_), channel_id=1, source_target_pairs={{0,7},{1,0},{2,1},{3,2},{4,3},{5,4},{6,5},{7,6},{8,15},{9,8},{10,9... | collective-permute-start | bytes 786440 | tf_op jit(solution)/shard_map/ppermute | solution.py:339
  59.8 26.3 %copy-start.14 = (bf16[4,2,128,128]{3,2,1,0:T(8,128)(2,1)}, bf16[4,2,128,128]{3,2,1,0:T(8,128)(2,1)S(1)}, u32[]{:S(2)}) copy-start(bf16[4,2,128,128]{3,2,1,0:T(8,128)(2,1)S(1)} %collective-permute-done.4.refs_5_) | copy-start | bytes 786436
  59.8 8.2 %collective-permute-start.5 = (bf16[4,2,128,128]{3,2,1,0:T(8,128)(2,1)S(1)}, bf16[4,2,128,128]{3,2,1,0:T(8,128)(2,1)S(1)}, u32[]{:S(2)}, u32[]{:S(2)}) collective-permute-start(bf16[4,2,128,128]{3,2,1,0:T(8,128)(2,1)S(1)} %collective-permute-done.4.refs_5_), channel_id=1, source_target_pairs={{0,1},{1,2},{2,3},{3,4},{4,5},{5,6},{6,7},{7,0},{8,9},{9,10},{10,1... | collective-permute-start | bytes 786440 | tf_op jit(solution)/shard_map/ppermute | solution.py:339
  66.1 5.9 %collective-permute-start.10 = (bf16[2,2,128,128]{3,2,1,0:T(8,128)(2,1)S(1)}, bf16[2,2,128,128]{3,2,1,0:T(8,128)(2,1)S(1)}, u32[]{:S(2)}, u32[]{:S(2)}) collective-permute-start(bf16[2,2,128,128]{3,2,1,0:T(8,128)(2,1)S(1)} %slice.29), channel_id=1, source_target_pairs={{0,7},{1,0},{2,1},{3,2},{4,3},{5,4},{6,5},{7,6},{8,15},{9,8},{10,9... | collective-permute-start | bytes 393224 | tf_op jit(solution)/shard_map/ppermute | solution.py:339
  68.0 6.9 %collective-permute-start.9 = (bf16[2,2,128,128]{3,2,1,0:T(8,128)(2,1)S(1)}, bf16[2,2,128,128]{3,2,1,0:T(8,128)(2,1)S(1)}, u32[]{:S(2)}, u32[]{:S(2)}) collective-permute-start(bf16[2,2,128,128]{3,2,1,0:T(8,128)(2,1)S(1)} %slice.28), channel_id=1, source_target_pairs={{0,1},{1,2},{2,3},{3,4},{4,5},{5,6},{6,7},{7,0},{8,9},{9,10},{10,1... | collective-permute-start | bytes 393224 | tf_op jit(solution)/shard_map/ppermute | solution.py:339
  99.3 101.8 %all-gather.7.cloned.1.call-start = ((), (), s32[]{:S(2)}) async-start(), calls=%async_computation.6 | async-start | bytes 3096576 | tf_op jit(solution)/shard_map/all_gather | solution.py:449
  99.3 3.4 %collective-permute-start.11 = (bf16[4,84,16,128]{3,2,1,0:T(8,128)(2,1)}, bf16[4,84,16,128]{3,2,1,0:T(8,128)(2,1)S(1)}, u32[]{:S(2)}, u32[]{:S(2)}) collective-permute-start(bf16[4,84,16,128]{3,2,1,0:T(8,128)(2,1)} %get-tuple-element.29), channel_id=1, source_target_pairs={{0,32},{32,0},{64,96},{96,64},{128,160},{160,128},{192,224},{224,1... | collective-permute-start | bytes 4128776 | tf_op jit(solution)/shard_map/ppermute | solution.py:417
  99.7 9.4 %collective-permute-start.15 = (bf16[4,84,16,128]{3,2,1,0:T(8,128)(2,1)}, bf16[4,84,16,128]{3,2,1,0:T(8,128)(2,1)S(1)}, u32[]{:S(2)}, u32[]{:S(2)}) collective-permute-start(bf16[4,84,16,128]{3,2,1,0:T(8,128)(2,1)} %get-tuple-element.35), channel_id=1, source_target_pairs={{0,32},{32,0},{64,96},{96,64},{128,160},{160,128},{192,224},{224,1... | collective-permute-start | bytes 4128776 | tf_op jit(solution)/shard_map/ppermute | solution.py:417
  104.1 34.4 %copy-start.6 = (s32[168]{0:T(256)S(1)}, s32[168]{0:T(256)}, u32[]{:S(2)}) copy-start(s32[168]{0:T(256)} %copy-done.5) | copy-start | bytes 2020
  104.1 34.4 %copy-start.7 = (s32[14]{0:T(128)S(1)}, s32[14]{0:T(128)}, u32[]{:S(2)}) copy-start(s32[14]{0:T(128)} %reshape.61.refs_1_.count_ref) | copy-start | bytes 172
  105.4 17.7 %collective-permute-start.12 = (bf16[84,16,128]{2,1,0:T(8,128)(2,1)S(1)}, bf16[84,16,128]{2,1,0:T(8,128)(2,1)S(1)}, u32[]{:S(2)}, u32[]{:S(2)}) collective-permute-start(bf16[84,16,128]{2,1,0:T(8,128)(2,1)S(1)} %get-tuple-element.31), channel_id=1, source_target_pairs={{0,64},{32,96},{64,128},{96,160},{128,192},{160,224},{192,0},{224,... | collective-permute-start | bytes 1032200 | tf_op jit(solution)/shard_map/ppermute | solution.py:397
  105.7 17.4 %collective-permute-start.13 = (bf16[84,16,128]{2,1,0:T(8,128)(2,1)S(1)}, bf16[84,16,128]{2,1,0:T(8,128)(2,1)S(1)}, u32[]{:S(2)}, u32[]{:S(2)}) collective-permute-start(bf16[84,16,128]{2,1,0:T(8,128)(2,1)S(1)} %get-tuple-element.32), channel_id=1, source_target_pairs={{0,128},{32,160},{64,192},{96,224},{128,0},{160,32},{192,64},{224,... | collective-permute-start | bytes 1032200 | tf_op jit(solution)/shard_map/ppermute | solution.py:397
  107.2 16.7 %collective-permute-start.14 = (bf16[84,16,128]{2,1,0:T(8,128)(2,1)S(1)}, bf16[84,16,128]{2,1,0:T(8,128)(2,1)S(1)}, u32[]{:S(2)}, u32[]{:S(2)}) collective-permute-start(bf16[84,16,128]{2,1,0:T(8,128)(2,1)S(1)} %get-tuple-element.33), channel_id=1, source_target_pairs={{0,192},{32,224},{64,0},{96,32},{128,64},{160,96},{192,128},{224,1... | collective-permute-start | bytes 1032200 | tf_op jit(solution)/shard_map/ppermute | solution.py:397
  110.3 27.9 %collective-permute-start.16 = (bf16[84,16,128]{2,1,0:T(8,128)(2,1)S(1)}, bf16[84,16,128]{2,1,0:T(8,128)(2,1)S(1)}, u32[]{:S(2)}, u32[]{:S(2)}) collective-permute-start(bf16[84,16,128]{2,1,0:T(8,128)(2,1)S(1)} %get-tuple-element.37), channel_id=1, source_target_pairs={{0,64},{32,96},{64,128},{96,160},{128,192},{160,224},{192,0},{224,... | collective-permute-start | bytes 1032200 | tf_op jit(solution)/shard_map/ppermute | solution.py:397
  110.4 27.8 %collective-permute-start.17 = (bf16[84,16,128]{2,1,0:T(8,128)(2,1)S(1)}, bf16[84,16,128]{2,1,0:T(8,128)(2,1)S(1)}, u32[]{:S(2)}, u32[]{:S(2)}) collective-permute-start(bf16[84,16,128]{2,1,0:T(8,128)(2,1)S(1)} %get-tuple-element.38), channel_id=1, source_target_pairs={{0,128},{32,160},{64,192},{96,224},{128,0},{160,32},{192,64},{224,... | collective-permute-start | bytes 1032200 | tf_op jit(solution)/shard_map/ppermute | solution.py:397
  123.1 15.4 %collective-permute-start.18 = (bf16[84,16,128]{2,1,0:T(8,128)(2,1)S(1)}, bf16[84,16,128]{2,1,0:T(8,128)(2,1)S(1)}, u32[]{:S(2)}, u32[]{:S(2)}) collective-permute-start(bf16[84,16,128]{2,1,0:T(8,128)(2,1)S(1)} %get-tuple-element.39), channel_id=1, source_target_pairs={{0,192},{32,224},{64,0},{96,32},{128,64},{160,96},{192,128},{224,1... | collective-permute-start | bytes 1032200 | tf_op jit(solution)/shard_map/ppermute | solution.py:397
  (10 other events, 133.0 us)
Sparse Core Ops, SparseCore 0:
  44.7 41.3 all-gather.4
  99.4 31.9 reduce-scatter.1
  171.0 30.0 all-gather.6

commit v4 on v3

--- a/solution.py
+++ b/solution.py
@@ -48,14 +48,16 @@
 
 
 def slot_of(cols_ref, me, owned, panels, m, visit):
+    by = 65536 // panels + 1
+
     def step(k, carry):
         last, rank = carry
-        holder = cols_ref[m, me * owned + k] // panels
+        holder = (cols_ref[m, me * owned + k] * by) >> 16
         rank = jnp.where(holder == last, rank + 1, 0)
         visit(k, holder, rank)
         return holder, rank
 
-    lax.fori_loop(0, owned, step, (jnp.int32(-1), jnp.int32(0)), unroll=6)
+    lax.fori_loop(0, owned, step, (jnp.int32(-1), jnp.int32(0)), unroll=7)
 
 
 def send_kernel(panels, place_ref, cols_ref, tiles_ref, tokens_ref, out_ref, blocks_ref):
@@ -255,26 +257,40 @@
             copy.wait()
 
 
-def sum_kernel(in_ref, out_ref):
-    def step(k, acc):
-        return tuple(a + in_ref[k, i].astype(F32) for i, a in enumerate(acc))
-
-    count = in_ref.shape[1]
-    acc = lax.fori_loop(
-        0, in_ref.shape[0], step, tuple(jnp.zeros(in_ref.shape[2:], F32) for _ in range(count))
-    )
-    for i in range(count):
-        out_ref[:, i * BLOCK : (i + 1) * BLOCK] = acc[i].astype(BF16)
-
-
-def widen_kernel(in_ref, out_ref):
+def widen_kernel(where_ref, *refs):
+    pieces, (blocks_ref, out_hbm, flat_ref, in_ref, out_ref, in_sems, out_sems) = refs[:-7], refs[-7:]
     parts, count, part, _ = in_ref.shape
-
-    def step(i, carry):
-        out_ref[i] = in_ref[:, i].reshape(parts * part, BLOCK).astype(F32)
-        return carry
-
-    lax.fori_loop(0, count, step, 0, unroll=2)
+    cuts = in_sems.shape[1]
+    stores = out_sems.shape[0]
+    core, y = where_ref[4], where_ref[5]
+
+    def load(i, h):
+        chunk = lax.rem(y + 4 - i // 2, 4) * 2 + (1 - core if i % 2 else core)
+        at = pl.ds(h * (count // cuts), count // cuts)
+        return pltpu.make_async_copy(pieces[i].at[at], in_ref.at[chunk, at], in_sems.at[i, h])
+
+    def store(i):
+        at = pl.ds(i * (count // stores), count // stores)
+        return pltpu.make_async_copy(out_ref.at[at], out_hbm.at[at], out_sems.at[i])
+
+    for h in range(cuts):
+        for i in range(parts):
+            load(i, h).start()
+    for b in range(blocks_ref.shape[0]):
+        flat_ref[:, b * BLOCK : (b + 1) * BLOCK] = blocks_ref[b]
+    for i in range(stores):
+        if i % (stores // cuts) == 0:
+            for k in range(parts):
+                load(k, i // (stores // cuts)).wait()
+
+        def step(k, carry):
+            out_ref[k] = in_ref[:, k].reshape(parts * part, BLOCK).astype(F32)
+            return carry
+
+        lax.fori_loop(i * (count // stores), (i + 1) * (count // stores), step, 0, unroll=2)
+        store(i).start()
+    for i in range(stores):
+        store(i).wait()
 
 
 def whole(shape):
@@ -413,8 +429,11 @@
             name="core_sum",
         )(where, mine, other)
 
+    def swap(value):
+        return lax.ppermute(value, "dp", [(d, d ^ 1) for d in range(groups)])
+
     mine = [mine_g, mine_u]
-    other = [lax.ppermute(v, "dp", [(d, d ^ 1) for d in range(groups)]) for v in (other_g, other_u)]
+    other = [swap(other_g), swap(other_u)]
     sent = [reduced(mine[m], other[m]) for m in range(2)]
     came = [[sent[m][0]] + [around(sent[m][s], s) for s in (1, 2, 3)] for m in range(2)]
     columns = [[x * ring + z for x in range(sides)] for z in range(ring)]
@@ -445,27 +464,34 @@
         compiler_params=params,
         name="own_slots",
     )(where, tile_cols, exchange(returning))
-    own, row_terms = lax.optimization_barrier((own, row_terms))
-    full = lax.all_gather(own, "dp").reshape(groups, 2 * owned, part, BLOCK)
-    column = lax.all_to_all(
-        row_terms.reshape(ring, my_blocks, tok_rows, BLOCK), "mp", 0, 0, axis_index_groups=rows
+    own = own.reshape(2 * owned, part, BLOCK)
+    full = [own] + [around(own, s) for s in (1, 2, 3)]
+    full = [v for t in full for v in (t, swap(t))]
+    input_grad = lax.psum_scatter(
+        row_terms, "mp", scatter_dimension=0, axis_index_groups=rows, tiled=True
     )
-    input_grad = pl.pallas_call(
-        sum_kernel,
-        out_shape=jax.ShapeDtypeStruct(tokens.shape, BF16),
-        compiler_params=params,
-        name="input_sum",
-    )(column)
-    some = 2 * owned // 6
-    tile_grads = pl.pallas_call(
+    tile_grads, input_grad = pl.pallas_call(
         widen_kernel,
-        out_shape=jax.ShapeDtypeStruct((2 * owned, BLOCK, BLOCK), F32),
-        grid=(6,),
-        in_specs=[pl.BlockSpec((groups, some, part, BLOCK), lambda i: (0, i, 0, 0))],
-        out_specs=pl.BlockSpec((some, BLOCK, BLOCK), lambda i: (i, 0, 0)),
-        compiler_params=params,
+        out_shape=(
+            jax.ShapeDtypeStruct((2 * owned, BLOCK, BLOCK), F32),
+            jax.ShapeDtypeStruct(tokens.shape, BF16),
+        ),
+        grid_spec=pltpu.PrefetchScalarGridSpec(
+            num_scalar_prefetch=1,
+            grid=(1,),
+            in_specs=[anywhere] * groups + [whole((my_blocks, tok_rows, BLOCK))],
+            out_specs=(anywhere, whole(tokens.shape)),
+            scratch_shapes=[
+                pltpu.VMEM((groups, 2 * owned, part, BLOCK), BF16),
+                pltpu.VMEM((2 * owned, BLOCK, BLOCK), F32),
+                pltpu.SemaphoreType.DMA((groups, 2)),
+                pltpu.SemaphoreType.DMA((6,)),
+            ],
+        ),
+        compiler_params=alone,
         name="widen",
-    )(full).reshape(tiles.shape)
+    )(where, *full, input_grad)
+    tile_grads = tile_grads.reshape(tiles.shape)
     return hidden, input_grad, tile_grads
 
 

time: 213 us -> 209 us (0.981)
  blocking collectives: 47.2 us -> 0 us
  starting transfers between devices: 30.1 us -> 59.9 us
  waiting for transfers between devices: 83.7 us -> 95 us
    all_to_all x2 -> x0, blocking collectives: 47.2 us -> none  [the longest x1 28.9 us: exchange(): lax.all_to_all(values.reshape(shape), 'mp', 0, 0).reshape(values.shape)]
    all_to_all x1 -> x2, waiting for transfers between devices: 10.7 us -> 28.7 us  [exchange(): lax.all_to_all(values.reshape(shape), 'mp', 0, 0).reshape(values.shape)]
    ppermute x2 -> x6, starting transfers between devices: 0.6 us -> 16.7 us  [swap(): return lax.ppermute(value, 'dp', [(d, d ^ 1) for d in range(groups)])]
    all_gather x1 -> x0, waiting for transfers between devices: 11.2 us -> none  [per_device(): full = lax.all_gather(own, 'dp').reshape(groups, 2 * owned, part, BLOCK)]
    all_to_all x1 -> x2, starting transfers between devices: 12 us -> 21.3 us  [exchange(): lax.all_to_all(values.reshape(shape), 'mp', 0, 0).reshape(values.shape)]
    ppermute x6 -> x9, starting transfers between devices: 5.29 us -> 9.54 us  [around(): return lax.ppermute(value, 'dp', pairs)]
    ppermute x6 -> x9, waiting for transfers between devices: 26.6 us -> 29.1 us  [around(): return lax.ppermute(value, 'dp', pairs)]
    pallas_call x2 -> x1, Pallas kernels: 4.24 us -> 6.25 us  [per_device(): pl.pallas_call(widen_kernel, out_shape=(jax.ShapeDtypeStruct((2 * owned,...]
  transfers between devices with their start and end apart: 23 -> 31, of which waited for: 15 -> 18; matrix products, arithmetic and copies ran while one was open for 3% -> 3% of each run, Pallas kernels for 3% -> 3%
where the time goes in v4:
time: 209 us; the launch traced here: 207 us
  waiting for transfers between devices  95 us (45%)
  starting transfers between devices  59.9 us (29%)
  Pallas kernels  30.1 us (14%)
  between operations  14.2 us (7%)
  other arithmetic  4.39 us (2%)
  local copies, waits for them, and re-layouts  3.78 us (2%)
    ppermute x9, waiting for transfers between devices, around(): return lax.ppermute(value, 'dp', pairs)  29.1 us
    all_to_all x2, waiting for transfers between devices, exchange(): lax.all_to_all(values.reshape(shape), 'mp', 0, 0).reshape(values.shape)  28.7 us
    all_to_all x2, starting transfers between devices, exchange(): lax.all_to_all(values.reshape(shape), 'mp', 0, 0).reshape(values.shape)  21.3 us
    ppermute x8, waiting for transfers between devices, along(): return lax.ppermute(value, 'mp', pairs)  21.1 us
    ppermute x6, starting transfers between devices, swap(): return lax.ppermute(value, 'dp', [(d, d ^ 1) for d in range(groups)])  16.7 us
    pallas_call x1, Pallas kernels, per_device(): pl.pallas_call(lambda *refs: main_kernel(sides, ring, panels, *refs), out...  13.2 us
    all_gather x1, waiting for transfers between devices, per_device(): held = lax.all_gather(ordered, 'dp')  11.2 us
    ppermute x9, starting transfers between devices, around(): return lax.ppermute(value, 'dp', pairs)  9.54 us
  transfers between devices with their start and end apart: 31, of which 18 were waited for; matrix products, arithmetic and copies ran while one was open for 3% of the time, Pallas kernels for 3%

profile of v4, /device:TPU:1, one launch (start us, length us, event | category | flops | bytes accessed | tf_op | source)
XLA Modules:
  0.0 207.3 jit_solution(1111414591694442374)
XLA Ops:
  7.9 3.1 %send_pack.1 = (bf16[192,16,128]{2,1,0:T(8,128)(2,1)}, bf16[2,128,128]{2,1,0:T(8,128)(2,1)}) custom-call(s32[6]{0:T(128)} %stack.42.refs_0_.refs_2_.where_ref, s32[2,1344]{1,0:T(2,128)} %refs_1_.3, bf16[2,42,128,128]{3,2,1,0:T(8,128)(2,1)} %refs_2_.1, bf16[128,256]{1,0:T(8,128)(2,1)} %refs_3_.1), custom_call_target="tpu_custom_call" | custom-call | tf_op jit(solution)/shard_map/send_pack/pallas_call | solution.py:320
  11.0 12.0 %all-to-all-start = ((bf16[32,6,16,128]{3,2,1,0:T(8,128)(2,1)}), bf16[32,6,16,128]{3,2,1,0:T(8,128)(2,1)S(1)}, u32[]{:S(2)}, u32[]{:S(2)}) async-start(bf16[32,6,16,128]{3,2,1,0:T(8,128)(2,1)} %bitcast.33), calls=%async_computation | async-start | bytes 1572864 | tf_op jit(solution)/shard_map/all_to_all | solution.py:341
  23.1 2.6 %collective-permute-start.2 = (bf16[2,128,128]{2,1,0:T(8,128)(2,1)}, bf16[2,128,128]{2,1,0:T(8,128)(2,1)S(1)}, u32[]{:S(2)}, u32[]{:S(2)}) collective-permute-start(bf16[2,128,128]{2,1,0:T(8,128)(2,1)} %get-tuple-element.24), channel_id=1, source_target_pairs={{0,24},{1,25},{2,26},{3,27},{4,28},{5,29},{6,30},{7,31},{8,0},{9,1... | collective-permute-start | bytes 196616 | tf_op jit(solution)/shard_map/ppermute | solution.py:349
  28.2 3.2 %select_reduce_fusion = s32[7,2,12]{2,1,0:T(2,128)S(1)} fusion(s32[2,32,42]{2,1,0:T(8,128)S(1)} %get-tuple-element.46, s32[7,2,32,42]{3,2,1,0:T(8,128)S(1)} %add_select_fusion), kind=kLoop, calls=%fused_computation | loop fusion | flops 677208 | bytes 86688 | tf_op jit(solution)/shard_map/reduce_sum | solution.py:46
  31.6 10.7 %all-to-all-done = bf16[32,6,16,128]{3,2,1,0:T(8,128)(2,1)S(1)} async-done(((bf16[32,6,16,128]{3,2,1,0:T(8,128)(2,1)}), bf16[32,6,16,128]{3,2,1,0:T(8,128)(2,1)S(1)}, u32[]{:S(2)}, u32[]{:S(2)}) %all-to-all-start) | async-done | bytes 786464 | tf_op jit(solution)/shard_map/all_to_all | solution.py:341
  42.3 2.0 sort_slots.1
  44.3 2.1 %collective-permute-start.6 = (bf16[4,2,128,128]{3,2,1,0:T(8,128)(2,1)S(1)}, bf16[4,2,128,128]{3,2,1,0:T(8,128)(2,1)S(1)}, u32[]{:S(2)}, u32[]{:S(2)}) collective-permute-start(bf16[4,2,128,128]{3,2,1,0:T(8,128)(2,1)S(1)} %pad_maximum_fusion.refs_3_), channel_id=1, source_target_pairs={{0,7},{1,0},{2,1},{3,2},{4,3},{5,4},{6,5},{7,6},{8,15},{9,8},{10,9... | collective-permute-start | bytes 786440 | tf_op jit(solution)/shard_map/ppermute | solution.py:355
  46.4 1.5 collective-permute-start.3
  47.9 3.7 %collective-permute-done.6.refs_9_ = bf16[4,2,128,128]{3,2,1,0:T(8,128)(2,1)S(1)} collective-permute-done((bf16[4,2,128,128]{3,2,1,0:T(8,128)(2,1)S(1)}, bf16[4,2,128,128]{3,2,1,0:T(8,128)(2,1)S(1)}, u32[]{:S(2)}, u32[]{:S(2)}) %collective-permute-start.6) | collective-permute-done | bytes 262176 | tf_op jit(solution)/shard_map/ppermute | solution.py:355
  53.2 4.8 %collective-permute-done.7.refs_8_ = bf16[4,2,128,128]{3,2,1,0:T(8,128)(2,1)S(1)} collective-permute-done((bf16[4,2,128,128]{3,2,1,0:T(8,128)(2,1)S(1)}, bf16[4,2,128,128]{3,2,1,0:T(8,128)(2,1)S(1)}, u32[]{:S(2)}, u32[]{:S(2)}) %collective-permute-start.7) | collective-permute-done | bytes 262176 | tf_op jit(solution)/shard_map/ppermute | solution.py:355
  59.7 6.1 %collective-permute-done.8.refs_7_ = bf16[4,2,128,128]{3,2,1,0:T(8,128)(2,1)S(1)} collective-permute-done((bf16[4,2,128,128]{3,2,1,0:T(8,128)(2,1)S(1)}, bf16[4,2,128,128]{3,2,1,0:T(8,128)(2,1)S(1)}, u32[]{:S(2)}, u32[]{:S(2)}) %collective-permute-start.8) | collective-permute-done | bytes 262176 | tf_op jit(solution)/shard_map/ppermute | solution.py:355
  65.8 1.7 collective-permute-start.10
  68.5 3.2 %collective-permute-done.10.refs_11_ = bf16[2,2,128,128]{3,2,1,0:T(8,128)(2,1)S(1)} collective-permute-done((bf16[2,2,128,128]{3,2,1,0:T(8,128)(2,1)S(1)}, bf16[2,2,128,128]{3,2,1,0:T(8,128)(2,1)S(1)}, u32[]{:S(2)}, u32[]{:S(2)}) %collective-permute-start.10) | collective-permute-done | bytes 131104 | tf_op jit(solution)/shard_map/ppermute | solution.py:355
  71.7 2.9 %collective-permute-done.9.refs_10_ = bf16[2,2,128,128]{3,2,1,0:T(8,128)(2,1)S(1)} collective-permute-done((bf16[2,2,128,128]{3,2,1,0:T(8,128)(2,1)S(1)}, bf16[2,2,128,128]{3,2,1,0:T(8,128)(2,1)S(1)}, u32[]{:S(2)}, u32[]{:S(2)}) %collective-permute-start.9) | collective-permute-done | bytes 131104 | tf_op jit(solution)/shard_map/ppermute | solution.py:355
  74.6 11.2 %all-gather.3.cloned.1.call-done = bf16[1344,16,128]{2,1,0:T(8,128)(2,1)} async-done(((bf16[168,16,128]{2,1,0:T(8,128)(2,1)}), bf16[1344,16,128]{2,1,0:T(8,128)(2,1)}) %all-gather.3.cloned.1.call-update) | async-done | bytes 5505040 | tf_op jit(solution)/shard_map/all_gather | solution.py:372
  85.9 13.2 %gated_pair.1 = (bf16[128,896]{1,0:T(8,128)(2,1)}, bf16[4,84,16,128]{3,2,1,0:T(8,128)(2,1)}, bf16[4,84,16,128]{3,2,1,0:T(8,128)(2,1)}, bf16[4,84,16,128]{3,2,1,0...) custom-call(s32[168]{0:T(256)} %copy-done.5, s32[14]{0:T(128)} %reshape.58.refs_1_.count_ref, ...), custom_call_target="tpu_custom_call" | custom-call | tf_op jit(solution)/shard_map/gated_pair/pallas_call | solution.py:382
  99.7 2.8 %collective-permute-done.11.other_ref = bf16[4,84,16,128]{3,2,1,0:T(8,128)(2,1)S(1)} collective-permute-done((bf16[4,84,16,128]{3,2,1,0:T(8,128)(2,1)}, bf16[4,84,16,128]{3,2,1,0:T(8,128)(2,1)S(1)}, u32[]{:S(2)}, u32[]{:S(2)}) %collective-permute-start.11) | collective-permute-done | bytes 1376288 | tf_op jit(solution)/shard_map/ppermute | solution.py:433
  102.5 1.3 copy-done.2
  105.4 1.5 collective-permute-start.13
  106.9 1.8 collective-permute-start.14
  110.0 1.6 collective-permute-start.17
  111.6 11.2 %collective-permute-done.12.refs_1_ = bf16[84,16,128]{2,1,0:T(8,128)(2,1)S(1)} collective-permute-done((bf16[84,16,128]{2,1,0:T(8,128)(2,1)S(1)}, bf16[84,16,128]{2,1,0:T(8,128)(2,1)S(1)}, u32[]{:S(2)}, u32[]{:S(2)}) %collective-permute-start.12) | collective-permute-done | bytes 344096 | tf_op jit(solution)/shard_map/ppermute | solution.py:413
  123.6 14.3 %collective-permute-done.16.refs_5_ = bf16[84,16,128]{2,1,0:T(8,128)(2,1)S(1)} collective-permute-done((bf16[84,16,128]{2,1,0:T(8,128)(2,1)S(1)}, bf16[84,16,128]{2,1,0:T(8,128)(2,1)S(1)}, u32[]{:S(2)}, u32[]{:S(2)}) %collective-permute-start.16) | collective-permute-done | bytes 344096 | tf_op jit(solution)/shard_map/ppermute | solution.py:413
  138.3 2.0 unsort_slots.1
  140.3 9.3 %all-to-all-start.1 = ((bf16[32,6,16,128]{3,2,1,0:T(8,128)(2,1)}), bf16[32,6,16,128]{3,2,1,0:T(8,128)(2,1)S(1)}, u32[]{:S(2)}, u32[]{:S(2)}) async-start(bf16[32,6,16,128]{3,2,1,0:T(8,128)(2,1)} %bitcast.15), calls=%async_computation.1 | async-start | bytes 1572864 | tf_op jit(solution)/shard_map/all_to_all | solution.py:341
  150.4 18.1 %all-to-all-done.1 = bf16[32,6,16,128]{3,2,1,0:T(8,128)(2,1)S(1)} async-done(((bf16[32,6,16,128]{3,2,1,0:T(8,128)(2,1)}), bf16[32,6,16,128]{3,2,1,0:T(8,128)(2,1)S(1)}, u32[]{:S(2)}, u32[]{:S(2)}) %all-to-all-start.1) | async-done | bytes 786464 | tf_op jit(solution)/shard_map/all_to_all | solution.py:341
  169.6 3.6 %collective-permute-start.24 = (bf16[84,16,128]{2,1,0:T(8,128)(2,1)S(1)}, bf16[84,16,128]{2,1,0:T(8,128)(2,1)S(1)}, u32[]{:S(2)}, u32[]{:S(2)}) collective-permute-start(bf16[84,16,128]{2,1,0:T(8,128)(2,1)S(1)} %bitcast.25), channel_id=1, source_target_pairs={{0,192},{32,224},{64,0},{96,32},{128,64},{160,96},{192,128},{224,1... | collective-permute-start | bytes 1032200 | tf_op jit(solution)/shard_map/ppermute | solution.py:413
  173.9 5.8 %collective-permute-start.19 = (bf16[84,16,128]{2,1,0:T(8,128)(2,1)S(1)}, bf16[84,16,128]{2,1,0:T(8,128)(2,1)S(1)}, u32[]{:S(2)}, u32[]{:S(2)}) collective-permute-start(bf16[84,16,128]{2,1,0:T(8,128)(2,1)S(1)} %bitcast.28), channel_id=1, source_target_pairs={{0,32},{32,0},{64,96},{96,64},{128,160},{160,128},{192,224},{224,1... | collective-permute-start | bytes 1032200 | tf_op jit(solution)/shard_map/ppermute | solution.py:433
  179.7 2.0 collective-permute-done.24.refs_6_
  181.6 7.2 %collective-permute-start.25 = (bf16[84,16,128]{2,1,0:T(8,128)(2,1)S(1)}, bf16[84,16,128]{2,1,0:T(8,128)(2,1)S(1)}, u32[]{:S(2)}, u32[]{:S(2)}) collective-permute-start(bf16[84,16,128]{2,1,0:T(8,128)(2,1)S(1)} %collective-permute-done.24.refs_6_), channel_id=1, source_target_pairs={{0,32},{32,0},{64,96},{96,64},{128,160},{160,128},{192,224},{224,1... | collective-permute-start | bytes 1032200 | tf_op jit(solution)/shard_map/ppermute | solution.py:433
  189.6 2.9 %collective-permute-start.21 = (bf16[84,16,128]{2,1,0:T(8,128)(2,1)S(1)}, bf16[84,16,128]{2,1,0:T(8,128)(2,1)S(1)}, u32[]{:S(2)}, u32[]{:S(2)}) collective-permute-start(bf16[84,16,128]{2,1,0:T(8,128)(2,1)S(1)} %collective-permute-done.20.refs_2_), channel_id=1, source_target_pairs={{0,32},{32,0},{64,96},{96,64},{128,160},{160,128},{192,224},{224,1... | collective-permute-start | bytes 1032200 | tf_op jit(solution)/shard_map/ppermute | solution.py:433
  194.5 6.3 %widen.1 = (f32[84,128,128]{2,1,0:T(8,128)}, bf16[128,256]{1,0:T(8,128)(2,1)}) custom-call(s32[6]{0:T(128)} %stack.42.refs_0_.refs_2_.where_ref, bf16[84,16,128]{2,1,0:T(8,128)(2,1)} %bitcast.29, bf16[84,16,128]{2,1,0:T(8,128)(2,1)} %copy-done.14, bf16[84,16,128]{2,1,0:T(8,128)(2,1)} %copy-done.13, bf16[84,16,128]{2,1,0:T(8,128)(2,1)} %copy-done.17, ...), custom_call_target="tpu_custom_call" | custom-call | tf_op jit(solution)/shard_map/widen/pallas_call | solution.py:473
  (111 shorter events, 17.6 us)
Async XLA Ops:
  11.0 31.3 %all-to-all-start = ((bf16[32,6,16,128]{3,2,1,0:T(8,128)(2,1)}), bf16[32,6,16,128]{3,2,1,0:T(8,128)(2,1)S(1)}, u32[]{:S(2)}, u32[]{:S(2)}) async-start(bf16[32,6,16,128]{3,2,1,0:T(8,128)(2,1)} %bitcast.33), calls=%async_computation | async-start | bytes 1572864 | tf_op jit(solution)/shard_map/all_to_all | solution.py:341
  23.0 62.8 %all-gather.3.cloned.1.call-start = ((), (), s32[]{:S(2)}) async-start(), calls=%async_computation.6 | async-start | bytes 6193152 | tf_op jit(solution)/shard_map/all_gather | solution.py:372
  23.1 8.4 %collective-permute-start.2 = (bf16[2,128,128]{2,1,0:T(8,128)(2,1)}, bf16[2,128,128]{2,1,0:T(8,128)(2,1)S(1)}, u32[]{:S(2)}, u32[]{:S(2)}) collective-permute-start(bf16[2,128,128]{2,1,0:T(8,128)(2,1)} %get-tuple-element.24), channel_id=1, source_target_pairs={{0,24},{1,25},{2,26},{3,27},{4,28},{5,29},{6,30},{7,31},{8,0},{9,1... | collective-permute-start | bytes 196616 | tf_op jit(solution)/shard_map/ppermute | solution.py:349
  25.6 5.9 %collective-permute-start.1 = (bf16[2,128,128]{2,1,0:T(8,128)(2,1)}, bf16[2,128,128]{2,1,0:T(8,128)(2,1)S(1)}, u32[]{:S(2)}, u32[]{:S(2)}) collective-permute-start(bf16[2,128,128]{2,1,0:T(8,128)(2,1)} %get-tuple-element.24), channel_id=1, source_target_pairs={{0,16},{1,17},{2,18},{3,19},{4,20},{5,21},{6,22},{7,23},{8,24},{9,... | collective-permute-start | bytes 196616 | tf_op jit(solution)/shard_map/ppermute | solution.py:349
  26.2 5.4 %collective-permute-start = (bf16[2,128,128]{2,1,0:T(8,128)(2,1)}, bf16[2,128,128]{2,1,0:T(8,128)(2,1)S(1)}, u32[]{:S(2)}, u32[]{:S(2)}) collective-permute-start(bf16[2,128,128]{2,1,0:T(8,128)(2,1)} %get-tuple-element.24), channel_id=1, source_target_pairs={{0,8},{1,9},{2,10},{3,11},{4,12},{5,13},{6,14},{7,15},{8,16},{9,17... | collective-permute-start | bytes 196616 | tf_op jit(solution)/shard_map/ppermute | solution.py:349
  31.4 54.3 %copy-start.5 = (s32[168]{0:T(256)}, s32[168]{0:T(256)S(1)}, u32[]{:S(2)}) copy-start(s32[168]{0:T(256)S(1)} %reshape.57.table_ref.refs_0_) | copy-start | bytes 2020
  44.3 105.5 %reduce-scatter.3.cloned.1.call-start = ((), (), s32[]{:S(2)}) async-start(), calls=%async_computation.4 | async-start | bytes 2621440 | tf_op jit(solution)/shard_map/reduce_scatter | solution.py:440
  44.3 7.3 %collective-permute-start.6 = (bf16[4,2,128,128]{3,2,1,0:T(8,128)(2,1)S(1)}, bf16[4,2,128,128]{3,2,1,0:T(8,128)(2,1)S(1)}, u32[]{:S(2)}, u32[]{:S(2)}) collective-permute-start(bf16[4,2,128,128]{3,2,1,0:T(8,128)(2,1)S(1)} %pad_maximum_fusion.refs_3_), channel_id=1, source_target_pairs={{0,7},{1,0},{2,1},{3,2},{4,3},{5,4},{6,5},{7,6},{8,15},{9,8},{10,9... | collective-permute-start | bytes 786440 | tf_op jit(solution)/shard_map/ppermute | solution.py:355
  46.4 6.4 %collective-permute-start.3 = (bf16[4,2,128,128]{3,2,1,0:T(8,128)(2,1)S(1)}, bf16[4,2,128,128]{3,2,1,0:T(8,128)(2,1)S(1)}, u32[]{:S(2)}, u32[]{:S(2)}) collective-permute-start(bf16[4,2,128,128]{3,2,1,0:T(8,128)(2,1)S(1)} %pad_maximum_fusion.refs_3_), channel_id=1, source_target_pairs={{0,1},{1,2},{2,3},{3,4},{4,5},{5,6},{6,7},{7,0},{8,9},{9,10},{10,1... | collective-permute-start | bytes 786440 | tf_op jit(solution)/shard_map/ppermute | solution.py:355
  51.6 6.4 %collective-permute-start.7 = (bf16[4,2,128,128]{3,2,1,0:T(8,128)(2,1)S(1)}, bf16[4,2,128,128]{3,2,1,0:T(8,128)(2,1)S(1)}, u32[]{:S(2)}, u32[]{:S(2)}) collective-permute-start(bf16[4,2,128,128]{3,2,1,0:T(8,128)(2,1)S(1)} %collective-permute-done.6.refs_9_), channel_id=1, source_target_pairs={{0,7},{1,0},{2,1},{3,2},{4,3},{5,4},{6,5},{7,6},{8,15},{9,8},{10,9... | collective-permute-start | bytes 786440 | tf_op jit(solution)/shard_map/ppermute | solution.py:355
  52.8 6.7 %collective-permute-start.4 = (bf16[4,2,128,128]{3,2,1,0:T(8,128)(2,1)S(1)}, bf16[4,2,128,128]{3,2,1,0:T(8,128)(2,1)S(1)}, u32[]{:S(2)}, u32[]{:S(2)}) collective-permute-start(bf16[4,2,128,128]{3,2,1,0:T(8,128)(2,1)S(1)} %collective-permute-done.3.refs_4_), channel_id=1, source_target_pairs={{0,1},{1,2},{2,3},{3,4},{4,5},{5,6},{6,7},{7,0},{8,9},{9,10},{10,1... | collective-permute-start | bytes 786440 | tf_op jit(solution)/shard_map/ppermute | solution.py:355
  58.0 7.8 %collective-permute-start.8 = (bf16[4,2,128,128]{3,2,1,0:T(8,128)(2,1)S(1)}, bf16[4,2,128,128]{3,2,1,0:T(8,128)(2,1)S(1)}, u32[]{:S(2)}, u32[]{:S(2)}) collective-permute-start(bf16[4,2,128,128]{3,2,1,0:T(8,128)(2,1)S(1)} %collective-permute-done.7.refs_8_), channel_id=1, source_target_pairs={{0,7},{1,0},{2,1},{3,2},{4,3},{5,4},{6,5},{7,6},{8,15},{9,8},{10,9... | collective-permute-start | bytes 786440 | tf_op jit(solution)/shard_map/ppermute | solution.py:355
  59.5 8.2 %collective-permute-start.5 = (bf16[4,2,128,128]{3,2,1,0:T(8,128)(2,1)S(1)}, bf16[4,2,128,128]{3,2,1,0:T(8,128)(2,1)S(1)}, u32[]{:S(2)}, u32[]{:S(2)}) collective-permute-start(bf16[4,2,128,128]{3,2,1,0:T(8,128)(2,1)S(1)} %collective-permute-done.4.refs_5_), channel_id=1, source_target_pairs={{0,1},{1,2},{2,3},{3,4},{4,5},{5,6},{6,7},{7,0},{8,9},{9,10},{10,1... | collective-permute-start | bytes 786440 | tf_op jit(solution)/shard_map/ppermute | solution.py:355
  65.8 5.9 %collective-permute-start.10 = (bf16[2,2,128,128]{3,2,1,0:T(8,128)(2,1)S(1)}, bf16[2,2,128,128]{3,2,1,0:T(8,128)(2,1)S(1)}, u32[]{:S(2)}, u32[]{:S(2)}) collective-permute-start(bf16[2,2,128,128]{3,2,1,0:T(8,128)(2,1)S(1)} %slice.29), channel_id=1, source_target_pairs={{0,7},{1,0},{2,1},{3,2},{4,3},{5,4},{6,5},{7,6},{8,15},{9,8},{10,9... | collective-permute-start | bytes 393224 | tf_op jit(solution)/shard_map/ppermute | solution.py:355
  67.7 6.9 %collective-permute-start.9 = (bf16[2,2,128,128]{3,2,1,0:T(8,128)(2,1)S(1)}, bf16[2,2,128,128]{3,2,1,0:T(8,128)(2,1)S(1)}, u32[]{:S(2)}, u32[]{:S(2)}) collective-permute-start(bf16[2,2,128,128]{3,2,1,0:T(8,128)(2,1)S(1)} %slice.28), channel_id=1, source_target_pairs={{0,1},{1,2},{2,3},{3,4},{4,5},{5,6},{6,7},{7,0},{8,9},{9,10},{10,1... | collective-permute-start | bytes 393224 | tf_op jit(solution)/shard_map/ppermute | solution.py:355
  99.1 3.4 %collective-permute-start.11 = (bf16[4,84,16,128]{3,2,1,0:T(8,128)(2,1)}, bf16[4,84,16,128]{3,2,1,0:T(8,128)(2,1)S(1)}, u32[]{:S(2)}, u32[]{:S(2)}) collective-permute-start(bf16[4,84,16,128]{3,2,1,0:T(8,128)(2,1)} %get-tuple-element.29), channel_id=1, source_target_pairs={{0,32},{32,0},{64,96},{96,64},{128,160},{160,128},{192,224},{224,1... | collective-permute-start | bytes 4128776 | tf_op jit(solution)/shard_map/ppermute | solution.py:433
  99.4 9.3 %collective-permute-start.15 = (bf16[4,84,16,128]{3,2,1,0:T(8,128)(2,1)}, bf16[4,84,16,128]{3,2,1,0:T(8,128)(2,1)S(1)}, u32[]{:S(2)}, u32[]{:S(2)}) collective-permute-start(bf16[4,84,16,128]{3,2,1,0:T(8,128)(2,1)} %get-tuple-element.35), channel_id=1, source_target_pairs={{0,32},{32,0},{64,96},{96,64},{128,160},{160,128},{192,224},{224,1... | collective-permute-start | bytes 4128776 | tf_op jit(solution)/shard_map/ppermute | solution.py:433
  105.1 17.8 %collective-permute-start.12 = (bf16[84,16,128]{2,1,0:T(8,128)(2,1)S(1)}, bf16[84,16,128]{2,1,0:T(8,128)(2,1)S(1)}, u32[]{:S(2)}, u32[]{:S(2)}) collective-permute-start(bf16[84,16,128]{2,1,0:T(8,128)(2,1)S(1)} %get-tuple-element.31), channel_id=1, source_target_pairs={{0,64},{32,96},{64,128},{96,160},{128,192},{160,224},{192,0},{224,... | collective-permute-start | bytes 1032200 | tf_op jit(solution)/shard_map/ppermute | solution.py:413
  105.4 17.5 %collective-permute-start.13 = (bf16[84,16,128]{2,1,0:T(8,128)(2,1)S(1)}, bf16[84,16,128]{2,1,0:T(8,128)(2,1)S(1)}, u32[]{:S(2)}, u32[]{:S(2)}) collective-permute-start(bf16[84,16,128]{2,1,0:T(8,128)(2,1)S(1)} %get-tuple-element.32), channel_id=1, source_target_pairs={{0,128},{32,160},{64,192},{96,224},{128,0},{160,32},{192,64},{224,... | collective-permute-start | bytes 1032200 | tf_op jit(solution)/shard_map/ppermute | solution.py:413
  106.9 16.8 %collective-permute-start.14 = (bf16[84,16,128]{2,1,0:T(8,128)(2,1)S(1)}, bf16[84,16,128]{2,1,0:T(8,128)(2,1)S(1)}, u32[]{:S(2)}, u32[]{:S(2)}) collective-permute-start(bf16[84,16,128]{2,1,0:T(8,128)(2,1)S(1)} %get-tuple-element.33), channel_id=1, source_target_pairs={{0,192},{32,224},{64,0},{96,32},{128,64},{160,96},{192,128},{224,1... | collective-permute-start | bytes 1032200 | tf_op jit(solution)/shard_map/ppermute | solution.py:413
  110.0 28.0 %collective-permute-start.16 = (bf16[84,16,128]{2,1,0:T(8,128)(2,1)S(1)}, bf16[84,16,128]{2,1,0:T(8,128)(2,1)S(1)}, u32[]{:S(2)}, u32[]{:S(2)}) collective-permute-start(bf16[84,16,128]{2,1,0:T(8,128)(2,1)S(1)} %get-tuple-element.37), channel_id=1, source_target_pairs={{0,64},{32,96},{64,128},{96,160},{128,192},{160,224},{192,0},{224,... | collective-permute-start | bytes 1032200 | tf_op jit(solution)/shard_map/ppermute | solution.py:413
  110.0 27.9 %collective-permute-start.17 = (bf16[84,16,128]{2,1,0:T(8,128)(2,1)S(1)}, bf16[84,16,128]{2,1,0:T(8,128)(2,1)S(1)}, u32[]{:S(2)}, u32[]{:S(2)}) collective-permute-start(bf16[84,16,128]{2,1,0:T(8,128)(2,1)S(1)} %get-tuple-element.38), channel_id=1, source_target_pairs={{0,128},{32,160},{64,192},{96,224},{128,0},{160,32},{192,64},{224,... | collective-permute-start | bytes 1032200 | tf_op jit(solution)/shard_map/ppermute | solution.py:413
  122.9 15.4 %collective-permute-start.18 = (bf16[84,16,128]{2,1,0:T(8,128)(2,1)S(1)}, bf16[84,16,128]{2,1,0:T(8,128)(2,1)S(1)}, u32[]{:S(2)}, u32[]{:S(2)}) collective-permute-start(bf16[84,16,128]{2,1,0:T(8,128)(2,1)S(1)} %get-tuple-element.39), channel_id=1, source_target_pairs={{0,192},{32,224},{64,0},{96,32},{128,64},{160,96},{192,128},{224,1... | collective-permute-start | bytes 1032200 | tf_op jit(solution)/shard_map/ppermute | solution.py:413
  140.3 28.2 %all-to-all-start.1 = ((bf16[32,6,16,128]{3,2,1,0:T(8,128)(2,1)}), bf16[32,6,16,128]{3,2,1,0:T(8,128)(2,1)S(1)}, u32[]{:S(2)}, u32[]{:S(2)}) async-start(bf16[32,6,16,128]{3,2,1,0:T(8,128)(2,1)} %bitcast.15), calls=%async_computation.1 | async-start | bytes 1572864 | tf_op jit(solution)/shard_map/all_to_all | solution.py:341
  149.6 44.1 %reduce-scatter.5.cloned.1.call-start = ((), (), s32[]{:S(2)}) async-start(), calls=%async_computation.5 | async-start | bytes 589824 | tf_op jit(solution)/shard_map/reduce_scatter | solution.py:470
  169.6 12.0 %collective-permute-start.24 = (bf16[84,16,128]{2,1,0:T(8,128)(2,1)S(1)}, bf16[84,16,128]{2,1,0:T(8,128)(2,1)S(1)}, u32[]{:S(2)}, u32[]{:S(2)}) collective-permute-start(bf16[84,16,128]{2,1,0:T(8,128)(2,1)S(1)} %bitcast.25), channel_id=1, source_target_pairs={{0,192},{32,224},{64,0},{96,32},{128,64},{160,96},{192,128},{224,1... | collective-permute-start | bytes 1032200 | tf_op jit(solution)/shard_map/ppermute | solution.py:413
  173.2 15.7 %collective-permute-start.22 = (bf16[84,16,128]{2,1,0:T(8,128)(2,1)S(1)}, bf16[84,16,128]{2,1,0:T(8,128)(2,1)S(1)}, u32[]{:S(2)}, u32[]{:S(2)}) collective-permute-start(bf16[84,16,128]{2,1,0:T(8,128)(2,1)S(1)} %bitcast.26), channel_id=1, source_target_pairs={{0,128},{32,160},{64,192},{96,224},{128,0},{160,32},{192,64},{224,... | collective-permute-start | bytes 1032200 | tf_op jit(solution)/shard_map/ppermute | solution.py:413
  173.4 16.1 %collective-permute-start.20 = (bf16[84,16,128]{2,1,0:T(8,128)(2,1)S(1)}, bf16[84,16,128]{2,1,0:T(8,128)(2,1)S(1)}, u32[]{:S(2)}, u32[]{:S(2)}) collective-permute-start(bf16[84,16,128]{2,1,0:T(8,128)(2,1)S(1)} %bitcast.27), channel_id=1, source_target_pairs={{0,64},{32,96},{64,128},{96,160},{128,192},{160,224},{192,0},{224,... | collective-permute-start | bytes 1032200 | tf_op jit(solution)/shard_map/ppermute | solution.py:413
  173.9 18.6 %collective-permute-start.19 = (bf16[84,16,128]{2,1,0:T(8,128)(2,1)S(1)}, bf16[84,16,128]{2,1,0:T(8,128)(2,1)S(1)}, u32[]{:S(2)}, u32[]{:S(2)}) collective-permute-start(bf16[84,16,128]{2,1,0:T(8,128)(2,1)S(1)} %bitcast.28), channel_id=1, source_target_pairs={{0,32},{32,0},{64,96},{96,64},{128,160},{160,128},{192,224},{224,1... | collective-permute-start | bytes 1032200 | tf_op jit(solution)/shard_map/ppermute | solution.py:433
  181.6 10.9 %collective-permute-start.25 = (bf16[84,16,128]{2,1,0:T(8,128)(2,1)S(1)}, bf16[84,16,128]{2,1,0:T(8,128)(2,1)S(1)}, u32[]{:S(2)}, u32[]{:S(2)}) collective-permute-start(bf16[84,16,128]{2,1,0:T(8,128)(2,1)S(1)} %collective-permute-done.24.refs_6_), channel_id=1, source_target_pairs={{0,32},{32,0},{64,96},{96,64},{128,160},{160,128},{192,224},{224,1... | collective-permute-start | bytes 1032200 | tf_op jit(solution)/shard_map/ppermute | solution.py:433
  188.9 3.7 %collective-permute-start.23 = (bf16[84,16,128]{2,1,0:T(8,128)(2,1)S(1)}, bf16[84,16,128]{2,1,0:T(8,128)(2,1)S(1)}, u32[]{:S(2)}, u32[]{:S(2)}) collective-permute-start(bf16[84,16,128]{2,1,0:T(8,128)(2,1)S(1)} %collective-permute-done.22.refs_4_), channel_id=1, source_target_pairs={{0,32},{32,0},{64,96},{96,64},{128,160},{160,128},{192,224},{224,1... | collective-permute-start | bytes 1032200 | tf_op jit(solution)/shard_map/ppermute | solution.py:433
  189.6 4.2 %collective-permute-start.21 = (bf16[84,16,128]{2,1,0:T(8,128)(2,1)S(1)}, bf16[84,16,128]{2,1,0:T(8,128)(2,1)S(1)}, u32[]{:S(2)}, u32[]{:S(2)}) collective-permute-start(bf16[84,16,128]{2,1,0:T(8,128)(2,1)S(1)} %collective-permute-done.20.refs_2_), channel_id=1, source_target_pairs={{0,32},{32,0},{64,96},{96,64},{128,160},{160,128},{192,224},{224,1... | collective-permute-start | bytes 1032200 | tf_op jit(solution)/shard_map/ppermute | solution.py:433
  (25 other events, 445.6 us)
Sparse Core Ops, SparseCore 0:
  44.4 41.3 all-gather.2
  99.2 31.7 reduce-scatter.2
  153.1 35.0 reduce-scatter.4

commit v5 on v4

--- a/solution.py
+++ b/solution.py
@@ -258,37 +258,24 @@
 
 
 def widen_kernel(where_ref, *refs):
-    pieces, (blocks_ref, out_hbm, flat_ref, in_ref, out_ref, in_sems, out_sems) = refs[:-7], refs[-7:]
-    parts, count, part, _ = in_ref.shape
-    cuts = in_sems.shape[1]
-    stores = out_sems.shape[0]
+    pieces, (blocks_ref, out_hbm, flat_ref, out_ref, sems) = refs[:-5], refs[-5:]
+    count, part, _ = pieces[0].shape
+    stores = sems.shape[0]
+    some = count // stores
     core, y = where_ref[4], where_ref[5]
 
-    def load(i, h):
-        chunk = lax.rem(y + 4 - i // 2, 4) * 2 + (1 - core if i % 2 else core)
-        at = pl.ds(h * (count // cuts), count // cuts)
-        return pltpu.make_async_copy(pieces[i].at[at], in_ref.at[chunk, at], in_sems.at[i, h])
-
     def store(i):
-        at = pl.ds(i * (count // stores), count // stores)
-        return pltpu.make_async_copy(out_ref.at[at], out_hbm.at[at], out_sems.at[i])
-
-    for h in range(cuts):
-        for i in range(parts):
-            load(i, h).start()
+        at = pl.ds(i * some, some)
+        return pltpu.make_async_copy(out_ref.at[at], out_hbm.at[at], sems.at[i])
+
+    for i in range(stores):
+        for k, piece in enumerate(pieces):
+            chunk = lax.rem(y + 4 - k // 2, 4) * 2 + (1 - core if k % 2 else core)
+            rows = pl.ds(pl.multiple_of(chunk * part, part), part)
+            out_ref[i * some : (i + 1) * some, rows, :] = piece[i * some : (i + 1) * some].astype(F32)
+        store(i).start()
     for b in range(blocks_ref.shape[0]):
         flat_ref[:, b * BLOCK : (b + 1) * BLOCK] = blocks_ref[b]
-    for i in range(stores):
-        if i % (stores // cuts) == 0:
-            for k in range(parts):
-                load(k, i // (stores // cuts)).wait()
-
-        def step(k, carry):
-            out_ref[k] = in_ref[:, k].reshape(parts * part, BLOCK).astype(F32)
-            return carry
-
-        lax.fori_loop(i * (count // stores), (i + 1) * (count // stores), step, 0, unroll=2)
-        store(i).start()
     for i in range(stores):
         store(i).wait()
 
@@ -311,6 +298,7 @@
     slots = members * 2 * PAIR
     used = panels * 2 * MOST
     params = pltpu.CompilerParams(vmem_limit_bytes=48 * 1024 * 1024)
+    less = pltpu.CompilerParams(vmem_limit_bytes=24 * 1024 * 1024)
     alone = pltpu.CompilerParams(vmem_limit_bytes=60 * 1024 * 1024)
     sides = 4
     ring = members // sides
@@ -435,7 +423,7 @@
     mine = [mine_g, mine_u]
     other = [swap(other_g), swap(other_u)]
     sent = [reduced(mine[m], other[m]) for m in range(2)]
-    came = [[sent[m][0]] + [around(sent[m][s], s) for s in (1, 2, 3)] for m in range(2)]
+    came = [[sent[m][0]] + [around(sent[m][s], s) for s in (2, 1, 3)] for m in range(2)]
     columns = [[x * ring + z for x in range(sides)] for z in range(ring)]
     row_terms = lax.psum_scatter(
         terms, "mp", scatter_dimension=0, axis_index_groups=columns, tiled=True
@@ -449,7 +437,7 @@
             in_specs=[whole(piece.shape)] * 8,
             out_specs=whole((slots, part, BLOCK)),
         ),
-        compiler_params=params,
+        compiler_params=less,
         name="unsort_slots",
     )(table, count, *came[0], *came[1])
     own = pl.pallas_call(
@@ -465,7 +453,8 @@
         name="own_slots",
     )(where, tile_cols, exchange(returning))
     own = own.reshape(2 * owned, part, BLOCK)
-    full = [own] + [around(own, s) for s in (1, 2, 3)]
+    far, near, back = (around(own, s) for s in (2, 1, 3))
+    full = [own, near, far, back]
     full = [v for t in full for v in (t, swap(t))]
     input_grad = lax.psum_scatter(
         row_terms, "mp", scatter_dimension=0, axis_index_groups=rows, tiled=True
@@ -479,16 +468,15 @@
         grid_spec=pltpu.PrefetchScalarGridSpec(
             num_scalar_prefetch=1,
             grid=(1,),
-            in_specs=[anywhere] * groups + [whole((my_blocks, tok_rows, BLOCK))],
+            in_specs=[whole((2 * owned, part, BLOCK))] * groups
+            + [whole((my_blocks, tok_rows, BLOCK))],
             out_specs=(anywhere, whole(tokens.shape)),
             scratch_shapes=[
-                pltpu.VMEM((groups, 2 * owned, part, BLOCK), BF16),
                 pltpu.VMEM((2 * owned, BLOCK, BLOCK), F32),
-                pltpu.SemaphoreType.DMA((groups, 2)),
                 pltpu.SemaphoreType.DMA((6,)),
             ],
         ),
-        compiler_params=alone,
+        compiler_params=less,
         name="widen",
     )(where, *full, input_grad)
     tile_grads = tile_grads.reshape(tiles.shape)

time: 209 us -> 204 us (0.976)
  Pallas kernels: 30.1 us -> 27.5 us
    pallas_call x1, Pallas kernels: 6.25 us -> 3.72 us  [per_device(): pl.pallas_call(widen_kernel, out_shape=(jax.ShapeDtypeStruct((2 * owned,...]
    ppermute x9, waiting for transfers between devices: 29.1 us -> 27 us  [around(): return lax.ppermute(value, 'dp', pairs)]
  transfers between devices with their start and end apart: 31 -> 31, of which waited for: 18 -> 16; matrix products, arithmetic and copies ran while one was open for 3% -> 3% of each run, Pallas kernels for 3% -> 3%
where the time goes in v5:
time: 204 us; the launch traced here: 203 us
  waiting for transfers between devices  93.1 us (46%)
  starting transfers between devices  59.8 us (29%)
  Pallas kernels  27.5 us (13%)
  between operations  14.1 us (7%)
  other arithmetic  4.39 us (2%)
  local copies, waits for them, and re-layouts  3.82 us (2%)
    all_to_all x2, waiting for transfers between devices, exchange(): lax.all_to_all(values.reshape(shape), 'mp', 0, 0).reshape(values.shape)  28.9 us
    ppermute x9, waiting for transfers between devices, around(): return lax.ppermute(value, 'dp', pairs)  27 us
    all_to_all x2, starting transfers between devices, exchange(): lax.all_to_all(values.reshape(shape), 'mp', 0, 0).reshape(values.shape)  21.5 us
    ppermute x8, waiting for transfers between devices, along(): return lax.ppermute(value, 'mp', pairs)  21.1 us
    ppermute x6, starting transfers between devices, swap(): return lax.ppermute(value, 'dp', [(d, d ^ 1) for d in range(groups)])  18.1 us
    pallas_call x1, Pallas kernels, per_device(): pl.pallas_call(lambda *refs: main_kernel(sides, ring, panels, *refs), out...  13.1 us
    all_gather x1, waiting for transfers between devices, per_device(): held = lax.all_gather(ordered, 'dp')  11.2 us
    ppermute x8, starting transfers between devices, along(): return lax.ppermute(value, 'mp', pairs)  8.46 us
  transfers between devices with their start and end apart: 31, of which 16 were waited for; matrix products, arithmetic and copies ran while one was open for 3% of the time, Pallas kernels for 3%

profile of v5, /device:TPU:1, one launch (start us, length us, event | category | flops | bytes accessed | tf_op | source)
XLA Modules:
  0.0 202.7 jit_solution(9367011091153297700)
XLA Ops:
  7.8 3.1 %send_pack.1 = (bf16[192,16,128]{2,1,0:T(8,128)(2,1)}, bf16[2,128,128]{2,1,0:T(8,128)(2,1)}) custom-call(s32[6]{0:T(128)} %stack.42.refs_0_.refs_2_.where_ref, s32[2,1344]{1,0:T(2,128)} %refs_1_.3, bf16[2,42,128,128]{3,2,1,0:T(8,128)(2,1)} %refs_2_.1, bf16[128,256]{1,0:T(8,128)(2,1)} %refs_3_.1), custom_call_target="tpu_custom_call" | custom-call | tf_op jit(solution)/shard_map/send_pack/pallas_call | solution.py:308
  10.9 12.0 %all-to-all-start = ((bf16[32,6,16,128]{3,2,1,0:T(8,128)(2,1)}), bf16[32,6,16,128]{3,2,1,0:T(8,128)(2,1)S(1)}, u32[]{:S(2)}, u32[]{:S(2)}) async-start(bf16[32,6,16,128]{3,2,1,0:T(8,128)(2,1)} %bitcast.33), calls=%async_computation | async-start | bytes 1572864 | tf_op jit(solution)/shard_map/all_to_all | solution.py:329
  23.0 2.6 %collective-permute-start.2 = (bf16[2,128,128]{2,1,0:T(8,128)(2,1)}, bf16[2,128,128]{2,1,0:T(8,128)(2,1)S(1)}, u32[]{:S(2)}, u32[]{:S(2)}) collective-permute-start(bf16[2,128,128]{2,1,0:T(8,128)(2,1)} %get-tuple-element.24), channel_id=1, source_target_pairs={{0,24},{1,25},{2,26},{3,27},{4,28},{5,29},{6,30},{7,31},{8,0},{9,1... | collective-permute-start | bytes 196616 | tf_op jit(solution)/shard_map/ppermute | solution.py:337
  28.1 3.2 %select_reduce_fusion = s32[7,2,12]{2,1,0:T(2,128)S(1)} fusion(s32[2,32,42]{2,1,0:T(8,128)S(1)} %get-tuple-element.46, s32[7,2,32,42]{3,2,1,0:T(8,128)S(1)} %add_select_fusion), kind=kLoop, calls=%fused_computation | loop fusion | flops 677208 | bytes 86688 | tf_op jit(solution)/shard_map/reduce_sum | solution.py:46
  31.5 10.7 %all-to-all-done = bf16[32,6,16,128]{3,2,1,0:T(8,128)(2,1)S(1)} async-done(((bf16[32,6,16,128]{3,2,1,0:T(8,128)(2,1)}), bf16[32,6,16,128]{3,2,1,0:T(8,128)(2,1)S(1)}, u32[]{:S(2)}, u32[]{:S(2)}) %all-to-all-start) | async-done | bytes 786464 | tf_op jit(solution)/shard_map/all_to_all | solution.py:329
  42.2 2.0 sort_slots.1
  44.2 2.1 %collective-permute-start.6 = (bf16[4,2,128,128]{3,2,1,0:T(8,128)(2,1)S(1)}, bf16[4,2,128,128]{3,2,1,0:T(8,128)(2,1)S(1)}, u32[]{:S(2)}, u32[]{:S(2)}) collective-permute-start(bf16[4,2,128,128]{3,2,1,0:T(8,128)(2,1)S(1)} %pad_maximum_fusion.refs_3_), channel_id=1, source_target_pairs={{0,7},{1,0},{2,1},{3,2},{4,3},{5,4},{6,5},{7,6},{8,15},{9,8},{10,9... | collective-permute-start | bytes 786440 | tf_op jit(solution)/shard_map/ppermute | solution.py:343
  46.3 1.5 collective-permute-start.3
  47.8 3.7 %collective-permute-done.6.refs_9_ = bf16[4,2,128,128]{3,2,1,0:T(8,128)(2,1)S(1)} collective-permute-done((bf16[4,2,128,128]{3,2,1,0:T(8,128)(2,1)S(1)}, bf16[4,2,128,128]{3,2,1,0:T(8,128)(2,1)S(1)}, u32[]{:S(2)}, u32[]{:S(2)}) %collective-permute-start.6) | collective-permute-done | bytes 262176 | tf_op jit(solution)/shard_map/ppermute | solution.py:343
  53.1 4.8 %collective-permute-done.7.refs_8_ = bf16[4,2,128,128]{3,2,1,0:T(8,128)(2,1)S(1)} collective-permute-done((bf16[4,2,128,128]{3,2,1,0:T(8,128)(2,1)S(1)}, bf16[4,2,128,128]{3,2,1,0:T(8,128)(2,1)S(1)}, u32[]{:S(2)}, u32[]{:S(2)}) %collective-permute-start.7) | collective-permute-done | bytes 262176 | tf_op jit(solution)/shard_map/ppermute | solution.py:343
  59.6 6.1 %collective-permute-done.8.refs_7_ = bf16[4,2,128,128]{3,2,1,0:T(8,128)(2,1)S(1)} collective-permute-done((bf16[4,2,128,128]{3,2,1,0:T(8,128)(2,1)S(1)}, bf16[4,2,128,128]{3,2,1,0:T(8,128)(2,1)S(1)}, u32[]{:S(2)}, u32[]{:S(2)}) %collective-permute-start.8) | collective-permute-done | bytes 262176 | tf_op jit(solution)/shard_map/ppermute | solution.py:343
  65.7 1.7 collective-permute-start.10
  68.4 3.2 %collective-permute-done.10.refs_11_ = bf16[2,2,128,128]{3,2,1,0:T(8,128)(2,1)S(1)} collective-permute-done((bf16[2,2,128,128]{3,2,1,0:T(8,128)(2,1)S(1)}, bf16[2,2,128,128]{3,2,1,0:T(8,128)(2,1)S(1)}, u32[]{:S(2)}, u32[]{:S(2)}) %collective-permute-start.10) | collective-permute-done | bytes 131104 | tf_op jit(solution)/shard_map/ppermute | solution.py:343
  71.6 2.9 %collective-permute-done.9.refs_10_ = bf16[2,2,128,128]{3,2,1,0:T(8,128)(2,1)S(1)} collective-permute-done((bf16[2,2,128,128]{3,2,1,0:T(8,128)(2,1)S(1)}, bf16[2,2,128,128]{3,2,1,0:T(8,128)(2,1)S(1)}, u32[]{:S(2)}, u32[]{:S(2)}) %collective-permute-start.9) | collective-permute-done | bytes 131104 | tf_op jit(solution)/shard_map/ppermute | solution.py:343
  74.5 11.2 %all-gather.3.cloned.1.call-done = bf16[1344,16,128]{2,1,0:T(8,128)(2,1)} async-done(((bf16[168,16,128]{2,1,0:T(8,128)(2,1)}), bf16[1344,16,128]{2,1,0:T(8,128)(2,1)}) %all-gather.3.cloned.1.call-update) | async-done | bytes 5505040 | tf_op jit(solution)/shard_map/all_gather | solution.py:360
  85.8 13.1 %gated_pair.1 = (bf16[128,896]{1,0:T(8,128)(2,1)}, bf16[4,84,16,128]{3,2,1,0:T(8,128)(2,1)}, bf16[4,84,16,128]{3,2,1,0:T(8,128)(2,1)}, bf16[4,84,16,128]{3,2,1,0...) custom-call(s32[168]{0:T(256)} %copy-done.5, s32[14]{0:T(128)} %reshape.58.refs_1_.count_ref, ...), custom_call_target="tpu_custom_call" | custom-call | tf_op jit(solution)/shard_map/gated_pair/pallas_call | solution.py:370
  99.5 2.8 %collective-permute-done.11.other_ref = bf16[4,84,16,128]{3,2,1,0:T(8,128)(2,1)S(1)} collective-permute-done((bf16[4,84,16,128]{3,2,1,0:T(8,128)(2,1)}, bf16[4,84,16,128]{3,2,1,0:T(8,128)(2,1)S(1)}, u32[]{:S(2)}, u32[]{:S(2)}) %collective-permute-start.11) | collective-permute-done | bytes 1376288 | tf_op jit(solution)/shard_map/ppermute | solution.py:421
  104.9 1.6 collective-permute-start.12
  106.5 2.7 %collective-permute-start.14 = (bf16[84,16,128]{2,1,0:T(8,128)(2,1)S(1)}, bf16[84,16,128]{2,1,0:T(8,128)(2,1)S(1)}, u32[]{:S(2)}, u32[]{:S(2)}) collective-permute-start(bf16[84,16,128]{2,1,0:T(8,128)(2,1)S(1)} %get-tuple-element.33), channel_id=1, source_target_pairs={{0,192},{32,224},{64,0},{96,32},{128,64},{160,96},{192,128},{224,1... | collective-permute-start | bytes 1032200 | tf_op jit(solution)/shard_map/ppermute | solution.py:401
  111.1 4.8 %collective-permute-done.12.refs_1_ = bf16[84,16,128]{2,1,0:T(8,128)(2,1)S(1)} collective-permute-done((bf16[84,16,128]{2,1,0:T(8,128)(2,1)S(1)}, bf16[84,16,128]{2,1,0:T(8,128)(2,1)S(1)}, u32[]{:S(2)}, u32[]{:S(2)}) %collective-permute-start.12) | collective-permute-done | bytes 344096 | tf_op jit(solution)/shard_map/ppermute | solution.py:401
  116.5 8.0 %collective-permute-done.13.refs_2_ = bf16[84,16,128]{2,1,0:T(8,128)(2,1)S(1)} collective-permute-done((bf16[84,16,128]{2,1,0:T(8,128)(2,1)S(1)}, bf16[84,16,128]{2,1,0:T(8,128)(2,1)S(1)}, u32[]{:S(2)}, u32[]{:S(2)}) %collective-permute-start.13) | collective-permute-done | bytes 344096 | tf_op jit(solution)/shard_map/ppermute | solution.py:401
  124.5 6.2 %collective-permute-done.16.refs_5_ = bf16[84,16,128]{2,1,0:T(8,128)(2,1)S(1)} collective-permute-done((bf16[84,16,128]{2,1,0:T(8,128)(2,1)S(1)}, bf16[84,16,128]{2,1,0:T(8,128)(2,1)S(1)}, u32[]{:S(2)}, u32[]{:S(2)}) %collective-permute-start.16) | collective-permute-done | bytes 344096 | tf_op jit(solution)/shard_map/ppermute | solution.py:401
  130.7 7.9 %collective-permute-done.17.refs_6_ = bf16[84,16,128]{2,1,0:T(8,128)(2,1)S(1)} collective-permute-done((bf16[84,16,128]{2,1,0:T(8,128)(2,1)S(1)}, bf16[84,16,128]{2,1,0:T(8,128)(2,1)S(1)}, u32[]{:S(2)}, u32[]{:S(2)}) %collective-permute-start.17) | collective-permute-done | bytes 344096 | tf_op jit(solution)/shard_map/ppermute | solution.py:401
  138.6 2.0 unsort_slots.1
  140.6 9.5 %all-to-all-start.1 = ((bf16[32,6,16,128]{3,2,1,0:T(8,128)(2,1)}), bf16[32,6,16,128]{3,2,1,0:T(8,128)(2,1)S(1)}, u32[]{:S(2)}, u32[]{:S(2)}) async-start(bf16[32,6,16,128]{3,2,1,0:T(8,128)(2,1)} %bitcast.15), calls=%async_computation.1 | async-start | bytes 1572864 | tf_op jit(solution)/shard_map/all_to_all | solution.py:329
  150.9 18.2 %all-to-all-done.1 = bf16[32,6,16,128]{3,2,1,0:T(8,128)(2,1)S(1)} async-done(((bf16[32,6,16,128]{3,2,1,0:T(8,128)(2,1)}), bf16[32,6,16,128]{3,2,1,0:T(8,128)(2,1)S(1)}, u32[]{:S(2)}, u32[]{:S(2)}) %all-to-all-start.1) | async-done | bytes 786464 | tf_op jit(solution)/shard_map/all_to_all | solution.py:329
  171.0 1.5 collective-permute-start.22
  172.8 6.1 %collective-permute-start.19 = (bf16[84,16,128]{2,1,0:T(8,128)(2,1)S(1)}, bf16[84,16,128]{2,1,0:T(8,128)(2,1)S(1)}, u32[]{:S(2)}, u32[]{:S(2)}) collective-permute-start(bf16[84,16,128]{2,1,0:T(8,128)(2,1)S(1)} %bitcast.28), channel_id=1, source_target_pairs={{0,32},{32,0},{64,96},{96,64},{128,160},{160,128},{192,224},{224,1... | collective-permute-start | bytes 1032200 | tf_op jit(solution)/shard_map/ppermute | solution.py:421
  178.8 5.8 %collective-permute-start.25 = (bf16[84,16,128]{2,1,0:T(8,128)(2,1)S(1)}, bf16[84,16,128]{2,1,0:T(8,128)(2,1)S(1)}, u32[]{:S(2)}, u32[]{:S(2)}) collective-permute-start(bf16[84,16,128]{2,1,0:T(8,128)(2,1)S(1)} %collective-permute-done.24.refs_6_), channel_id=1, source_target_pairs={{0,32},{32,0},{64,96},{96,64},{128,160},{160,128},{192,224},{224,1... | collective-permute-start | bytes 1032200 | tf_op jit(solution)/shard_map/ppermute | solution.py:421
  184.6 2.2 %collective-permute-start.23 = (bf16[84,16,128]{2,1,0:T(8,128)(2,1)S(1)}, bf16[84,16,128]{2,1,0:T(8,128)(2,1)S(1)}, u32[]{:S(2)}, u32[]{:S(2)}) collective-permute-start(bf16[84,16,128]{2,1,0:T(8,128)(2,1)S(1)} %collective-permute-done.22.refs_4_), channel_id=1, source_target_pairs={{0,32},{32,0},{64,96},{96,64},{128,160},{160,128},{192,224},{224,1... | collective-permute-start | bytes 1032200 | tf_op jit(solution)/shard_map/ppermute | solution.py:421
  186.8 3.5 %collective-permute-start.21 = (bf16[84,16,128]{2,1,0:T(8,128)(2,1)S(1)}, bf16[84,16,128]{2,1,0:T(8,128)(2,1)S(1)}, u32[]{:S(2)}, u32[]{:S(2)}) collective-permute-start(bf16[84,16,128]{2,1,0:T(8,128)(2,1)S(1)} %collective-permute-done.20.refs_2_), channel_id=1, source_target_pairs={{0,32},{32,0},{64,96},{96,64},{128,160},{160,128},{192,224},{224,1... | collective-permute-start | bytes 1032200 | tf_op jit(solution)/shard_map/ppermute | solution.py:421
  192.4 3.7 %widen.1 = (f32[84,128,128]{2,1,0:T(8,128)}, bf16[128,256]{1,0:T(8,128)(2,1)}) custom-call(s32[6]{0:T(128)S(1)} %copy-done.4, bf16[84,16,128]{2,1,0:T(8,128)(2,1)S(1)} %bitcast.29, bf16[84,16,128]{2,1,0:T(8,128)(2,1)S(1)} %collective-permute-done.19.refs_1_, bf16[84,16,128]{2,1,0:T(8,128)(2,1)S(1)} %collective-permute-done.20.refs_2_, ...), custom_call_target="tpu_custom_call" | custom-call | tf_op jit(solution)/shard_map/widen/pallas_call | solution.py:462
  (97 shorter events, 18.4 us)
Async XLA Ops:
  10.9 31.3 %all-to-all-start = ((bf16[32,6,16,128]{3,2,1,0:T(8,128)(2,1)}), bf16[32,6,16,128]{3,2,1,0:T(8,128)(2,1)S(1)}, u32[]{:S(2)}, u32[]{:S(2)}) async-start(bf16[32,6,16,128]{3,2,1,0:T(8,128)(2,1)} %bitcast.33), calls=%async_computation | async-start | bytes 1572864 | tf_op jit(solution)/shard_map/all_to_all | solution.py:329
  22.9 62.8 %all-gather.3.cloned.1.call-start = ((), (), s32[]{:S(2)}) async-start(), calls=%async_computation.6 | async-start | bytes 6193152 | tf_op jit(solution)/shard_map/all_gather | solution.py:360
  23.0 8.4 %collective-permute-start.2 = (bf16[2,128,128]{2,1,0:T(8,128)(2,1)}, bf16[2,128,128]{2,1,0:T(8,128)(2,1)S(1)}, u32[]{:S(2)}, u32[]{:S(2)}) collective-permute-start(bf16[2,128,128]{2,1,0:T(8,128)(2,1)} %get-tuple-element.24), channel_id=1, source_target_pairs={{0,24},{1,25},{2,26},{3,27},{4,28},{5,29},{6,30},{7,31},{8,0},{9,1... | collective-permute-start | bytes 196616 | tf_op jit(solution)/shard_map/ppermute | solution.py:337
  25.5 5.9 %collective-permute-start.1 = (bf16[2,128,128]{2,1,0:T(8,128)(2,1)}, bf16[2,128,128]{2,1,0:T(8,128)(2,1)S(1)}, u32[]{:S(2)}, u32[]{:S(2)}) collective-permute-start(bf16[2,128,128]{2,1,0:T(8,128)(2,1)} %get-tuple-element.24), channel_id=1, source_target_pairs={{0,16},{1,17},{2,18},{3,19},{4,20},{5,21},{6,22},{7,23},{8,24},{9,... | collective-permute-start | bytes 196616 | tf_op jit(solution)/shard_map/ppermute | solution.py:337
  26.1 5.4 %collective-permute-start = (bf16[2,128,128]{2,1,0:T(8,128)(2,1)}, bf16[2,128,128]{2,1,0:T(8,128)(2,1)S(1)}, u32[]{:S(2)}, u32[]{:S(2)}) collective-permute-start(bf16[2,128,128]{2,1,0:T(8,128)(2,1)} %get-tuple-element.24), channel_id=1, source_target_pairs={{0,8},{1,9},{2,10},{3,11},{4,12},{5,13},{6,14},{7,15},{8,16},{9,17... | collective-permute-start | bytes 196616 | tf_op jit(solution)/shard_map/ppermute | solution.py:337
  31.4 54.3 %copy-start.5 = (s32[168]{0:T(256)}, s32[168]{0:T(256)S(1)}, u32[]{:S(2)}) copy-start(s32[168]{0:T(256)S(1)} %reshape.57.table_ref.refs_0_) | copy-start | bytes 2020
  44.2 106.1 %reduce-scatter.3.cloned.1.call-start = ((), (), s32[]{:S(2)}) async-start(), calls=%async_computation.4 | async-start | bytes 2621440 | tf_op jit(solution)/shard_map/reduce_scatter | solution.py:428
  44.2 7.3 %collective-permute-start.6 = (bf16[4,2,128,128]{3,2,1,0:T(8,128)(2,1)S(1)}, bf16[4,2,128,128]{3,2,1,0:T(8,128)(2,1)S(1)}, u32[]{:S(2)}, u32[]{:S(2)}) collective-permute-start(bf16[4,2,128,128]{3,2,1,0:T(8,128)(2,1)S(1)} %pad_maximum_fusion.refs_3_), channel_id=1, source_target_pairs={{0,7},{1,0},{2,1},{3,2},{4,3},{5,4},{6,5},{7,6},{8,15},{9,8},{10,9... | collective-permute-start | bytes 786440 | tf_op jit(solution)/shard_map/ppermute | solution.py:343
  46.3 6.4 %collective-permute-start.3 = (bf16[4,2,128,128]{3,2,1,0:T(8,128)(2,1)S(1)}, bf16[4,2,128,128]{3,2,1,0:T(8,128)(2,1)S(1)}, u32[]{:S(2)}, u32[]{:S(2)}) collective-permute-start(bf16[4,2,128,128]{3,2,1,0:T(8,128)(2,1)S(1)} %pad_maximum_fusion.refs_3_), channel_id=1, source_target_pairs={{0,1},{1,2},{2,3},{3,4},{4,5},{5,6},{6,7},{7,0},{8,9},{9,10},{10,1... | collective-permute-start | bytes 786440 | tf_op jit(solution)/shard_map/ppermute | solution.py:343
  51.5 6.4 %collective-permute-start.7 = (bf16[4,2,128,128]{3,2,1,0:T(8,128)(2,1)S(1)}, bf16[4,2,128,128]{3,2,1,0:T(8,128)(2,1)S(1)}, u32[]{:S(2)}, u32[]{:S(2)}) collective-permute-start(bf16[4,2,128,128]{3,2,1,0:T(8,128)(2,1)S(1)} %collective-permute-done.6.refs_9_), channel_id=1, source_target_pairs={{0,7},{1,0},{2,1},{3,2},{4,3},{5,4},{6,5},{7,6},{8,15},{9,8},{10,9... | collective-permute-start | bytes 786440 | tf_op jit(solution)/shard_map/ppermute | solution.py:343
  52.7 6.7 %collective-permute-start.4 = (bf16[4,2,128,128]{3,2,1,0:T(8,128)(2,1)S(1)}, bf16[4,2,128,128]{3,2,1,0:T(8,128)(2,1)S(1)}, u32[]{:S(2)}, u32[]{:S(2)}) collective-permute-start(bf16[4,2,128,128]{3,2,1,0:T(8,128)(2,1)S(1)} %collective-permute-done.3.refs_4_), channel_id=1, source_target_pairs={{0,1},{1,2},{2,3},{3,4},{4,5},{5,6},{6,7},{7,0},{8,9},{9,10},{10,1... | collective-permute-start | bytes 786440 | tf_op jit(solution)/shard_map/ppermute | solution.py:343
  57.9 7.8 %collective-permute-start.8 = (bf16[4,2,128,128]{3,2,1,0:T(8,128)(2,1)S(1)}, bf16[4,2,128,128]{3,2,1,0:T(8,128)(2,1)S(1)}, u32[]{:S(2)}, u32[]{:S(2)}) collective-permute-start(bf16[4,2,128,128]{3,2,1,0:T(8,128)(2,1)S(1)} %collective-permute-done.7.refs_8_), channel_id=1, source_target_pairs={{0,7},{1,0},{2,1},{3,2},{4,3},{5,4},{6,5},{7,6},{8,15},{9,8},{10,9... | collective-permute-start | bytes 786440 | tf_op jit(solution)/shard_map/ppermute | solution.py:343
  59.4 8.2 %collective-permute-start.5 = (bf16[4,2,128,128]{3,2,1,0:T(8,128)(2,1)S(1)}, bf16[4,2,128,128]{3,2,1,0:T(8,128)(2,1)S(1)}, u32[]{:S(2)}, u32[]{:S(2)}) collective-permute-start(bf16[4,2,128,128]{3,2,1,0:T(8,128)(2,1)S(1)} %collective-permute-done.4.refs_5_), channel_id=1, source_target_pairs={{0,1},{1,2},{2,3},{3,4},{4,5},{5,6},{6,7},{7,0},{8,9},{9,10},{10,1... | collective-permute-start | bytes 786440 | tf_op jit(solution)/shard_map/ppermute | solution.py:343
  65.7 5.9 %collective-permute-start.10 = (bf16[2,2,128,128]{3,2,1,0:T(8,128)(2,1)S(1)}, bf16[2,2,128,128]{3,2,1,0:T(8,128)(2,1)S(1)}, u32[]{:S(2)}, u32[]{:S(2)}) collective-permute-start(bf16[2,2,128,128]{3,2,1,0:T(8,128)(2,1)S(1)} %slice.29), channel_id=1, source_target_pairs={{0,7},{1,0},{2,1},{3,2},{4,3},{5,4},{6,5},{7,6},{8,15},{9,8},{10,9... | collective-permute-start | bytes 393224 | tf_op jit(solution)/shard_map/ppermute | solution.py:343
  67.6 6.9 %collective-permute-start.9 = (bf16[2,2,128,128]{3,2,1,0:T(8,128)(2,1)S(1)}, bf16[2,2,128,128]{3,2,1,0:T(8,128)(2,1)S(1)}, u32[]{:S(2)}, u32[]{:S(2)}) collective-permute-start(bf16[2,2,128,128]{3,2,1,0:T(8,128)(2,1)S(1)} %slice.28), channel_id=1, source_target_pairs={{0,1},{1,2},{2,3},{3,4},{4,5},{5,6},{6,7},{7,0},{8,9},{9,10},{10,1... | collective-permute-start | bytes 393224 | tf_op jit(solution)/shard_map/ppermute | solution.py:343
  98.9 3.4 %collective-permute-start.11 = (bf16[4,84,16,128]{3,2,1,0:T(8,128)(2,1)}, bf16[4,84,16,128]{3,2,1,0:T(8,128)(2,1)S(1)}, u32[]{:S(2)}, u32[]{:S(2)}) collective-permute-start(bf16[4,84,16,128]{3,2,1,0:T(8,128)(2,1)} %get-tuple-element.29), channel_id=1, source_target_pairs={{0,32},{32,0},{64,96},{96,64},{128,160},{160,128},{192,224},{224,1... | collective-permute-start | bytes 4128776 | tf_op jit(solution)/shard_map/ppermute | solution.py:421
  99.2 9.9 %collective-permute-start.15 = (bf16[4,84,16,128]{3,2,1,0:T(8,128)(2,1)}, bf16[4,84,16,128]{3,2,1,0:T(8,128)(2,1)S(1)}, u32[]{:S(2)}, u32[]{:S(2)}) collective-permute-start(bf16[4,84,16,128]{3,2,1,0:T(8,128)(2,1)} %get-tuple-element.35), channel_id=1, source_target_pairs={{0,32},{32,0},{64,96},{96,64},{128,160},{160,128},{192,224},{224,1... | collective-permute-start | bytes 4128776 | tf_op jit(solution)/shard_map/ppermute | solution.py:421
  104.9 11.0 %collective-permute-start.12 = (bf16[84,16,128]{2,1,0:T(8,128)(2,1)S(1)}, bf16[84,16,128]{2,1,0:T(8,128)(2,1)S(1)}, u32[]{:S(2)}, u32[]{:S(2)}) collective-permute-start(bf16[84,16,128]{2,1,0:T(8,128)(2,1)S(1)} %get-tuple-element.31), channel_id=1, source_target_pairs={{0,128},{32,160},{64,192},{96,224},{128,0},{160,32},{192,64},{224,... | collective-permute-start | bytes 1032200 | tf_op jit(solution)/shard_map/ppermute | solution.py:401
  106.5 18.0 %collective-permute-start.13 = (bf16[84,16,128]{2,1,0:T(8,128)(2,1)S(1)}, bf16[84,16,128]{2,1,0:T(8,128)(2,1)S(1)}, u32[]{:S(2)}, u32[]{:S(2)}) collective-permute-start(bf16[84,16,128]{2,1,0:T(8,128)(2,1)S(1)} %get-tuple-element.32), channel_id=1, source_target_pairs={{0,64},{32,96},{64,128},{96,160},{128,192},{160,224},{192,0},{224,... | collective-permute-start | bytes 1032200 | tf_op jit(solution)/shard_map/ppermute | solution.py:401
  106.5 18.0 %collective-permute-start.14 = (bf16[84,16,128]{2,1,0:T(8,128)(2,1)S(1)}, bf16[84,16,128]{2,1,0:T(8,128)(2,1)S(1)}, u32[]{:S(2)}, u32[]{:S(2)}) collective-permute-start(bf16[84,16,128]{2,1,0:T(8,128)(2,1)S(1)} %get-tuple-element.33), channel_id=1, source_target_pairs={{0,192},{32,224},{64,0},{96,32},{128,64},{160,96},{192,128},{224,1... | collective-permute-start | bytes 1032200 | tf_op jit(solution)/shard_map/ppermute | solution.py:401
  110.4 20.3 %collective-permute-start.16 = (bf16[84,16,128]{2,1,0:T(8,128)(2,1)S(1)}, bf16[84,16,128]{2,1,0:T(8,128)(2,1)S(1)}, u32[]{:S(2)}, u32[]{:S(2)}) collective-permute-start(bf16[84,16,128]{2,1,0:T(8,128)(2,1)S(1)} %get-tuple-element.37), channel_id=1, source_target_pairs={{0,128},{32,160},{64,192},{96,224},{128,0},{160,32},{192,64},{224,... | collective-permute-start | bytes 1032200 | tf_op jit(solution)/shard_map/ppermute | solution.py:401
  110.8 27.8 %collective-permute-start.17 = (bf16[84,16,128]{2,1,0:T(8,128)(2,1)S(1)}, bf16[84,16,128]{2,1,0:T(8,128)(2,1)S(1)}, u32[]{:S(2)}, u32[]{:S(2)}) collective-permute-start(bf16[84,16,128]{2,1,0:T(8,128)(2,1)S(1)} %get-tuple-element.38), channel_id=1, source_target_pairs={{0,64},{32,96},{64,128},{96,160},{128,192},{160,224},{192,0},{224,... | collective-permute-start | bytes 1032200 | tf_op jit(solution)/shard_map/ppermute | solution.py:401
  116.0 22.7 %collective-permute-start.18 = (bf16[84,16,128]{2,1,0:T(8,128)(2,1)S(1)}, bf16[84,16,128]{2,1,0:T(8,128)(2,1)S(1)}, u32[]{:S(2)}, u32[]{:S(2)}) collective-permute-start(bf16[84,16,128]{2,1,0:T(8,128)(2,1)S(1)} %get-tuple-element.39), channel_id=1, source_target_pairs={{0,192},{32,224},{64,0},{96,32},{128,64},{160,96},{192,128},{224,1... | collective-permute-start | bytes 1032200 | tf_op jit(solution)/shard_map/ppermute | solution.py:401
  140.6 28.5 %all-to-all-start.1 = ((bf16[32,6,16,128]{3,2,1,0:T(8,128)(2,1)}), bf16[32,6,16,128]{3,2,1,0:T(8,128)(2,1)S(1)}, u32[]{:S(2)}, u32[]{:S(2)}) async-start(bf16[32,6,16,128]{3,2,1,0:T(8,128)(2,1)} %bitcast.15), calls=%async_computation.1 | async-start | bytes 1572864 | tf_op jit(solution)/shard_map/all_to_all | solution.py:329
  150.2 41.4 %reduce-scatter.5.cloned.1.call-start = ((), (), s32[]{:S(2)}) async-start(), calls=%async_computation.5 | async-start | bytes 589824 | tf_op jit(solution)/shard_map/reduce_scatter | solution.py:459
  170.3 8.5 %collective-permute-start.24 = (bf16[84,16,128]{2,1,0:T(8,128)(2,1)S(1)}, bf16[84,16,128]{2,1,0:T(8,128)(2,1)S(1)}, u32[]{:S(2)}, u32[]{:S(2)}) collective-permute-start(bf16[84,16,128]{2,1,0:T(8,128)(2,1)S(1)} %bitcast.25), channel_id=1, source_target_pairs={{0,192},{32,224},{64,0},{96,32},{128,64},{160,96},{192,128},{224,1... | collective-permute-start | bytes 1032200 | tf_op jit(solution)/shard_map/ppermute | solution.py:401
  171.0 13.6 %collective-permute-start.22 = (bf16[84,16,128]{2,1,0:T(8,128)(2,1)S(1)}, bf16[84,16,128]{2,1,0:T(8,128)(2,1)S(1)}, u32[]{:S(2)}, u32[]{:S(2)}) collective-permute-start(bf16[84,16,128]{2,1,0:T(8,128)(2,1)S(1)} %bitcast.26), channel_id=1, source_target_pairs={{0,128},{32,160},{64,192},{96,224},{128,0},{160,32},{192,64},{224,... | collective-permute-start | bytes 1032200 | tf_op jit(solution)/shard_map/ppermute | solution.py:401
  172.4 14.4 %collective-permute-start.20 = (bf16[84,16,128]{2,1,0:T(8,128)(2,1)S(1)}, bf16[84,16,128]{2,1,0:T(8,128)(2,1)S(1)}, u32[]{:S(2)}, u32[]{:S(2)}) collective-permute-start(bf16[84,16,128]{2,1,0:T(8,128)(2,1)S(1)} %bitcast.27), channel_id=1, source_target_pairs={{0,64},{32,96},{64,128},{96,160},{128,192},{160,224},{192,0},{224,... | collective-permute-start | bytes 1032200 | tf_op jit(solution)/shard_map/ppermute | solution.py:401
  172.8 17.6 %collective-permute-start.19 = (bf16[84,16,128]{2,1,0:T(8,128)(2,1)S(1)}, bf16[84,16,128]{2,1,0:T(8,128)(2,1)S(1)}, u32[]{:S(2)}, u32[]{:S(2)}) collective-permute-start(bf16[84,16,128]{2,1,0:T(8,128)(2,1)S(1)} %bitcast.28), channel_id=1, source_target_pairs={{0,32},{32,0},{64,96},{96,64},{128,160},{160,128},{192,224},{224,1... | collective-permute-start | bytes 1032200 | tf_op jit(solution)/shard_map/ppermute | solution.py:421
  178.8 11.5 %collective-permute-start.25 = (bf16[84,16,128]{2,1,0:T(8,128)(2,1)S(1)}, bf16[84,16,128]{2,1,0:T(8,128)(2,1)S(1)}, u32[]{:S(2)}, u32[]{:S(2)}) collective-permute-start(bf16[84,16,128]{2,1,0:T(8,128)(2,1)S(1)} %collective-permute-done.24.refs_6_), channel_id=1, source_target_pairs={{0,32},{32,0},{64,96},{96,64},{128,160},{160,128},{192,224},{224,1... | collective-permute-start | bytes 1032200 | tf_op jit(solution)/shard_map/ppermute | solution.py:421
  184.6 5.7 %collective-permute-start.23 = (bf16[84,16,128]{2,1,0:T(8,128)(2,1)S(1)}, bf16[84,16,128]{2,1,0:T(8,128)(2,1)S(1)}, u32[]{:S(2)}, u32[]{:S(2)}) collective-permute-start(bf16[84,16,128]{2,1,0:T(8,128)(2,1)S(1)} %collective-permute-done.22.refs_4_), channel_id=1, source_target_pairs={{0,32},{32,0},{64,96},{96,64},{128,160},{160,128},{192,224},{224,1... | collective-permute-start | bytes 1032200 | tf_op jit(solution)/shard_map/ppermute | solution.py:421
  186.8 4.8 %collective-permute-start.21 = (bf16[84,16,128]{2,1,0:T(8,128)(2,1)S(1)}, bf16[84,16,128]{2,1,0:T(8,128)(2,1)S(1)}, u32[]{:S(2)}, u32[]{:S(2)}) collective-permute-start(bf16[84,16,128]{2,1,0:T(8,128)(2,1)S(1)} %collective-permute-done.20.refs_2_), channel_id=1, source_target_pairs={{0,32},{32,0},{64,96},{96,64},{128,160},{160,128},{192,224},{224,1... | collective-permute-start | bytes 1032200 | tf_op jit(solution)/shard_map/ppermute | solution.py:421
  (18 other events, 397.6 us)
Sparse Core Ops, SparseCore 0:
  44.3 41.3 all-gather.2
  99.0 31.8 reduce-scatter.2
  153.7 34.1 reduce-scatter.4

commit v6 on v5

--- a/solution.py
+++ b/solution.py
@@ -60,13 +60,13 @@
     lax.fori_loop(0, owned, step, (jnp.int32(-1), jnp.int32(0)), unroll=7)
 
 
-def send_kernel(panels, place_ref, cols_ref, tiles_ref, tokens_ref, out_ref, blocks_ref):
+def send_kernel(panels, cols_ref, tiles_ref, tokens_ref, out_ref, blocks_ref):
     for m in range(2):
 
         def visit(k, holder, rank):
             out_ref[holder * (2 * PAIR) + m * PAIR + rank] = tiles_ref[m, k]
 
-        slot_of(cols_ref, place_ref[0], tiles_ref.shape[1], panels, m, visit)
+        slot_of(cols_ref, lax.axis_index("mp"), tiles_ref.shape[1], panels, m, visit)
     for b in range(blocks_ref.shape[0]):
         blocks_ref[b] = tokens_ref[:, b * BLOCK : (b + 1) * BLOCK]
 
@@ -258,7 +258,7 @@
 
 
 def widen_kernel(where_ref, *refs):
-    pieces, (blocks_ref, out_hbm, flat_ref, out_ref, sems) = refs[:-5], refs[-5:]
+    pieces, (blocks_hbm, out_hbm, flat_hbm, out_ref, sems, flat_sems) = refs[:-6], refs[-6:]
     count, part, _ = pieces[0].shape
     stores = sems.shape[0]
     some = count // stores
@@ -268,16 +268,24 @@
         at = pl.ds(i * some, some)
         return pltpu.make_async_copy(out_ref.at[at], out_hbm.at[at], sems.at[i])
 
+    flat = [
+        pltpu.make_async_copy(
+            blocks_hbm.at[b], flat_hbm.at[:, pl.ds(b * BLOCK, BLOCK)], flat_sems.at[b]
+        )
+        for b in range(flat_sems.shape[0])
+    ]
+    for copy in flat:
+        copy.start()
     for i in range(stores):
         for k, piece in enumerate(pieces):
             chunk = lax.rem(y + 4 - k // 2, 4) * 2 + (1 - core if k % 2 else core)
             rows = pl.ds(pl.multiple_of(chunk * part, part), part)
             out_ref[i * some : (i + 1) * some, rows, :] = piece[i * some : (i + 1) * some].astype(F32)
         store(i).start()
-    for b in range(blocks_ref.shape[0]):
-        flat_ref[:, b * BLOCK : (b + 1) * BLOCK] = blocks_ref[b]
     for i in range(stores):
         store(i).wait()
+    for copy in flat:
+        copy.wait()
 
 
 def whole(shape):
@@ -312,17 +320,17 @@
             jax.ShapeDtypeStruct((my_blocks, tok_rows, BLOCK), BF16),
         ),
         grid_spec=pltpu.PrefetchScalarGridSpec(
-            num_scalar_prefetch=2,
+            num_scalar_prefetch=1,
             grid=(1,),
             in_specs=[
-                pl.BlockSpec((2, owned, part, BLOCK), lambda i, w, c: (0, 0, w[1], 0)),
+                pl.BlockSpec((2, owned, part, BLOCK), lambda i, c: (0, 0, lax.axis_index("dp"), 0)),
                 whole(tokens.shape),
             ],
             out_specs=(whole((slots, part, BLOCK)), whole((my_blocks, tok_rows, BLOCK))),
         ),
         compiler_params=alone,
         name="send_pack",
-    )(where, tile_cols, tiles, tokens)
+    )(tile_cols, tiles, tokens)
 
     def exchange(values):
         shape = (members, -1) + values.shape[1:]
@@ -469,11 +477,12 @@
             num_scalar_prefetch=1,
             grid=(1,),
             in_specs=[whole((2 * owned, part, BLOCK))] * groups
-            + [whole((my_blocks, tok_rows, BLOCK))],
-            out_specs=(anywhere, whole(tokens.shape)),
+            + [anywhere],
+            out_specs=(anywhere, anywhere),
             scratch_shapes=[
                 pltpu.VMEM((2 * owned, BLOCK, BLOCK), F32),
                 pltpu.SemaphoreType.DMA((6,)),
+                pltpu.SemaphoreType.DMA((my_blocks,)),
             ],
         ),
         compiler_params=less,

time: 204 us -> 203 us (level)
  no operation moved by 1% of the time
where the time goes in v6:
time: 203 us; the launch traced here: 202 us
  waiting for transfers between devices  92.5 us (46%)
  starting transfers between devices  61.4 us (30%)
  Pallas kernels  25.5 us (13%)
  between operations  14.1 us (7%)
  other arithmetic  4.38 us (2%)
  local copies, waits for them, and re-layouts  3.82 us (2%)
    all_to_all x2, waiting for transfers between devices, exchange(): lax.all_to_all(values.reshape(shape), 'mp', 0, 0).reshape(values.shape)  28.9 us
    ppermute x9, waiting for transfers between devices, around(): return lax.ppermute(value, 'dp', pairs)  27 us
    all_to_all x2, starting transfers between devices, exchange(): lax.all_to_all(values.reshape(shape), 'mp', 0, 0).reshape(values.shape)  23.2 us
    ppermute x8, waiting for transfers between devices, along(): return lax.ppermute(value, 'mp', pairs)  20.5 us
    ppermute x6, starting transfers between devices, swap(): return lax.ppermute(value, 'dp', [(d, d ^ 1) for d in range(groups)])  18.1 us
    pallas_call x1, Pallas kernels, per_device(): pl.pallas_call(lambda *refs: main_kernel(sides, ring, panels, *refs), out...  11.7 us
    all_gather x1, waiting for transfers between devices, per_device(): held = lax.all_gather(ordered, 'dp')  11.2 us
    ppermute x8, starting transfers between devices, along(): return lax.ppermute(value, 'mp', pairs)  8.46 us
  transfers between devices with their start and end apart: 31, of which 16 were waited for; matrix products, arithmetic and copies ran while one was open for 3% of the time, Pallas kernels for 3%

profile of v6, /device:TPU:1, one launch (start us, length us, event | category | flops | bytes accessed | tf_op | source)
XLA Modules:
  0.0 201.7 jit_solution(9218145381660653610)
XLA Ops:
  7.2 3.2 %send_pack.1 = (bf16[192,16,128]{2,1,0:T(8,128)(2,1)}, bf16[2,128,128]{2,1,0:T(8,128)(2,1)}) custom-call(s32[2,1344]{1,0:T(2,128)} %refs_1_.3, bf16[2,42,128,128]{3,2,1,0:T(8,128)(2,1)} %refs_1_.2, bf16[128,256]{1,0:T(8,128)(2,1)} %refs_2_.1), custom_call_target="tpu_custom_call" | custom-call | tf_op jit(solution)/shard_map/send_pack/pallas_call | solution.py:316
  10.4 12.0 %all-to-all-start = ((bf16[32,6,16,128]{3,2,1,0:T(8,128)(2,1)}), bf16[32,6,16,128]{3,2,1,0:T(8,128)(2,1)S(1)}, u32[]{:S(2)}, u32[]{:S(2)}) async-start(bf16[32,6,16,128]{3,2,1,0:T(8,128)(2,1)} %bitcast.33), calls=%async_computation | async-start | bytes 1572864 | tf_op jit(solution)/shard_map/all_to_all | solution.py:337
  22.5 2.6 %collective-permute-start.2 = (bf16[2,128,128]{2,1,0:T(8,128)(2,1)}, bf16[2,128,128]{2,1,0:T(8,128)(2,1)S(1)}, u32[]{:S(2)}, u32[]{:S(2)}) collective-permute-start(bf16[2,128,128]{2,1,0:T(8,128)(2,1)} %get-tuple-element.24), channel_id=1, source_target_pairs={{0,24},{1,25},{2,26},{3,27},{4,28},{5,29},{6,30},{7,31},{8,0},{9,1... | collective-permute-start | bytes 196616 | tf_op jit(solution)/shard_map/ppermute | solution.py:345
  27.6 3.2 %select_reduce_fusion = s32[7,2,12]{2,1,0:T(2,128)S(1)} fusion(s32[2,32,42]{2,1,0:T(8,128)S(1)} %get-tuple-element.46, s32[7,2,32,42]{3,2,1,0:T(8,128)S(1)} %add_select_fusion), kind=kLoop, calls=%fused_computation | loop fusion | flops 677208 | bytes 86688 | tf_op jit(solution)/shard_map/reduce_sum | solution.py:46
  31.0 10.7 %all-to-all-done = bf16[32,6,16,128]{3,2,1,0:T(8,128)(2,1)S(1)} async-done(((bf16[32,6,16,128]{3,2,1,0:T(8,128)(2,1)}), bf16[32,6,16,128]{3,2,1,0:T(8,128)(2,1)S(1)}, u32[]{:S(2)}, u32[]{:S(2)}) %all-to-all-start) | async-done | bytes 786464 | tf_op jit(solution)/shard_map/all_to_all | solution.py:337
  41.7 2.0 sort_slots.1
  43.7 2.1 %collective-permute-start.6 = (bf16[4,2,128,128]{3,2,1,0:T(8,128)(2,1)S(1)}, bf16[4,2,128,128]{3,2,1,0:T(8,128)(2,1)S(1)}, u32[]{:S(2)}, u32[]{:S(2)}) collective-permute-start(bf16[4,2,128,128]{3,2,1,0:T(8,128)(2,1)S(1)} %pad_maximum_fusion.refs_3_), channel_id=1, source_target_pairs={{0,7},{1,0},{2,1},{3,2},{4,3},{5,4},{6,5},{7,6},{8,15},{9,8},{10,9... | collective-permute-start | bytes 786440 | tf_op jit(solution)/shard_map/ppermute | solution.py:351
  45.8 1.5 collective-permute-start.3
  47.3 3.7 %collective-permute-done.6.refs_9_ = bf16[4,2,128,128]{3,2,1,0:T(8,128)(2,1)S(1)} collective-permute-done((bf16[4,2,128,128]{3,2,1,0:T(8,128)(2,1)S(1)}, bf16[4,2,128,128]{3,2,1,0:T(8,128)(2,1)S(1)}, u32[]{:S(2)}, u32[]{:S(2)}) %collective-permute-start.6) | collective-permute-done | bytes 262176 | tf_op jit(solution)/shard_map/ppermute | solution.py:351
  52.6 4.8 %collective-permute-done.7.refs_8_ = bf16[4,2,128,128]{3,2,1,0:T(8,128)(2,1)S(1)} collective-permute-done((bf16[4,2,128,128]{3,2,1,0:T(8,128)(2,1)S(1)}, bf16[4,2,128,128]{3,2,1,0:T(8,128)(2,1)S(1)}, u32[]{:S(2)}, u32[]{:S(2)}) %collective-permute-start.7) | collective-permute-done | bytes 262176 | tf_op jit(solution)/shard_map/ppermute | solution.py:351
  59.1 6.1 %collective-permute-done.8.refs_7_ = bf16[4,2,128,128]{3,2,1,0:T(8,128)(2,1)S(1)} collective-permute-done((bf16[4,2,128,128]{3,2,1,0:T(8,128)(2,1)S(1)}, bf16[4,2,128,128]{3,2,1,0:T(8,128)(2,1)S(1)}, u32[]{:S(2)}, u32[]{:S(2)}) %collective-permute-start.8) | collective-permute-done | bytes 262176 | tf_op jit(solution)/shard_map/ppermute | solution.py:351
  65.2 1.7 collective-permute-start.10
  68.5 2.6 %collective-permute-done.10.refs_11_ = bf16[2,2,128,128]{3,2,1,0:T(8,128)(2,1)S(1)} collective-permute-done((bf16[2,2,128,128]{3,2,1,0:T(8,128)(2,1)S(1)}, bf16[2,2,128,128]{3,2,1,0:T(8,128)(2,1)S(1)}, u32[]{:S(2)}, u32[]{:S(2)}) %collective-permute-start.10) | collective-permute-done | bytes 131104 | tf_op jit(solution)/shard_map/ppermute | solution.py:351
  71.1 2.9 %collective-permute-done.9.refs_10_ = bf16[2,2,128,128]{3,2,1,0:T(8,128)(2,1)S(1)} collective-permute-done((bf16[2,2,128,128]{3,2,1,0:T(8,128)(2,1)S(1)}, bf16[2,2,128,128]{3,2,1,0:T(8,128)(2,1)S(1)}, u32[]{:S(2)}, u32[]{:S(2)}) %collective-permute-start.9) | collective-permute-done | bytes 131104 | tf_op jit(solution)/shard_map/ppermute | solution.py:351
  74.0 11.2 %all-gather.3.cloned.1.call-done = bf16[1344,16,128]{2,1,0:T(8,128)(2,1)} async-done(((bf16[168,16,128]{2,1,0:T(8,128)(2,1)}), bf16[1344,16,128]{2,1,0:T(8,128)(2,1)}) %all-gather.3.cloned.1.call-update) | async-done | bytes 5505040 | tf_op jit(solution)/shard_map/all_gather | solution.py:368
  85.3 11.7 %gated_pair.1 = (bf16[128,896]{1,0:T(8,128)(2,1)}, bf16[4,84,16,128]{3,2,1,0:T(8,128)(2,1)}, bf16[4,84,16,128]{3,2,1,0:T(8,128)(2,1)}, bf16[4,84,16,128]{3,2,1,0...) custom-call(s32[168]{0:T(256)} %copy-done.5, s32[14]{0:T(128)} %reshape.58.refs_1_.count_ref, ...), custom_call_target="tpu_custom_call" | custom-call | tf_op jit(solution)/shard_map/gated_pair/pallas_call | solution.py:378
  97.6 2.8 %collective-permute-done.11.other_ref = bf16[4,84,16,128]{3,2,1,0:T(8,128)(2,1)S(1)} collective-permute-done((bf16[4,84,16,128]{3,2,1,0:T(8,128)(2,1)}, bf16[4,84,16,128]{3,2,1,0:T(8,128)(2,1)S(1)}, u32[]{:S(2)}, u32[]{:S(2)}) %collective-permute-start.11) | collective-permute-done | bytes 1376288 | tf_op jit(solution)/shard_map/ppermute | solution.py:429
  103.0 1.6 collective-permute-start.12
  104.6 2.7 %collective-permute-start.14 = (bf16[84,16,128]{2,1,0:T(8,128)(2,1)S(1)}, bf16[84,16,128]{2,1,0:T(8,128)(2,1)S(1)}, u32[]{:S(2)}, u32[]{:S(2)}) collective-permute-start(bf16[84,16,128]{2,1,0:T(8,128)(2,1)S(1)} %get-tuple-element.33), channel_id=1, source_target_pairs={{0,192},{32,224},{64,0},{96,32},{128,64},{160,96},{192,128},{224,1... | collective-permute-start | bytes 1032200 | tf_op jit(solution)/shard_map/ppermute | solution.py:409
  109.2 4.9 %collective-permute-done.12.refs_1_ = bf16[84,16,128]{2,1,0:T(8,128)(2,1)S(1)} collective-permute-done((bf16[84,16,128]{2,1,0:T(8,128)(2,1)S(1)}, bf16[84,16,128]{2,1,0:T(8,128)(2,1)S(1)}, u32[]{:S(2)}, u32[]{:S(2)}) %collective-permute-start.12) | collective-permute-done | bytes 344096 | tf_op jit(solution)/shard_map/ppermute | solution.py:409
  114.6 8.0 %collective-permute-done.13.refs_2_ = bf16[84,16,128]{2,1,0:T(8,128)(2,1)S(1)} collective-permute-done((bf16[84,16,128]{2,1,0:T(8,128)(2,1)S(1)}, bf16[84,16,128]{2,1,0:T(8,128)(2,1)S(1)}, u32[]{:S(2)}, u32[]{:S(2)}) %collective-permute-start.13) | collective-permute-done | bytes 344096 | tf_op jit(solution)/shard_map/ppermute | solution.py:409
  122.6 6.3 %collective-permute-done.16.refs_5_ = bf16[84,16,128]{2,1,0:T(8,128)(2,1)S(1)} collective-permute-done((bf16[84,16,128]{2,1,0:T(8,128)(2,1)S(1)}, bf16[84,16,128]{2,1,0:T(8,128)(2,1)S(1)}, u32[]{:S(2)}, u32[]{:S(2)}) %collective-permute-start.16) | collective-permute-done | bytes 344096 | tf_op jit(solution)/shard_map/ppermute | solution.py:409
  128.9 7.9 %collective-permute-done.17.refs_6_ = bf16[84,16,128]{2,1,0:T(8,128)(2,1)S(1)} collective-permute-done((bf16[84,16,128]{2,1,0:T(8,128)(2,1)S(1)}, bf16[84,16,128]{2,1,0:T(8,128)(2,1)S(1)}, u32[]{:S(2)}, u32[]{:S(2)}) %collective-permute-start.17) | collective-permute-done | bytes 344096 | tf_op jit(solution)/shard_map/ppermute | solution.py:409
  136.7 1.8 unsort_slots.1
  138.6 11.2 %all-to-all-start.1 = ((bf16[32,6,16,128]{3,2,1,0:T(8,128)(2,1)}), bf16[32,6,16,128]{3,2,1,0:T(8,128)(2,1)S(1)}, u32[]{:S(2)}, u32[]{:S(2)}) async-start(bf16[32,6,16,128]{3,2,1,0:T(8,128)(2,1)} %bitcast.15), calls=%async_computation.1 | async-start | bytes 1572864 | tf_op jit(solution)/shard_map/all_to_all | solution.py:337
  150.5 18.2 %all-to-all-done.1 = bf16[32,6,16,128]{3,2,1,0:T(8,128)(2,1)S(1)} async-done(((bf16[32,6,16,128]{3,2,1,0:T(8,128)(2,1)}), bf16[32,6,16,128]{3,2,1,0:T(8,128)(2,1)S(1)}, u32[]{:S(2)}, u32[]{:S(2)}) %all-to-all-start.1) | async-done | bytes 786464 | tf_op jit(solution)/shard_map/all_to_all | solution.py:337
  170.5 1.5 collective-permute-start.22
  172.3 6.0 %collective-permute-start.19 = (bf16[84,16,128]{2,1,0:T(8,128)(2,1)S(1)}, bf16[84,16,128]{2,1,0:T(8,128)(2,1)S(1)}, u32[]{:S(2)}, u32[]{:S(2)}) collective-permute-start(bf16[84,16,128]{2,1,0:T(8,128)(2,1)S(1)} %bitcast.28), channel_id=1, source_target_pairs={{0,32},{32,0},{64,96},{96,64},{128,160},{160,128},{192,224},{224,1... | collective-permute-start | bytes 1032200 | tf_op jit(solution)/shard_map/ppermute | solution.py:429
  178.3 5.8 %collective-permute-start.25 = (bf16[84,16,128]{2,1,0:T(8,128)(2,1)S(1)}, bf16[84,16,128]{2,1,0:T(8,128)(2,1)S(1)}, u32[]{:S(2)}, u32[]{:S(2)}) collective-permute-start(bf16[84,16,128]{2,1,0:T(8,128)(2,1)S(1)} %collective-permute-done.24.refs_6_), channel_id=1, source_target_pairs={{0,32},{32,0},{64,96},{96,64},{128,160},{160,128},{192,224},{224,1... | collective-permute-start | bytes 1032200 | tf_op jit(solution)/shard_map/ppermute | solution.py:429
  184.1 2.2 %collective-permute-start.23 = (bf16[84,16,128]{2,1,0:T(8,128)(2,1)S(1)}, bf16[84,16,128]{2,1,0:T(8,128)(2,1)S(1)}, u32[]{:S(2)}, u32[]{:S(2)}) collective-permute-start(bf16[84,16,128]{2,1,0:T(8,128)(2,1)S(1)} %collective-permute-done.22.refs_4_), channel_id=1, source_target_pairs={{0,32},{32,0},{64,96},{96,64},{128,160},{160,128},{192,224},{224,1... | collective-permute-start | bytes 1032200 | tf_op jit(solution)/shard_map/ppermute | solution.py:429
  186.4 3.5 %collective-permute-start.21 = (bf16[84,16,128]{2,1,0:T(8,128)(2,1)S(1)}, bf16[84,16,128]{2,1,0:T(8,128)(2,1)S(1)}, u32[]{:S(2)}, u32[]{:S(2)}) collective-permute-start(bf16[84,16,128]{2,1,0:T(8,128)(2,1)S(1)} %collective-permute-done.20.refs_2_), channel_id=1, source_target_pairs={{0,32},{32,0},{64,96},{96,64},{128,160},{160,128},{192,224},{224,1... | collective-permute-start | bytes 1032200 | tf_op jit(solution)/shard_map/ppermute | solution.py:429
  192.0 3.1 %widen.1 = (f32[84,128,128]{2,1,0:T(8,128)}, bf16[128,256]{1,0:T(8,128)(2,1)}) custom-call(s32[6]{0:T(128)S(1)} %copy-done.4, bf16[84,16,128]{2,1,0:T(8,128)(2,1)S(1)} %bitcast.29, bf16[84,16,128]{2,1,0:T(8,128)(2,1)S(1)} %collective-permute-done.19.refs_1_, bf16[84,16,128]{2,1,0:T(8,128)(2,1)S(1)} %collective-permute-done.20.refs_2_, ...), custom_call_target="tpu_custom_call" | custom-call | tf_op jit(solution)/shard_map/widen/pallas_call | solution.py:470
  (97 shorter events, 18.3 us)
Async XLA Ops:
  10.4 31.3 %all-to-all-start = ((bf16[32,6,16,128]{3,2,1,0:T(8,128)(2,1)}), bf16[32,6,16,128]{3,2,1,0:T(8,128)(2,1)S(1)}, u32[]{:S(2)}, u32[]{:S(2)}) async-start(bf16[32,6,16,128]{3,2,1,0:T(8,128)(2,1)} %bitcast.33), calls=%async_computation | async-start | bytes 1572864 | tf_op jit(solution)/shard_map/all_to_all | solution.py:337
  22.4 62.8 %all-gather.3.cloned.1.call-start = ((), (), s32[]{:S(2)}) async-start(), calls=%async_computation.6 | async-start | bytes 6193152 | tf_op jit(solution)/shard_map/all_gather | solution.py:368
  22.5 8.4 %collective-permute-start.2 = (bf16[2,128,128]{2,1,0:T(8,128)(2,1)}, bf16[2,128,128]{2,1,0:T(8,128)(2,1)S(1)}, u32[]{:S(2)}, u32[]{:S(2)}) collective-permute-start(bf16[2,128,128]{2,1,0:T(8,128)(2,1)} %get-tuple-element.24), channel_id=1, source_target_pairs={{0,24},{1,25},{2,26},{3,27},{4,28},{5,29},{6,30},{7,31},{8,0},{9,1... | collective-permute-start | bytes 196616 | tf_op jit(solution)/shard_map/ppermute | solution.py:345
  25.0 5.9 %collective-permute-start.1 = (bf16[2,128,128]{2,1,0:T(8,128)(2,1)}, bf16[2,128,128]{2,1,0:T(8,128)(2,1)S(1)}, u32[]{:S(2)}, u32[]{:S(2)}) collective-permute-start(bf16[2,128,128]{2,1,0:T(8,128)(2,1)} %get-tuple-element.24), channel_id=1, source_target_pairs={{0,16},{1,17},{2,18},{3,19},{4,20},{5,21},{6,22},{7,23},{8,24},{9,... | collective-permute-start | bytes 196616 | tf_op jit(solution)/shard_map/ppermute | solution.py:345
  25.6 5.4 %collective-permute-start = (bf16[2,128,128]{2,1,0:T(8,128)(2,1)}, bf16[2,128,128]{2,1,0:T(8,128)(2,1)S(1)}, u32[]{:S(2)}, u32[]{:S(2)}) collective-permute-start(bf16[2,128,128]{2,1,0:T(8,128)(2,1)} %get-tuple-element.24), channel_id=1, source_target_pairs={{0,8},{1,9},{2,10},{3,11},{4,12},{5,13},{6,14},{7,15},{8,16},{9,17... | collective-permute-start | bytes 196616 | tf_op jit(solution)/shard_map/ppermute | solution.py:345
  30.9 54.3 %copy-start.5 = (s32[168]{0:T(256)}, s32[168]{0:T(256)S(1)}, u32[]{:S(2)}) copy-start(s32[168]{0:T(256)S(1)} %reshape.57.table_ref.refs_0_) | copy-start | bytes 2020
  43.7 106.1 %reduce-scatter.3.cloned.1.call-start = ((), (), s32[]{:S(2)}) async-start(), calls=%async_computation.4 | async-start | bytes 2621440 | tf_op jit(solution)/shard_map/reduce_scatter | solution.py:436
  43.7 7.3 %collective-permute-start.6 = (bf16[4,2,128,128]{3,2,1,0:T(8,128)(2,1)S(1)}, bf16[4,2,128,128]{3,2,1,0:T(8,128)(2,1)S(1)}, u32[]{:S(2)}, u32[]{:S(2)}) collective-permute-start(bf16[4,2,128,128]{3,2,1,0:T(8,128)(2,1)S(1)} %pad_maximum_fusion.refs_3_), channel_id=1, source_target_pairs={{0,7},{1,0},{2,1},{3,2},{4,3},{5,4},{6,5},{7,6},{8,15},{9,8},{10,9... | collective-permute-start | bytes 786440 | tf_op jit(solution)/shard_map/ppermute | solution.py:351
  45.8 6.4 %collective-permute-start.3 = (bf16[4,2,128,128]{3,2,1,0:T(8,128)(2,1)S(1)}, bf16[4,2,128,128]{3,2,1,0:T(8,128)(2,1)S(1)}, u32[]{:S(2)}, u32[]{:S(2)}) collective-permute-start(bf16[4,2,128,128]{3,2,1,0:T(8,128)(2,1)S(1)} %pad_maximum_fusion.refs_3_), channel_id=1, source_target_pairs={{0,1},{1,2},{2,3},{3,4},{4,5},{5,6},{6,7},{7,0},{8,9},{9,10},{10,1... | collective-permute-start | bytes 786440 | tf_op jit(solution)/shard_map/ppermute | solution.py:351
  51.0 6.4 %collective-permute-start.7 = (bf16[4,2,128,128]{3,2,1,0:T(8,128)(2,1)S(1)}, bf16[4,2,128,128]{3,2,1,0:T(8,128)(2,1)S(1)}, u32[]{:S(2)}, u32[]{:S(2)}) collective-permute-start(bf16[4,2,128,128]{3,2,1,0:T(8,128)(2,1)S(1)} %collective-permute-done.6.refs_9_), channel_id=1, source_target_pairs={{0,7},{1,0},{2,1},{3,2},{4,3},{5,4},{6,5},{7,6},{8,15},{9,8},{10,9... | collective-permute-start | bytes 786440 | tf_op jit(solution)/shard_map/ppermute | solution.py:351
  52.3 6.7 %collective-permute-start.4 = (bf16[4,2,128,128]{3,2,1,0:T(8,128)(2,1)S(1)}, bf16[4,2,128,128]{3,2,1,0:T(8,128)(2,1)S(1)}, u32[]{:S(2)}, u32[]{:S(2)}) collective-permute-start(bf16[4,2,128,128]{3,2,1,0:T(8,128)(2,1)S(1)} %collective-permute-done.3.refs_4_), channel_id=1, source_target_pairs={{0,1},{1,2},{2,3},{3,4},{4,5},{5,6},{6,7},{7,0},{8,9},{9,10},{10,1... | collective-permute-start | bytes 786440 | tf_op jit(solution)/shard_map/ppermute | solution.py:351
  57.4 7.8 %collective-permute-start.8 = (bf16[4,2,128,128]{3,2,1,0:T(8,128)(2,1)S(1)}, bf16[4,2,128,128]{3,2,1,0:T(8,128)(2,1)S(1)}, u32[]{:S(2)}, u32[]{:S(2)}) collective-permute-start(bf16[4,2,128,128]{3,2,1,0:T(8,128)(2,1)S(1)} %collective-permute-done.7.refs_8_), channel_id=1, source_target_pairs={{0,7},{1,0},{2,1},{3,2},{4,3},{5,4},{6,5},{7,6},{8,15},{9,8},{10,9... | collective-permute-start | bytes 786440 | tf_op jit(solution)/shard_map/ppermute | solution.py:351
  59.0 8.2 %collective-permute-start.5 = (bf16[4,2,128,128]{3,2,1,0:T(8,128)(2,1)S(1)}, bf16[4,2,128,128]{3,2,1,0:T(8,128)(2,1)S(1)}, u32[]{:S(2)}, u32[]{:S(2)}) collective-permute-start(bf16[4,2,128,128]{3,2,1,0:T(8,128)(2,1)S(1)} %collective-permute-done.4.refs_5_), channel_id=1, source_target_pairs={{0,1},{1,2},{2,3},{3,4},{4,5},{5,6},{6,7},{7,0},{8,9},{9,10},{10,1... | collective-permute-start | bytes 786440 | tf_op jit(solution)/shard_map/ppermute | solution.py:351
  65.2 5.9 %collective-permute-start.10 = (bf16[2,2,128,128]{3,2,1,0:T(8,128)(2,1)S(1)}, bf16[2,2,128,128]{3,2,1,0:T(8,128)(2,1)S(1)}, u32[]{:S(2)}, u32[]{:S(2)}) collective-permute-start(bf16[2,2,128,128]{3,2,1,0:T(8,128)(2,1)S(1)} %slice.29), channel_id=1, source_target_pairs={{0,7},{1,0},{2,1},{3,2},{4,3},{5,4},{6,5},{7,6},{8,15},{9,8},{10,9... | collective-permute-start | bytes 393224 | tf_op jit(solution)/shard_map/ppermute | solution.py:351
  67.1 6.9 %collective-permute-start.9 = (bf16[2,2,128,128]{3,2,1,0:T(8,128)(2,1)S(1)}, bf16[2,2,128,128]{3,2,1,0:T(8,128)(2,1)S(1)}, u32[]{:S(2)}, u32[]{:S(2)}) collective-permute-start(bf16[2,2,128,128]{3,2,1,0:T(8,128)(2,1)S(1)} %slice.28), channel_id=1, source_target_pairs={{0,1},{1,2},{2,3},{3,4},{4,5},{5,6},{6,7},{7,0},{8,9},{9,10},{10,1... | collective-permute-start | bytes 393224 | tf_op jit(solution)/shard_map/ppermute | solution.py:351
  97.0 3.4 %collective-permute-start.11 = (bf16[4,84,16,128]{3,2,1,0:T(8,128)(2,1)}, bf16[4,84,16,128]{3,2,1,0:T(8,128)(2,1)S(1)}, u32[]{:S(2)}, u32[]{:S(2)}) collective-permute-start(bf16[4,84,16,128]{3,2,1,0:T(8,128)(2,1)} %get-tuple-element.29), channel_id=1, source_target_pairs={{0,32},{32,0},{64,96},{96,64},{128,160},{160,128},{192,224},{224,1... | collective-permute-start | bytes 4128776 | tf_op jit(solution)/shard_map/ppermute | solution.py:429
  97.4 9.9 %collective-permute-start.15 = (bf16[4,84,16,128]{3,2,1,0:T(8,128)(2,1)}, bf16[4,84,16,128]{3,2,1,0:T(8,128)(2,1)S(1)}, u32[]{:S(2)}, u32[]{:S(2)}) collective-permute-start(bf16[4,84,16,128]{3,2,1,0:T(8,128)(2,1)} %get-tuple-element.35), channel_id=1, source_target_pairs={{0,32},{32,0},{64,96},{96,64},{128,160},{160,128},{192,224},{224,1... | collective-permute-start | bytes 4128776 | tf_op jit(solution)/shard_map/ppermute | solution.py:429
  103.0 11.0 %collective-permute-start.12 = (bf16[84,16,128]{2,1,0:T(8,128)(2,1)S(1)}, bf16[84,16,128]{2,1,0:T(8,128)(2,1)S(1)}, u32[]{:S(2)}, u32[]{:S(2)}) collective-permute-start(bf16[84,16,128]{2,1,0:T(8,128)(2,1)S(1)} %get-tuple-element.31), channel_id=1, source_target_pairs={{0,128},{32,160},{64,192},{96,224},{128,0},{160,32},{192,64},{224,... | collective-permute-start | bytes 1032200 | tf_op jit(solution)/shard_map/ppermute | solution.py:409
  104.6 18.0 %collective-permute-start.13 = (bf16[84,16,128]{2,1,0:T(8,128)(2,1)S(1)}, bf16[84,16,128]{2,1,0:T(8,128)(2,1)S(1)}, u32[]{:S(2)}, u32[]{:S(2)}) collective-permute-start(bf16[84,16,128]{2,1,0:T(8,128)(2,1)S(1)} %get-tuple-element.32), channel_id=1, source_target_pairs={{0,64},{32,96},{64,128},{96,160},{128,192},{160,224},{192,0},{224,... | collective-permute-start | bytes 1032200 | tf_op jit(solution)/shard_map/ppermute | solution.py:409
  104.6 18.0 %collective-permute-start.14 = (bf16[84,16,128]{2,1,0:T(8,128)(2,1)S(1)}, bf16[84,16,128]{2,1,0:T(8,128)(2,1)S(1)}, u32[]{:S(2)}, u32[]{:S(2)}) collective-permute-start(bf16[84,16,128]{2,1,0:T(8,128)(2,1)S(1)} %get-tuple-element.33), channel_id=1, source_target_pairs={{0,192},{32,224},{64,0},{96,32},{128,64},{160,96},{192,128},{224,1... | collective-permute-start | bytes 1032200 | tf_op jit(solution)/shard_map/ppermute | solution.py:409
  108.5 20.4 %collective-permute-start.16 = (bf16[84,16,128]{2,1,0:T(8,128)(2,1)S(1)}, bf16[84,16,128]{2,1,0:T(8,128)(2,1)S(1)}, u32[]{:S(2)}, u32[]{:S(2)}) collective-permute-start(bf16[84,16,128]{2,1,0:T(8,128)(2,1)S(1)} %get-tuple-element.37), channel_id=1, source_target_pairs={{0,128},{32,160},{64,192},{96,224},{128,0},{160,32},{192,64},{224,... | collective-permute-start | bytes 1032200 | tf_op jit(solution)/shard_map/ppermute | solution.py:409
  108.9 27.8 %collective-permute-start.17 = (bf16[84,16,128]{2,1,0:T(8,128)(2,1)S(1)}, bf16[84,16,128]{2,1,0:T(8,128)(2,1)S(1)}, u32[]{:S(2)}, u32[]{:S(2)}) collective-permute-start(bf16[84,16,128]{2,1,0:T(8,128)(2,1)S(1)} %get-tuple-element.38), channel_id=1, source_target_pairs={{0,64},{32,96},{64,128},{96,160},{128,192},{160,224},{192,0},{224,... | collective-permute-start | bytes 1032200 | tf_op jit(solution)/shard_map/ppermute | solution.py:409
  114.1 22.6 %collective-permute-start.18 = (bf16[84,16,128]{2,1,0:T(8,128)(2,1)S(1)}, bf16[84,16,128]{2,1,0:T(8,128)(2,1)S(1)}, u32[]{:S(2)}, u32[]{:S(2)}) collective-permute-start(bf16[84,16,128]{2,1,0:T(8,128)(2,1)S(1)} %get-tuple-element.39), channel_id=1, source_target_pairs={{0,192},{32,224},{64,0},{96,32},{128,64},{160,96},{192,128},{224,1... | collective-permute-start | bytes 1032200 | tf_op jit(solution)/shard_map/ppermute | solution.py:409
  138.6 30.2 %all-to-all-start.1 = ((bf16[32,6,16,128]{3,2,1,0:T(8,128)(2,1)}), bf16[32,6,16,128]{3,2,1,0:T(8,128)(2,1)S(1)}, u32[]{:S(2)}, u32[]{:S(2)}) async-start(bf16[32,6,16,128]{3,2,1,0:T(8,128)(2,1)} %bitcast.15), calls=%async_computation.1 | async-start | bytes 1572864 | tf_op jit(solution)/shard_map/all_to_all | solution.py:337
  149.7 41.4 %reduce-scatter.5.cloned.1.call-start = ((), (), s32[]{:S(2)}) async-start(), calls=%async_computation.5 | async-start | bytes 589824 | tf_op jit(solution)/shard_map/reduce_scatter | solution.py:467
  169.9 8.4 %collective-permute-start.24 = (bf16[84,16,128]{2,1,0:T(8,128)(2,1)S(1)}, bf16[84,16,128]{2,1,0:T(8,128)(2,1)S(1)}, u32[]{:S(2)}, u32[]{:S(2)}) collective-permute-start(bf16[84,16,128]{2,1,0:T(8,128)(2,1)S(1)} %bitcast.25), channel_id=1, source_target_pairs={{0,192},{32,224},{64,0},{96,32},{128,64},{160,96},{192,128},{224,1... | collective-permute-start | bytes 1032200 | tf_op jit(solution)/shard_map/ppermute | solution.py:409
  170.5 13.6 %collective-permute-start.22 = (bf16[84,16,128]{2,1,0:T(8,128)(2,1)S(1)}, bf16[84,16,128]{2,1,0:T(8,128)(2,1)S(1)}, u32[]{:S(2)}, u32[]{:S(2)}) collective-permute-start(bf16[84,16,128]{2,1,0:T(8,128)(2,1)S(1)} %bitcast.26), channel_id=1, source_target_pairs={{0,128},{32,160},{64,192},{96,224},{128,0},{160,32},{192,64},{224,... | collective-permute-start | bytes 1032200 | tf_op jit(solution)/shard_map/ppermute | solution.py:409
  172.0 14.4 %collective-permute-start.20 = (bf16[84,16,128]{2,1,0:T(8,128)(2,1)S(1)}, bf16[84,16,128]{2,1,0:T(8,128)(2,1)S(1)}, u32[]{:S(2)}, u32[]{:S(2)}) collective-permute-start(bf16[84,16,128]{2,1,0:T(8,128)(2,1)S(1)} %bitcast.27), channel_id=1, source_target_pairs={{0,64},{32,96},{64,128},{96,160},{128,192},{160,224},{192,0},{224,... | collective-permute-start | bytes 1032200 | tf_op jit(solution)/shard_map/ppermute | solution.py:409
  172.3 17.6 %collective-permute-start.19 = (bf16[84,16,128]{2,1,0:T(8,128)(2,1)S(1)}, bf16[84,16,128]{2,1,0:T(8,128)(2,1)S(1)}, u32[]{:S(2)}, u32[]{:S(2)}) collective-permute-start(bf16[84,16,128]{2,1,0:T(8,128)(2,1)S(1)} %bitcast.28), channel_id=1, source_target_pairs={{0,32},{32,0},{64,96},{96,64},{128,160},{160,128},{192,224},{224,1... | collective-permute-start | bytes 1032200 | tf_op jit(solution)/shard_map/ppermute | solution.py:429
  178.3 11.6 %collective-permute-start.25 = (bf16[84,16,128]{2,1,0:T(8,128)(2,1)S(1)}, bf16[84,16,128]{2,1,0:T(8,128)(2,1)S(1)}, u32[]{:S(2)}, u32[]{:S(2)}) collective-permute-start(bf16[84,16,128]{2,1,0:T(8,128)(2,1)S(1)} %collective-permute-done.24.refs_6_), channel_id=1, source_target_pairs={{0,32},{32,0},{64,96},{96,64},{128,160},{160,128},{192,224},{224,1... | collective-permute-start | bytes 1032200 | tf_op jit(solution)/shard_map/ppermute | solution.py:429
  184.1 5.7 %collective-permute-start.23 = (bf16[84,16,128]{2,1,0:T(8,128)(2,1)S(1)}, bf16[84,16,128]{2,1,0:T(8,128)(2,1)S(1)}, u32[]{:S(2)}, u32[]{:S(2)}) collective-permute-start(bf16[84,16,128]{2,1,0:T(8,128)(2,1)S(1)} %collective-permute-done.22.refs_4_), channel_id=1, source_target_pairs={{0,32},{32,0},{64,96},{96,64},{128,160},{160,128},{192,224},{224,1... | collective-permute-start | bytes 1032200 | tf_op jit(solution)/shard_map/ppermute | solution.py:429
  186.4 4.8 %collective-permute-start.21 = (bf16[84,16,128]{2,1,0:T(8,128)(2,1)S(1)}, bf16[84,16,128]{2,1,0:T(8,128)(2,1)S(1)}, u32[]{:S(2)}, u32[]{:S(2)}) collective-permute-start(bf16[84,16,128]{2,1,0:T(8,128)(2,1)S(1)} %collective-permute-done.20.refs_2_), channel_id=1, source_target_pairs={{0,32},{32,0},{64,96},{96,64},{128,160},{160,128},{192,224},{224,1... | collective-permute-start | bytes 1032200 | tf_op jit(solution)/shard_map/ppermute | solution.py:429
  (18 other events, 395.3 us)
Sparse Core Ops, SparseCore 0:
  43.8 41.3 all-gather.2
  97.1 33.0 reduce-scatter.2
  153.3 34.1 reduce-scatter.4

commit v7 on v6

--- a/solution.py
+++ b/solution.py
@@ -116,6 +116,14 @@
     for k, out_ref in enumerate(out_refs):
         y = lax.rem(where_ref[5] + k, 4)
         out_ref[...] = (mine_ref[y].astype(F32) + other_ref[y].astype(F32)).astype(BF16)
+
+
+def relay_kernel(near_ref, back_ref, first_ref, last_ref, near_out, back_out):
+    half = first_ref.shape[0]
+    near_out[:half] = (near_ref[:half].astype(F32) + first_ref[...].astype(F32)).astype(BF16)
+    near_out[half:] = near_ref[half:]
+    back_out[:half] = back_ref[:half]
+    back_out[half:] = (back_ref[half:].astype(F32) + last_ref[...].astype(F32)).astype(BF16)
 
 
 def main_kernel(sides, ring, panels, table_ref, count_ref, where_ref, *refs):
@@ -431,7 +439,17 @@
     mine = [mine_g, mine_u]
     other = [swap(other_g), swap(other_u)]
     sent = [reduced(mine[m], other[m]) for m in range(2)]
-    came = [[sent[m][0]] + [around(sent[m][s], s) for s in (2, 1, 3)] for m in range(2)]
+    middle = used // 4
+    passed = [(around(sent[m][2][:middle], 1), around(sent[m][2][middle:], 3)) for m in range(2)]
+    came = []
+    for m in range(2):
+        near, back = pl.pallas_call(
+            relay_kernel,
+            out_shape=(piece, piece),
+            compiler_params=params,
+            name="relay",
+        )(sent[m][1], sent[m][3], *passed[m])
+        came.append([sent[m][0], around(near, 1), around(back, 3)])
     columns = [[x * ring + z for x in range(sides)] for z in range(ring)]
     row_terms = lax.psum_scatter(
         terms, "mp", scatter_dimension=0, axis_index_groups=columns, tiled=True
@@ -442,7 +460,7 @@
         grid_spec=pltpu.PrefetchScalarGridSpec(
             num_scalar_prefetch=2,
             grid=(1,),
-            in_specs=[whole(piece.shape)] * 8,
+            in_specs=[whole(piece.shape)] * 6,
             out_specs=whole((slots, part, BLOCK)),
         ),
         compiler_params=less,

time: 203 us -> 193 us (0.951)
  waiting for transfers between devices: 92.5 us -> 82.3 us
    ppermute x9 -> x11, waiting for transfers between devices: 27 us -> 16.4 us  [around(): return lax.ppermute(value, 'dp', pairs)]
    ppermute x9 -> x11, starting transfers between devices: 7.85 us -> 10.6 us  [around(): return lax.ppermute(value, 'dp', pairs)]
  transfers between devices with their start and end apart: 31 -> 33, of which waited for: 16 -> 18; matrix products, arithmetic and copies ran while one was open for 3% -> 3% of each run, Pallas kernels for 3% -> 3%
where the time goes in v7:
time: 193 us
  waiting for transfers between devices  82.3 us (43%)
  starting transfers between devices  63.4 us (33%)
  Pallas kernels  25.7 us (13%)
  between operations  14.1 us (7%)
  other arithmetic  4.39 us (2%)
  local copies, waits for them, and re-layouts  2.65 us (1%)
    all_to_all x2, waiting for transfers between devices, exchange(): lax.all_to_all(values.reshape(shape), 'mp', 0, 0).reshape(values.shape)  29.5 us
    all_to_all x2, starting transfers between devices, exchange(): lax.all_to_all(values.reshape(shape), 'mp', 0, 0).reshape(values.shape)  22.7 us
    ppermute x8, waiting for transfers between devices, along(): return lax.ppermute(value, 'mp', pairs)  20.4 us
    ppermute x6, starting transfers between devices, swap(): return lax.ppermute(value, 'dp', [(d, d ^ 1) for d in range(groups)])  17.9 us
    ppermute x11, waiting for transfers between devices, around(): return lax.ppermute(value, 'dp', pairs)  16.4 us
    pallas_call x1, Pallas kernels, per_device(): pl.pallas_call(lambda *refs: main_kernel(sides, ring, panels, *refs), out...  11.7 us
    all_gather x1, waiting for transfers between devices, per_device(): held = lax.all_gather(ordered, 'dp')  11.2 us
    ppermute x11, starting transfers between devices, around(): return lax.ppermute(value, 'dp', pairs)  10.6 us
  transfers between devices with their start and end apart: 33, of which 18 were waited for; matrix products, arithmetic and copies ran while one was open for 3% of the time, Pallas kernels for 3%

profile of v7, /device:TPU:1, one launch (start us, length us, event | category | flops | bytes accessed | tf_op | source)
XLA Modules:
  0.0 192.5 jit_solution(17246919306710764204)
XLA Ops:
  7.2 3.2 %send_pack.1 = (bf16[192,16,128]{2,1,0:T(8,128)(2,1)}, bf16[2,128,128]{2,1,0:T(8,128)(2,1)}) custom-call(s32[2,1344]{1,0:T(2,128)} %refs_1_.3, bf16[2,42,128,128]{3,2,1,0:T(8,128)(2,1)} %refs_1_.2, bf16[128,256]{1,0:T(8,128)(2,1)} %refs_2_.1), custom_call_target="tpu_custom_call" | custom-call | tf_op jit(solution)/shard_map/send_pack/pallas_call | solution.py:324
  10.4 12.0 %all-to-all-start = ((bf16[32,6,16,128]{3,2,1,0:T(8,128)(2,1)}), bf16[32,6,16,128]{3,2,1,0:T(8,128)(2,1)S(1)}, u32[]{:S(2)}, u32[]{:S(2)}) async-start(bf16[32,6,16,128]{3,2,1,0:T(8,128)(2,1)} %bitcast.33), calls=%async_computation | async-start | bytes 1572864 | tf_op jit(solution)/shard_map/all_to_all | solution.py:345
  22.5 2.6 %collective-permute-start.2 = (bf16[2,128,128]{2,1,0:T(8,128)(2,1)}, bf16[2,128,128]{2,1,0:T(8,128)(2,1)S(1)}, u32[]{:S(2)}, u32[]{:S(2)}) collective-permute-start(bf16[2,128,128]{2,1,0:T(8,128)(2,1)} %get-tuple-element.28), channel_id=1, source_target_pairs={{0,24},{1,25},{2,26},{3,27},{4,28},{5,29},{6,30},{7,31},{8,0},{9,1... | collective-permute-start | bytes 196616 | tf_op jit(solution)/shard_map/ppermute | solution.py:353
  27.6 3.2 %select_reduce_fusion = s32[7,2,12]{2,1,0:T(2,128)S(1)} fusion(s32[2,32,42]{2,1,0:T(8,128)S(1)} %get-tuple-element.58, s32[7,2,32,42]{3,2,1,0:T(8,128)S(1)} %add_select_fusion), kind=kLoop, calls=%fused_computation | loop fusion | flops 677208 | bytes 86688 | tf_op jit(solution)/shard_map/reduce_sum | solution.py:46
  31.0 10.7 %all-to-all-done = bf16[32,6,16,128]{3,2,1,0:T(8,128)(2,1)S(1)} async-done(((bf16[32,6,16,128]{3,2,1,0:T(8,128)(2,1)}), bf16[32,6,16,128]{3,2,1,0:T(8,128)(2,1)S(1)}, u32[]{:S(2)}, u32[]{:S(2)}) %all-to-all-start) | async-done | bytes 786464 | tf_op jit(solution)/shard_map/all_to_all | solution.py:345
  41.7 2.0 %sort_slots.1 = bf16[168,16,128]{2,1,0:T(8,128)(2,1)} custom-call(s32[168]{0:T(256)S(1)} %reshape.57.table_ref.refs_0_, bf16[192,16,128]{2,1,0:T(8,128)(2,1)S(1)} %bitcast.23), custom_call_target="tpu_custom_call" | custom-call | tf_op jit(solution)/shard_map/sort_slots/pallas_call | solution.py:364
  43.7 2.1 %collective-permute-start.6 = (bf16[4,2,128,128]{3,2,1,0:T(8,128)(2,1)S(1)}, bf16[4,2,128,128]{3,2,1,0:T(8,128)(2,1)S(1)}, u32[]{:S(2)}, u32[]{:S(2)}) collective-permute-start(bf16[4,2,128,128]{3,2,1,0:T(8,128)(2,1)S(1)} %pad_maximum_fusion.refs_3_), channel_id=1, source_target_pairs={{0,7},{1,0},{2,1},{3,2},{4,3},{5,4},{6,5},{7,6},{8,15},{9,8},{10,9... | collective-permute-start | bytes 786440 | tf_op jit(solution)/shard_map/ppermute | solution.py:359
  45.8 1.5 collective-permute-start.3
  47.3 3.7 %collective-permute-done.6.refs_9_ = bf16[4,2,128,128]{3,2,1,0:T(8,128)(2,1)S(1)} collective-permute-done((bf16[4,2,128,128]{3,2,1,0:T(8,128)(2,1)S(1)}, bf16[4,2,128,128]{3,2,1,0:T(8,128)(2,1)S(1)}, u32[]{:S(2)}, u32[]{:S(2)}) %collective-permute-start.6) | collective-permute-done | bytes 262176 | tf_op jit(solution)/shard_map/ppermute | solution.py:359
  52.6 4.8 %collective-permute-done.7.refs_8_ = bf16[4,2,128,128]{3,2,1,0:T(8,128)(2,1)S(1)} collective-permute-done((bf16[4,2,128,128]{3,2,1,0:T(8,128)(2,1)S(1)}, bf16[4,2,128,128]{3,2,1,0:T(8,128)(2,1)S(1)}, u32[]{:S(2)}, u32[]{:S(2)}) %collective-permute-start.7) | collective-permute-done | bytes 262176 | tf_op jit(solution)/shard_map/ppermute | solution.py:359
  59.1 6.1 %collective-permute-done.8.refs_7_ = bf16[4,2,128,128]{3,2,1,0:T(8,128)(2,1)S(1)} collective-permute-done((bf16[4,2,128,128]{3,2,1,0:T(8,128)(2,1)S(1)}, bf16[4,2,128,128]{3,2,1,0:T(8,128)(2,1)S(1)}, u32[]{:S(2)}, u32[]{:S(2)}) %collective-permute-start.8) | collective-permute-done | bytes 262176 | tf_op jit(solution)/shard_map/ppermute | solution.py:359
  65.2 1.7 collective-permute-start.10
  68.6 2.5 %collective-permute-done.10.refs_11_ = bf16[2,2,128,128]{3,2,1,0:T(8,128)(2,1)S(1)} collective-permute-done((bf16[2,2,128,128]{3,2,1,0:T(8,128)(2,1)S(1)}, bf16[2,2,128,128]{3,2,1,0:T(8,128)(2,1)S(1)}, u32[]{:S(2)}, u32[]{:S(2)}) %collective-permute-start.10) | collective-permute-done | bytes 131104 | tf_op jit(solution)/shard_map/ppermute | solution.py:359
  71.1 2.9 %collective-permute-done.9.refs_10_ = bf16[2,2,128,128]{3,2,1,0:T(8,128)(2,1)S(1)} collective-permute-done((bf16[2,2,128,128]{3,2,1,0:T(8,128)(2,1)S(1)}, bf16[2,2,128,128]{3,2,1,0:T(8,128)(2,1)S(1)}, u32[]{:S(2)}, u32[]{:S(2)}) %collective-permute-start.9) | collective-permute-done | bytes 131104 | tf_op jit(solution)/shard_map/ppermute | solution.py:359
  74.0 11.2 %all-gather.3.cloned.1.call-done = bf16[1344,16,128]{2,1,0:T(8,128)(2,1)} async-done(((bf16[168,16,128]{2,1,0:T(8,128)(2,1)}), bf16[1344,16,128]{2,1,0:T(8,128)(2,1)}) %all-gather.3.cloned.1.call-update) | async-done | bytes 5505040 | tf_op jit(solution)/shard_map/all_gather | solution.py:376
  85.3 11.7 %gated_pair.1 = (bf16[128,896]{1,0:T(8,128)(2,1)}, bf16[4,84,16,128]{3,2,1,0:T(8,128)(2,1)}, bf16[4,84,16,128]{3,2,1,0:T(8,128)(2,1)}, bf16[4,84,16,128]{3,2,1,0...) custom-call(s32[168]{0:T(256)} %copy-done.5, s32[14]{0:T(128)} %reshape.58.refs_1_.count_ref, ...), custom_call_target="tpu_custom_call" | custom-call | tf_op jit(solution)/shard_map/gated_pair/pallas_call | solution.py:386
  97.6 2.8 %collective-permute-done.11.other_ref = bf16[4,84,16,128]{3,2,1,0:T(8,128)(2,1)S(1)} collective-permute-done((bf16[4,84,16,128]{3,2,1,0:T(8,128)(2,1)}, bf16[4,84,16,128]{3,2,1,0:T(8,128)(2,1)S(1)}, u32[]{:S(2)}, u32[]{:S(2)}) %collective-permute-start.11) | collective-permute-done | bytes 1376288 | tf_op jit(solution)/shard_map/ppermute | solution.py:437
  104.6 1.8 collective-permute-start.18
  107.6 1.4 collective-permute-done.12.first_ref
  109.2 2.7 %collective-permute-start.15 = (bf16[84,16,128]{2,1,0:T(8,128)(2,1)S(1)}, bf16[84,16,128]{2,1,0:T(8,128)(2,1)S(1)}, u32[]{:S(2)}, u32[]{:S(2)}) collective-permute-start(bf16[84,16,128]{2,1,0:T(8,128)(2,1)S(1)} %get-tuple-element.39), channel_id=1, source_target_pairs={{0,192},{32,224},{64,0},{96,32},{128,64},{160,96},{192,128},{224,1... | collective-permute-start | bytes 1032200 | tf_op jit(solution)/shard_map/ppermute | solution.py:417
  112.8 2.5 %collective-permute-start.20 = (bf16[84,16,128]{2,1,0:T(8,128)(2,1)S(1)}, bf16[84,16,128]{2,1,0:T(8,128)(2,1)S(1)}, u32[]{:S(2)}, u32[]{:S(2)}) collective-permute-start(bf16[84,16,128]{2,1,0:T(8,128)(2,1)S(1)} %get-tuple-element.47), channel_id=1, source_target_pairs={{0,192},{32,224},{64,0},{96,32},{128,64},{160,96},{192,128},{224,1... | collective-permute-start | bytes 1032200 | tf_op jit(solution)/shard_map/ppermute | solution.py:417
  115.3 5.3 %collective-permute-done.14.refs_1_ = bf16[84,16,128]{2,1,0:T(8,128)(2,1)S(1)} collective-permute-done((bf16[84,16,128]{2,1,0:T(8,128)(2,1)S(1)}, bf16[84,16,128]{2,1,0:T(8,128)(2,1)S(1)}, u32[]{:S(2)}, u32[]{:S(2)}) %collective-permute-start.14) | collective-permute-done | bytes 344096 | tf_op jit(solution)/shard_map/ppermute | solution.py:417
  120.6 7.4 %collective-permute-done.19.refs_4_ = bf16[84,16,128]{2,1,0:T(8,128)(2,1)S(1)} collective-permute-done((bf16[84,16,128]{2,1,0:T(8,128)(2,1)S(1)}, bf16[84,16,128]{2,1,0:T(8,128)(2,1)S(1)}, u32[]{:S(2)}, u32[]{:S(2)}) %collective-permute-start.19) | collective-permute-done | bytes 344096 | tf_op jit(solution)/shard_map/ppermute | solution.py:417
  128.0 1.8 unsort_slots.1
  129.8 10.7 %all-to-all-start.1 = ((bf16[32,6,16,128]{3,2,1,0:T(8,128)(2,1)}), bf16[32,6,16,128]{3,2,1,0:T(8,128)(2,1)S(1)}, u32[]{:S(2)}, u32[]{:S(2)}) async-start(bf16[32,6,16,128]{3,2,1,0:T(8,128)(2,1)} %bitcast.15), calls=%async_computation.1 | async-start | bytes 1572864 | tf_op jit(solution)/shard_map/all_to_all | solution.py:345
  141.2 18.8 %all-to-all-done.1 = bf16[32,6,16,128]{3,2,1,0:T(8,128)(2,1)S(1)} async-done(((bf16[32,6,16,128]{3,2,1,0:T(8,128)(2,1)}), bf16[32,6,16,128]{3,2,1,0:T(8,128)(2,1)S(1)}, u32[]{:S(2)}, u32[]{:S(2)}) %all-to-all-start.1) | async-done | bytes 786464 | tf_op jit(solution)/shard_map/all_to_all | solution.py:345
  161.3 1.6 collective-permute-start.24
  162.9 5.2 %collective-permute-start.21 = (bf16[84,16,128]{2,1,0:T(8,128)(2,1)S(1)}, bf16[84,16,128]{2,1,0:T(8,128)(2,1)S(1)}, u32[]{:S(2)}, u32[]{:S(2)}) collective-permute-start(bf16[84,16,128]{2,1,0:T(8,128)(2,1)S(1)} %bitcast.28), channel_id=1, source_target_pairs={{0,32},{32,0},{64,96},{96,64},{128,160},{160,128},{192,224},{224,1... | collective-permute-start | bytes 1032200 | tf_op jit(solution)/shard_map/ppermute | solution.py:437
  168.1 7.3 %collective-permute-start.27 = (bf16[84,16,128]{2,1,0:T(8,128)(2,1)S(1)}, bf16[84,16,128]{2,1,0:T(8,128)(2,1)S(1)}, u32[]{:S(2)}, u32[]{:S(2)}) collective-permute-start(bf16[84,16,128]{2,1,0:T(8,128)(2,1)S(1)} %collective-permute-done.26.refs_6_), channel_id=1, source_target_pairs={{0,32},{32,0},{64,96},{96,64},{128,160},{160,128},{192,224},{224,1... | collective-permute-start | bytes 1032200 | tf_op jit(solution)/shard_map/ppermute | solution.py:437
  175.4 1.7 collective-permute-start.25
  177.7 3.0 %collective-permute-start.23 = (bf16[84,16,128]{2,1,0:T(8,128)(2,1)S(1)}, bf16[84,16,128]{2,1,0:T(8,128)(2,1)S(1)}, u32[]{:S(2)}, u32[]{:S(2)}) collective-permute-start(bf16[84,16,128]{2,1,0:T(8,128)(2,1)S(1)} %collective-permute-done.22.refs_2_), channel_id=1, source_target_pairs={{0,32},{32,0},{64,96},{96,64},{128,160},{160,128},{192,224},{224,1... | collective-permute-start | bytes 1032200 | tf_op jit(solution)/shard_map/ppermute | solution.py:437
  182.8 3.1 %widen.1 = (f32[84,128,128]{2,1,0:T(8,128)}, bf16[128,256]{1,0:T(8,128)(2,1)}) custom-call(s32[6]{0:T(128)S(1)} %copy-done.4, bf16[84,16,128]{2,1,0:T(8,128)(2,1)S(1)} %bitcast.29, bf16[84,16,128]{2,1,0:T(8,128)(2,1)S(1)} %collective-permute-done.21.refs_1_, bf16[84,16,128]{2,1,0:T(8,128)(2,1)S(1)} %collective-permute-done.22.refs_2_, ...), custom_call_target="tpu_custom_call" | custom-call | tf_op jit(solution)/shard_map/widen/pallas_call | solution.py:488
  (105 shorter events, 19.4 us)
Async XLA Ops:
  10.4 31.3 %all-to-all-start = ((bf16[32,6,16,128]{3,2,1,0:T(8,128)(2,1)}), bf16[32,6,16,128]{3,2,1,0:T(8,128)(2,1)S(1)}, u32[]{:S(2)}, u32[]{:S(2)}) async-start(bf16[32,6,16,128]{3,2,1,0:T(8,128)(2,1)} %bitcast.33), calls=%async_computation | async-start | bytes 1572864 | tf_op jit(solution)/shard_map/all_to_all | solution.py:345
  22.4 62.8 %all-gather.3.cloned.1.call-start = ((), (), s32[]{:S(2)}) async-start(), calls=%async_computation.6 | async-start | bytes 6193152 | tf_op jit(solution)/shard_map/all_gather | solution.py:376
  22.5 8.4 %collective-permute-start.2 = (bf16[2,128,128]{2,1,0:T(8,128)(2,1)}, bf16[2,128,128]{2,1,0:T(8,128)(2,1)S(1)}, u32[]{:S(2)}, u32[]{:S(2)}) collective-permute-start(bf16[2,128,128]{2,1,0:T(8,128)(2,1)} %get-tuple-element.28), channel_id=1, source_target_pairs={{0,24},{1,25},{2,26},{3,27},{4,28},{5,29},{6,30},{7,31},{8,0},{9,1... | collective-permute-start | bytes 196616 | tf_op jit(solution)/shard_map/ppermute | solution.py:353
  25.0 5.9 %collective-permute-start.1 = (bf16[2,128,128]{2,1,0:T(8,128)(2,1)}, bf16[2,128,128]{2,1,0:T(8,128)(2,1)S(1)}, u32[]{:S(2)}, u32[]{:S(2)}) collective-permute-start(bf16[2,128,128]{2,1,0:T(8,128)(2,1)} %get-tuple-element.28), channel_id=1, source_target_pairs={{0,16},{1,17},{2,18},{3,19},{4,20},{5,21},{6,22},{7,23},{8,24},{9,... | collective-permute-start | bytes 196616 | tf_op jit(solution)/shard_map/ppermute | solution.py:353
  25.6 5.4 %collective-permute-start = (bf16[2,128,128]{2,1,0:T(8,128)(2,1)}, bf16[2,128,128]{2,1,0:T(8,128)(2,1)S(1)}, u32[]{:S(2)}, u32[]{:S(2)}) collective-permute-start(bf16[2,128,128]{2,1,0:T(8,128)(2,1)} %get-tuple-element.28), channel_id=1, source_target_pairs={{0,8},{1,9},{2,10},{3,11},{4,12},{5,13},{6,14},{7,15},{8,16},{9,17... | collective-permute-start | bytes 196616 | tf_op jit(solution)/shard_map/ppermute | solution.py:353
  43.7 96.9 %reduce-scatter.3.cloned.1.call-start = ((), (), s32[]{:S(2)}) async-start(), calls=%async_computation.4 | async-start | bytes 2621440 | tf_op jit(solution)/shard_map/reduce_scatter | solution.py:454
  43.7 7.3 %collective-permute-start.6 = (bf16[4,2,128,128]{3,2,1,0:T(8,128)(2,1)S(1)}, bf16[4,2,128,128]{3,2,1,0:T(8,128)(2,1)S(1)}, u32[]{:S(2)}, u32[]{:S(2)}) collective-permute-start(bf16[4,2,128,128]{3,2,1,0:T(8,128)(2,1)S(1)} %pad_maximum_fusion.refs_3_), channel_id=1, source_target_pairs={{0,7},{1,0},{2,1},{3,2},{4,3},{5,4},{6,5},{7,6},{8,15},{9,8},{10,9... | collective-permute-start | bytes 786440 | tf_op jit(solution)/shard_map/ppermute | solution.py:359
  45.8 6.4 %collective-permute-start.3 = (bf16[4,2,128,128]{3,2,1,0:T(8,128)(2,1)S(1)}, bf16[4,2,128,128]{3,2,1,0:T(8,128)(2,1)S(1)}, u32[]{:S(2)}, u32[]{:S(2)}) collective-permute-start(bf16[4,2,128,128]{3,2,1,0:T(8,128)(2,1)S(1)} %pad_maximum_fusion.refs_3_), channel_id=1, source_target_pairs={{0,1},{1,2},{2,3},{3,4},{4,5},{5,6},{6,7},{7,0},{8,9},{9,10},{10,1... | collective-permute-start | bytes 786440 | tf_op jit(solution)/shard_map/ppermute | solution.py:359
  51.0 6.4 %collective-permute-start.7 = (bf16[4,2,128,128]{3,2,1,0:T(8,128)(2,1)S(1)}, bf16[4,2,128,128]{3,2,1,0:T(8,128)(2,1)S(1)}, u32[]{:S(2)}, u32[]{:S(2)}) collective-permute-start(bf16[4,2,128,128]{3,2,1,0:T(8,128)(2,1)S(1)} %collective-permute-done.6.refs_9_), channel_id=1, source_target_pairs={{0,7},{1,0},{2,1},{3,2},{4,3},{5,4},{6,5},{7,6},{8,15},{9,8},{10,9... | collective-permute-start | bytes 786440 | tf_op jit(solution)/shard_map/ppermute | solution.py:359
  52.3 6.7 %collective-permute-start.4 = (bf16[4,2,128,128]{3,2,1,0:T(8,128)(2,1)S(1)}, bf16[4,2,128,128]{3,2,1,0:T(8,128)(2,1)S(1)}, u32[]{:S(2)}, u32[]{:S(2)}) collective-permute-start(bf16[4,2,128,128]{3,2,1,0:T(8,128)(2,1)S(1)} %collective-permute-done.3.refs_4_), channel_id=1, source_target_pairs={{0,1},{1,2},{2,3},{3,4},{4,5},{5,6},{6,7},{7,0},{8,9},{9,10},{10,1... | collective-permute-start | bytes 786440 | tf_op jit(solution)/shard_map/ppermute | solution.py:359
  57.4 7.8 %collective-permute-start.8 = (bf16[4,2,128,128]{3,2,1,0:T(8,128)(2,1)S(1)}, bf16[4,2,128,128]{3,2,1,0:T(8,128)(2,1)S(1)}, u32[]{:S(2)}, u32[]{:S(2)}) collective-permute-start(bf16[4,2,128,128]{3,2,1,0:T(8,128)(2,1)S(1)} %collective-permute-done.7.refs_8_), channel_id=1, source_target_pairs={{0,7},{1,0},{2,1},{3,2},{4,3},{5,4},{6,5},{7,6},{8,15},{9,8},{10,9... | collective-permute-start | bytes 786440 | tf_op jit(solution)/shard_map/ppermute | solution.py:359
  59.0 8.2 %collective-permute-start.5 = (bf16[4,2,128,128]{3,2,1,0:T(8,128)(2,1)S(1)}, bf16[4,2,128,128]{3,2,1,0:T(8,128)(2,1)S(1)}, u32[]{:S(2)}, u32[]{:S(2)}) collective-permute-start(bf16[4,2,128,128]{3,2,1,0:T(8,128)(2,1)S(1)} %collective-permute-done.4.refs_5_), channel_id=1, source_target_pairs={{0,1},{1,2},{2,3},{3,4},{4,5},{5,6},{6,7},{7,0},{8,9},{9,10},{10,1... | collective-permute-start | bytes 786440 | tf_op jit(solution)/shard_map/ppermute | solution.py:359
  65.2 5.9 %collective-permute-start.10 = (bf16[2,2,128,128]{3,2,1,0:T(8,128)(2,1)S(1)}, bf16[2,2,128,128]{3,2,1,0:T(8,128)(2,1)S(1)}, u32[]{:S(2)}, u32[]{:S(2)}) collective-permute-start(bf16[2,2,128,128]{3,2,1,0:T(8,128)(2,1)S(1)} %slice.45), channel_id=1, source_target_pairs={{0,7},{1,0},{2,1},{3,2},{4,3},{5,4},{6,5},{7,6},{8,15},{9,8},{10,9... | collective-permute-start | bytes 393224 | tf_op jit(solution)/shard_map/ppermute | solution.py:359
  67.1 6.9 %collective-permute-start.9 = (bf16[2,2,128,128]{3,2,1,0:T(8,128)(2,1)S(1)}, bf16[2,2,128,128]{3,2,1,0:T(8,128)(2,1)S(1)}, u32[]{:S(2)}, u32[]{:S(2)}) collective-permute-start(bf16[2,2,128,128]{3,2,1,0:T(8,128)(2,1)S(1)} %slice.44), channel_id=1, source_target_pairs={{0,1},{1,2},{2,3},{3,4},{4,5},{5,6},{6,7},{7,0},{8,9},{9,10},{10,1... | collective-permute-start | bytes 393224 | tf_op jit(solution)/shard_map/ppermute | solution.py:359
  97.4 5.9 %collective-permute-start.16 = (bf16[4,84,16,128]{3,2,1,0:T(8,128)(2,1)}, bf16[4,84,16,128]{3,2,1,0:T(8,128)(2,1)S(1)}, u32[]{:S(2)}, u32[]{:S(2)}) collective-permute-start(bf16[4,84,16,128]{3,2,1,0:T(8,128)(2,1)} %get-tuple-element.41), channel_id=1, source_target_pairs={{0,32},{32,0},{64,96},{96,64},{128,160},{160,128},{192,224},{224,1... | collective-permute-start | bytes 4128776 | tf_op jit(solution)/shard_map/ppermute | solution.py:437
  101.7 5.8 %collective-permute-start.13 = (bf16[42,16,128]{2,1,0:T(8,128)(2,1)S(1)}, bf16[42,16,128]{2,1,0:T(8,128)(2,1)S(1)}, u32[]{:S(2)}, u32[]{:S(2)}) collective-permute-start(bf16[42,16,128]{2,1,0:T(8,128)(2,1)S(1)} %get-tuple-element.55), channel_id=1, source_target_pairs={{0,192},{32,224},{64,0},{96,32},{128,64},{160,96},{192,128},{224,1... | collective-permute-start | bytes 516104 | tf_op jit(solution)/shard_map/ppermute | solution.py:417
  102.4 6.6 %collective-permute-start.12 = (bf16[42,16,128]{2,1,0:T(8,128)(2,1)S(1)}, bf16[42,16,128]{2,1,0:T(8,128)(2,1)S(1)}, u32[]{:S(2)}, u32[]{:S(2)}) collective-permute-start(bf16[42,16,128]{2,1,0:T(8,128)(2,1)S(1)} %get-tuple-element.56), channel_id=1, source_target_pairs={{0,64},{32,96},{64,128},{96,160},{128,192},{160,224},{192,0},{224,... | collective-permute-start | bytes 516104 | tf_op jit(solution)/shard_map/ppermute | solution.py:417
  104.6 7.3 %collective-permute-start.18 = (bf16[42,16,128]{2,1,0:T(8,128)(2,1)S(1)}, bf16[42,16,128]{2,1,0:T(8,128)(2,1)S(1)}, u32[]{:S(2)}, u32[]{:S(2)}) collective-permute-start(bf16[42,16,128]{2,1,0:T(8,128)(2,1)S(1)} %get-tuple-element.53), channel_id=1, source_target_pairs={{0,192},{32,224},{64,0},{96,32},{128,64},{160,96},{192,128},{224,1... | collective-permute-start | bytes 516104 | tf_op jit(solution)/shard_map/ppermute | solution.py:417
  106.4 6.0 %collective-permute-start.17 = (bf16[42,16,128]{2,1,0:T(8,128)(2,1)S(1)}, bf16[42,16,128]{2,1,0:T(8,128)(2,1)S(1)}, u32[]{:S(2)}, u32[]{:S(2)}) collective-permute-start(bf16[42,16,128]{2,1,0:T(8,128)(2,1)S(1)} %get-tuple-element.54), channel_id=1, source_target_pairs={{0,64},{32,96},{64,128},{96,160},{128,192},{160,224},{192,0},{224,... | collective-permute-start | bytes 516104 | tf_op jit(solution)/shard_map/ppermute | solution.py:417
  109.1 11.5 %collective-permute-start.14 = (bf16[84,16,128]{2,1,0:T(8,128)(2,1)S(1)}, bf16[84,16,128]{2,1,0:T(8,128)(2,1)S(1)}, u32[]{:S(2)}, u32[]{:S(2)}) collective-permute-start(bf16[84,16,128]{2,1,0:T(8,128)(2,1)S(1)} %get-tuple-element.38), channel_id=1, source_target_pairs={{0,64},{32,96},{64,128},{96,160},{128,192},{160,224},{192,0},{224,... | collective-permute-start | bytes 1032200 | tf_op jit(solution)/shard_map/ppermute | solution.py:417
  109.2 11.4 %collective-permute-start.15 = (bf16[84,16,128]{2,1,0:T(8,128)(2,1)S(1)}, bf16[84,16,128]{2,1,0:T(8,128)(2,1)S(1)}, u32[]{:S(2)}, u32[]{:S(2)}) collective-permute-start(bf16[84,16,128]{2,1,0:T(8,128)(2,1)S(1)} %get-tuple-element.39), channel_id=1, source_target_pairs={{0,192},{32,224},{64,0},{96,32},{128,64},{160,96},{192,128},{224,1... | collective-permute-start | bytes 1032200 | tf_op jit(solution)/shard_map/ppermute | solution.py:417
  112.5 15.4 %collective-permute-start.19 = (bf16[84,16,128]{2,1,0:T(8,128)(2,1)S(1)}, bf16[84,16,128]{2,1,0:T(8,128)(2,1)S(1)}, u32[]{:S(2)}, u32[]{:S(2)}) collective-permute-start(bf16[84,16,128]{2,1,0:T(8,128)(2,1)S(1)} %get-tuple-element.46), channel_id=1, source_target_pairs={{0,64},{32,96},{64,128},{96,160},{128,192},{160,224},{192,0},{224,... | collective-permute-start | bytes 1032200 | tf_op jit(solution)/shard_map/ppermute | solution.py:417
  112.8 15.2 %collective-permute-start.20 = (bf16[84,16,128]{2,1,0:T(8,128)(2,1)S(1)}, bf16[84,16,128]{2,1,0:T(8,128)(2,1)S(1)}, u32[]{:S(2)}, u32[]{:S(2)}) collective-permute-start(bf16[84,16,128]{2,1,0:T(8,128)(2,1)S(1)} %get-tuple-element.47), channel_id=1, source_target_pairs={{0,192},{32,224},{64,0},{96,32},{128,64},{160,96},{192,128},{224,1... | collective-permute-start | bytes 1032200 | tf_op jit(solution)/shard_map/ppermute | solution.py:417
  129.8 30.2 %all-to-all-start.1 = ((bf16[32,6,16,128]{3,2,1,0:T(8,128)(2,1)}), bf16[32,6,16,128]{3,2,1,0:T(8,128)(2,1)S(1)}, u32[]{:S(2)}, u32[]{:S(2)}) async-start(bf16[32,6,16,128]{3,2,1,0:T(8,128)(2,1)} %bitcast.15), calls=%async_computation.1 | async-start | bytes 1572864 | tf_op jit(solution)/shard_map/all_to_all | solution.py:345
  140.5 41.5 %reduce-scatter.5.cloned.1.call-start = ((), (), s32[]{:S(2)}) async-start(), calls=%async_computation.5 | async-start | bytes 589824 | tf_op jit(solution)/shard_map/reduce_scatter | solution.py:485
  161.2 6.9 %collective-permute-start.26 = (bf16[84,16,128]{2,1,0:T(8,128)(2,1)S(1)}, bf16[84,16,128]{2,1,0:T(8,128)(2,1)S(1)}, u32[]{:S(2)}, u32[]{:S(2)}) collective-permute-start(bf16[84,16,128]{2,1,0:T(8,128)(2,1)S(1)} %bitcast.25), channel_id=1, source_target_pairs={{0,192},{32,224},{64,0},{96,32},{128,64},{160,96},{192,128},{224,1... | collective-permute-start | bytes 1032200 | tf_op jit(solution)/shard_map/ppermute | solution.py:417
  161.3 14.2 %collective-permute-start.24 = (bf16[84,16,128]{2,1,0:T(8,128)(2,1)S(1)}, bf16[84,16,128]{2,1,0:T(8,128)(2,1)S(1)}, u32[]{:S(2)}, u32[]{:S(2)}) collective-permute-start(bf16[84,16,128]{2,1,0:T(8,128)(2,1)S(1)} %bitcast.26), channel_id=1, source_target_pairs={{0,128},{32,160},{64,192},{96,224},{128,0},{160,32},{192,64},{224,... | collective-permute-start | bytes 1032200 | tf_op jit(solution)/shard_map/ppermute | solution.py:417
  162.9 14.9 %collective-permute-start.22 = (bf16[84,16,128]{2,1,0:T(8,128)(2,1)S(1)}, bf16[84,16,128]{2,1,0:T(8,128)(2,1)S(1)}, u32[]{:S(2)}, u32[]{:S(2)}) collective-permute-start(bf16[84,16,128]{2,1,0:T(8,128)(2,1)S(1)} %bitcast.27), channel_id=1, source_target_pairs={{0,64},{32,96},{64,128},{96,160},{128,192},{160,224},{192,0},{224,... | collective-permute-start | bytes 1032200 | tf_op jit(solution)/shard_map/ppermute | solution.py:417
  162.9 17.8 %collective-permute-start.21 = (bf16[84,16,128]{2,1,0:T(8,128)(2,1)S(1)}, bf16[84,16,128]{2,1,0:T(8,128)(2,1)S(1)}, u32[]{:S(2)}, u32[]{:S(2)}) collective-permute-start(bf16[84,16,128]{2,1,0:T(8,128)(2,1)S(1)} %bitcast.28), channel_id=1, source_target_pairs={{0,32},{32,0},{64,96},{96,64},{128,160},{160,128},{192,224},{224,1... | collective-permute-start | bytes 1032200 | tf_op jit(solution)/shard_map/ppermute | solution.py:437
  168.1 12.6 %collective-permute-start.27 = (bf16[84,16,128]{2,1,0:T(8,128)(2,1)S(1)}, bf16[84,16,128]{2,1,0:T(8,128)(2,1)S(1)}, u32[]{:S(2)}, u32[]{:S(2)}) collective-permute-start(bf16[84,16,128]{2,1,0:T(8,128)(2,1)S(1)} %collective-permute-done.26.refs_6_), channel_id=1, source_target_pairs={{0,32},{32,0},{64,96},{96,64},{128,160},{160,128},{192,224},{224,1... | collective-permute-start | bytes 1032200 | tf_op jit(solution)/shard_map/ppermute | solution.py:437
  175.4 5.3 %collective-permute-start.25 = (bf16[84,16,128]{2,1,0:T(8,128)(2,1)S(1)}, bf16[84,16,128]{2,1,0:T(8,128)(2,1)S(1)}, u32[]{:S(2)}, u32[]{:S(2)}) collective-permute-start(bf16[84,16,128]{2,1,0:T(8,128)(2,1)S(1)} %collective-permute-done.24.refs_4_), channel_id=1, source_target_pairs={{0,32},{32,0},{64,96},{96,64},{128,160},{160,128},{192,224},{224,1... | collective-permute-start | bytes 1032200 | tf_op jit(solution)/shard_map/ppermute | solution.py:437
  177.7 4.3 %collective-permute-start.23 = (bf16[84,16,128]{2,1,0:T(8,128)(2,1)S(1)}, bf16[84,16,128]{2,1,0:T(8,128)(2,1)S(1)}, u32[]{:S(2)}, u32[]{:S(2)}) collective-permute-start(bf16[84,16,128]{2,1,0:T(8,128)(2,1)S(1)} %collective-permute-done.22.refs_2_), channel_id=1, source_target_pairs={{0,32},{32,0},{64,96},{96,64},{128,160},{160,128},{192,224},{224,1... | collective-permute-start | bytes 1032200 | tf_op jit(solution)/shard_map/ppermute | solution.py:437
  (20 other events, 430.6 us)
Sparse Core Ops, SparseCore 0:
  43.8 41.3 all-gather.2
  97.2 32.9 reduce-scatter.2
  144.0 34.9 reduce-scatter.4

commit v8 on v7

--- a/solution.py
+++ b/solution.py
@@ -479,7 +479,8 @@
         name="own_slots",
     )(where, tile_cols, exchange(returning))
     own = own.reshape(2 * owned, part, BLOCK)
-    far, near, back = (around(own, s) for s in (2, 1, 3))
+    near, back = around(own, 1), around(own, 3)
+    far = jnp.concatenate([around(near[:owned], 1), around(back[owned:], 3)], axis=0)
     full = [own, near, far, back]
     full = [v for t in full for v in (t, swap(t))]
     input_grad = lax.psum_scatter(

time: 193 us -> 208 us (1.078); the launches traced: 193 us -> 203 us
  blocking collectives: 0 us -> 28.1 us
  starting transfers between devices: 63.4 us -> 50.4 us
  waiting for transfers between devices: 82.3 us -> 77.4 us
    all_to_all x0 -> x1, blocking collectives: none -> 28.1 us  [exchange(): lax.all_to_all(values.reshape(shape), 'mp', 0, 0).reshape(values.shape)]
    all_to_all x2 -> x1, waiting for transfers between devices: 29.5 us -> 10.7 us  [exchange(): lax.all_to_all(values.reshape(shape), 'mp', 0, 0).reshape(values.shape)]
    all_to_all x2 -> x1, starting transfers between devices: 22.7 us -> 12 us  [exchange(): lax.all_to_all(values.reshape(shape), 'mp', 0, 0).reshape(values.shape)]
    reduce_scatter x1, waiting for transfers between devices: 0.01 us -> 10.6 us  [per_device(): lax.psum_scatter(row_terms, 'mp', scatter_dimension=0, axis_index_groups=...]
    ppermute x6, starting transfers between devices: 17.9 us -> 11.6 us  [swap(): return lax.ppermute(value, 'dp', [(d, d ^ 1) for d in range(groups)])]
    ppermute x11 -> x12, starting transfers between devices: 10.6 us -> 14.5 us  [around(): return lax.ppermute(value, 'dp', pairs)]
    ppermute x11 -> x12, waiting for transfers between devices: 16.4 us -> 20.3 us  [around(): return lax.ppermute(value, 'dp', pairs)]
  transfers between devices with their start and end apart: 33 -> 33, of which waited for: 18 -> 18; matrix products, arithmetic and copies ran while one was open for 3% -> 3% of each run, Pallas kernels for 3% -> 2%
where the time goes in v8:
time: 208 us; the launch traced here: 203 us
  waiting for transfers between devices  77.4 us (37%)
  starting transfers between devices  50.4 us (24%)
  blocking collectives  28.1 us (14%)
  Pallas kernels  26.4 us (13%)
  between operations  14.2 us (7%)
  other arithmetic  4.38 us (2%)
  local copies, waits for them, and re-layouts  2.6 us (1%)
    all_to_all x1, blocking collectives, exchange(): lax.all_to_all(values.reshape(shape), 'mp', 0, 0).reshape(values.shape)  28.1 us
    ppermute x8, waiting for transfers between devices, along(): return lax.ppermute(value, 'mp', pairs)  20.5 us
    ppermute x12, waiting for transfers between devices, around(): return lax.ppermute(value, 'dp', pairs)  20.3 us
    ppermute x12, starting transfers between devices, around(): return lax.ppermute(value, 'dp', pairs)  14.5 us
    pallas_call x1, Pallas kernels, per_device(): pl.pallas_call(lambda *refs: main_kernel(sides, ring, panels, *refs), out...  13.1 us
    all_to_all x1, starting transfers between devices, exchange(): lax.all_to_all(values.reshape(shape), 'mp', 0, 0).reshape(values.shape)  12 us
    ppermute x6, starting transfers between devices, swap(): return lax.ppermute(value, 'dp', [(d, d ^ 1) for d in range(groups)])  11.6 us
    all_gather x1, waiting for transfers between devices, per_device(): held = lax.all_gather(ordered, 'dp')  11.2 us
  transfers between devices with their start and end apart: 33, of which 18 were waited for; matrix products, arithmetic and copies ran while one was open for 3% of the time, Pallas kernels for 2%

profile of v8, /device:TPU:1, one launch (start us, length us, event | category | flops | bytes accessed | tf_op | source)
XLA Modules:
  0.0 203.5 jit_solution(9509854489342262728)
XLA Ops:
  7.2 3.2 %send_pack.1 = (bf16[192,16,128]{2,1,0:T(8,128)(2,1)}, bf16[2,128,128]{2,1,0:T(8,128)(2,1)}) custom-call(s32[2,1344]{1,0:T(2,128)} %refs_1_.3, bf16[2,42,128,128]{3,2,1,0:T(8,128)(2,1)} %refs_1_.2, bf16[128,256]{1,0:T(8,128)(2,1)} %refs_2_.1), custom_call_target="tpu_custom_call" | custom-call | tf_op jit(solution)/shard_map/send_pack/pallas_call | solution.py:324
  10.4 12.0 %all-to-all-start = ((bf16[32,6,16,128]{3,2,1,0:T(8,128)(2,1)}), bf16[32,6,16,128]{3,2,1,0:T(8,128)(2,1)S(1)}, u32[]{:S(2)}, u32[]{:S(2)}) async-start(bf16[32,6,16,128]{3,2,1,0:T(8,128)(2,1)} %bitcast.33), calls=%async_computation | async-start | bytes 1572864 | tf_op jit(solution)/shard_map/all_to_all | solution.py:345
  22.5 2.6 %collective-permute-start.2 = (bf16[2,128,128]{2,1,0:T(8,128)(2,1)}, bf16[2,128,128]{2,1,0:T(8,128)(2,1)S(1)}, u32[]{:S(2)}, u32[]{:S(2)}) collective-permute-start(bf16[2,128,128]{2,1,0:T(8,128)(2,1)} %get-tuple-element.28), channel_id=1, source_target_pairs={{0,24},{1,25},{2,26},{3,27},{4,28},{5,29},{6,30},{7,31},{8,0},{9,1... | collective-permute-start | bytes 196616 | tf_op jit(solution)/shard_map/ppermute | solution.py:353
  27.6 3.2 %select_reduce_fusion = s32[7,2,12]{2,1,0:T(2,128)S(1)} fusion(s32[2,32,42]{2,1,0:T(8,128)S(1)} %get-tuple-element.58, s32[7,2,32,42]{3,2,1,0:T(8,128)S(1)} %add_select_fusion), kind=kLoop, calls=%fused_computation | loop fusion | flops 677208 | bytes 86688 | tf_op jit(solution)/shard_map/reduce_sum | solution.py:46
  31.0 10.7 %all-to-all-done = bf16[32,6,16,128]{3,2,1,0:T(8,128)(2,1)S(1)} async-done(((bf16[32,6,16,128]{3,2,1,0:T(8,128)(2,1)}), bf16[32,6,16,128]{3,2,1,0:T(8,128)(2,1)S(1)}, u32[]{:S(2)}, u32[]{:S(2)}) %all-to-all-start) | async-done | bytes 786464 | tf_op jit(solution)/shard_map/all_to_all | solution.py:345
  41.7 2.0 sort_slots.1
  43.7 2.1 %collective-permute-start.6 = (bf16[4,2,128,128]{3,2,1,0:T(8,128)(2,1)S(1)}, bf16[4,2,128,128]{3,2,1,0:T(8,128)(2,1)S(1)}, u32[]{:S(2)}, u32[]{:S(2)}) collective-permute-start(bf16[4,2,128,128]{3,2,1,0:T(8,128)(2,1)S(1)} %pad_maximum_fusion.refs_3_), channel_id=1, source_target_pairs={{0,7},{1,0},{2,1},{3,2},{4,3},{5,4},{6,5},{7,6},{8,15},{9,8},{10,9... | collective-permute-start | bytes 786440 | tf_op jit(solution)/shard_map/ppermute | solution.py:359
  45.8 1.5 collective-permute-start.3
  47.3 3.7 %collective-permute-done.6.refs_9_ = bf16[4,2,128,128]{3,2,1,0:T(8,128)(2,1)S(1)} collective-permute-done((bf16[4,2,128,128]{3,2,1,0:T(8,128)(2,1)S(1)}, bf16[4,2,128,128]{3,2,1,0:T(8,128)(2,1)S(1)}, u32[]{:S(2)}, u32[]{:S(2)}) %collective-permute-start.6) | collective-permute-done | bytes 262176 | tf_op jit(solution)/shard_map/ppermute | solution.py:359
  52.6 4.8 %collective-permute-done.7.refs_8_ = bf16[4,2,128,128]{3,2,1,0:T(8,128)(2,1)S(1)} collective-permute-done((bf16[4,2,128,128]{3,2,1,0:T(8,128)(2,1)S(1)}, bf16[4,2,128,128]{3,2,1,0:T(8,128)(2,1)S(1)}, u32[]{:S(2)}, u32[]{:S(2)}) %collective-permute-start.7) | collective-permute-done | bytes 262176 | tf_op jit(solution)/shard_map/ppermute | solution.py:359
  57.4 1.3 collective-permute-start.8
  59.1 6.1 %collective-permute-done.8.refs_7_ = bf16[4,2,128,128]{3,2,1,0:T(8,128)(2,1)S(1)} collective-permute-done((bf16[4,2,128,128]{3,2,1,0:T(8,128)(2,1)S(1)}, bf16[4,2,128,128]{3,2,1,0:T(8,128)(2,1)S(1)}, u32[]{:S(2)}, u32[]{:S(2)}) %collective-permute-start.8) | collective-permute-done | bytes 262176 | tf_op jit(solution)/shard_map/ppermute | solution.py:359
  65.2 1.7 collective-permute-start.10
  68.5 2.6 %collective-permute-done.10.refs_11_ = bf16[2,2,128,128]{3,2,1,0:T(8,128)(2,1)S(1)} collective-permute-done((bf16[2,2,128,128]{3,2,1,0:T(8,128)(2,1)S(1)}, bf16[2,2,128,128]{3,2,1,0:T(8,128)(2,1)S(1)}, u32[]{:S(2)}, u32[]{:S(2)}) %collective-permute-start.10) | collective-permute-done | bytes 131104 | tf_op jit(solution)/shard_map/ppermute | solution.py:359
  71.1 2.9 %collective-permute-done.9.refs_10_ = bf16[2,2,128,128]{3,2,1,0:T(8,128)(2,1)S(1)} collective-permute-done((bf16[2,2,128,128]{3,2,1,0:T(8,128)(2,1)S(1)}, bf16[2,2,128,128]{3,2,1,0:T(8,128)(2,1)S(1)}, u32[]{:S(2)}, u32[]{:S(2)}) %collective-permute-start.9) | collective-permute-done | bytes 131104 | tf_op jit(solution)/shard_map/ppermute | solution.py:359
  74.0 11.2 %all-gather.3.cloned.1.call-done = bf16[1344,16,128]{2,1,0:T(8,128)(2,1)} async-done(((bf16[168,16,128]{2,1,0:T(8,128)(2,1)}), bf16[1344,16,128]{2,1,0:T(8,128)(2,1)}) %all-gather.3.cloned.1.call-update) | async-done | bytes 5505040 | tf_op jit(solution)/shard_map/all_gather | solution.py:376
  85.3 13.1 %gated_pair.1 = (bf16[128,896]{1,0:T(8,128)(2,1)}, bf16[4,84,16,128]{3,2,1,0:T(8,128)(2,1)}, bf16[4,84,16,128]{3,2,1,0:T(8,128)(2,1)}, bf16[4,84,16,128]{3,2,1,0...) custom-call(s32[168]{0:T(256)} %copy-done.5, s32[14]{0:T(128)} %reshape.58.refs_1_.count_ref, ...), custom_call_target="tpu_custom_call" | custom-call | tf_op jit(solution)/shard_map/gated_pair/pallas_call | solution.py:386
  99.1 2.8 %collective-permute-done.11.other_ref = bf16[4,84,16,128]{3,2,1,0:T(8,128)(2,1)S(1)} collective-permute-done((bf16[4,84,16,128]{3,2,1,0:T(8,128)(2,1)}, bf16[4,84,16,128]{3,2,1,0:T(8,128)(2,1)S(1)}, u32[]{:S(2)}, u32[]{:S(2)}) %collective-permute-start.11) | collective-permute-done | bytes 1376288 | tf_op jit(solution)/shard_map/ppermute | solution.py:437
  106.1 1.8 collective-permute-start.18
  109.0 1.5 collective-permute-done.12.first_ref
  110.7 2.7 %collective-permute-start.15 = (bf16[84,16,128]{2,1,0:T(8,128)(2,1)S(1)}, bf16[84,16,128]{2,1,0:T(8,128)(2,1)S(1)}, u32[]{:S(2)}, u32[]{:S(2)}) collective-permute-start(bf16[84,16,128]{2,1,0:T(8,128)(2,1)S(1)} %get-tuple-element.39), channel_id=1, source_target_pairs={{0,192},{32,224},{64,0},{96,32},{128,64},{160,96},{192,128},{224,1... | collective-permute-start | bytes 1032200 | tf_op jit(solution)/shard_map/ppermute | solution.py:417
  114.4 2.5 %collective-permute-start.20 = (bf16[84,16,128]{2,1,0:T(8,128)(2,1)S(1)}, bf16[84,16,128]{2,1,0:T(8,128)(2,1)S(1)}, u32[]{:S(2)}, u32[]{:S(2)}) collective-permute-start(bf16[84,16,128]{2,1,0:T(8,128)(2,1)S(1)} %get-tuple-element.47), channel_id=1, source_target_pairs={{0,192},{32,224},{64,0},{96,32},{128,64},{160,96},{192,128},{224,1... | collective-permute-start | bytes 1032200 | tf_op jit(solution)/shard_map/ppermute | solution.py:417
  116.9 5.2 %collective-permute-done.14.refs_1_ = bf16[84,16,128]{2,1,0:T(8,128)(2,1)S(1)} collective-permute-done((bf16[84,16,128]{2,1,0:T(8,128)(2,1)S(1)}, bf16[84,16,128]{2,1,0:T(8,128)(2,1)S(1)}, u32[]{:S(2)}, u32[]{:S(2)}) %collective-permute-start.14) | collective-permute-done | bytes 344096 | tf_op jit(solution)/shard_map/ppermute | solution.py:417
  122.1 7.3 %collective-permute-done.19.refs_4_ = bf16[84,16,128]{2,1,0:T(8,128)(2,1)S(1)} collective-permute-done((bf16[84,16,128]{2,1,0:T(8,128)(2,1)S(1)}, bf16[84,16,128]{2,1,0:T(8,128)(2,1)S(1)}, u32[]{:S(2)}, u32[]{:S(2)}) %collective-permute-start.19) | collective-permute-done | bytes 344096 | tf_op jit(solution)/shard_map/ppermute | solution.py:417
  130.5 28.1 %all_to_all.10 = bf16[32,6,16,128]{3,2,1,0:T(8,128)(2,1)S(1)} all-to-all(bf16[32,6,16,128]{3,2,1,0:T(8,128)(2,1)S(1)} %bitcast.25), channel_id=1, replica_groups=mesh['dp'=8,'mp'=32] {'mp'}, dimensions={0} | all-to-all | bytes 1572864 | tf_op jit(solution)/shard_map/all_to_all | solution.py:345
  159.9 2.7 %collective-permute-start.25 = (bf16[84,16,128]{2,1,0:T(8,128)(2,1)S(1)}, bf16[84,16,128]{2,1,0:T(8,128)(2,1)S(1)}, u32[]{:S(2)}, u32[]{:S(2)}) collective-permute-start(bf16[84,16,128]{2,1,0:T(8,128)(2,1)S(1)} %bitcast.27), channel_id=1, source_target_pairs={{0,192},{32,224},{64,0},{96,32},{128,64},{160,96},{192,128},{224,1... | collective-permute-start | bytes 1032200 | tf_op jit(solution)/shard_map/ppermute | solution.py:417
  162.6 4.5 %collective-permute-done.22.refs_2_ = bf16[84,16,128]{2,1,0:T(8,128)(2,1)S(1)} collective-permute-done((bf16[84,16,128]{2,1,0:T(8,128)(2,1)S(1)}, bf16[84,16,128]{2,1,0:T(8,128)(2,1)S(1)}, u32[]{:S(2)}, u32[]{:S(2)}) %collective-permute-start.22) | collective-permute-done | bytes 344096 | tf_op jit(solution)/shard_map/ppermute | solution.py:417
  167.3 2.7 %collective-permute-start.26 = (bf16[42,16,128]{2,1,0:T(8,128)(2,1)S(1)}, bf16[42,16,128]{2,1,0:T(8,128)(2,1)S(1)}, u32[]{:S(2)}, u32[]{:S(2)}) collective-permute-start(bf16[42,16,128]{2,1,0:T(8,128)(2,1)S(1)} %slice.55), channel_id=1, source_target_pairs={{0,192},{32,224},{64,0},{96,32},{128,64},{160,96},{192,128},{224,1... | collective-permute-start | bytes 516104 | tf_op jit(solution)/shard_map/ppermute | solution.py:417
  170.0 7.9 %collective-permute-start.21 = (bf16[84,16,128]{2,1,0:T(8,128)(2,1)S(1)}, bf16[84,16,128]{2,1,0:T(8,128)(2,1)S(1)}, u32[]{:S(2)}, u32[]{:S(2)}) collective-permute-start(bf16[84,16,128]{2,1,0:T(8,128)(2,1)S(1)} %bitcast.28), channel_id=1, source_target_pairs={{0,32},{32,0},{64,96},{96,64},{128,160},{160,128},{192,224},{224,1... | collective-permute-start | bytes 1032200 | tf_op jit(solution)/shard_map/ppermute | solution.py:437
  178.5 2.6 %collective-permute-start.27 = (bf16[84,16,128]{2,1,0:T(8,128)(2,1)S(1)}, bf16[84,16,128]{2,1,0:T(8,128)(2,1)S(1)}, u32[]{:S(2)}, u32[]{:S(2)}) collective-permute-start(bf16[84,16,128]{2,1,0:T(8,128)(2,1)S(1)} %constant_dynamic-update-slice_fusion.refs_4_), channel_id=1, source_target_pairs={{0,32},{32,0},{64,96},{96,64},{128,160},{160,128},{192,224},{224,1... | collective-permute-start | bytes 1032200 | tf_op jit(solution)/shard_map/ppermute | solution.py:437
  182.4 10.6 %reduce-scatter.5.cloned.1.call-done.refs_8_ = bf16[2,128,128]{2,1,0:T(8,128)(2,1)} async-done(((bf16[16,128,128]{2,1,0:T(8,128)(2,1)}), bf16[2,128,128]{2,1,0:T(8,128)(2,1)}) %reduce-scatter.5.cloned.1.call-update) | async-done | bytes 65552 | tf_op jit(solution)/shard_map/reduce_scatter | solution.py:486
  193.8 3.1 %widen.1 = (f32[84,128,128]{2,1,0:T(8,128)}, bf16[128,256]{1,0:T(8,128)(2,1)}) custom-call(s32[6]{0:T(128)S(1)} %copy-done.4, bf16[84,16,128]{2,1,0:T(8,128)(2,1)S(1)} %bitcast.29, bf16[84,16,128]{2,1,0:T(8,128)(2,1)S(1)} %collective-permute-done.21.refs_1_, bf16[84,16,128]{2,1,0:T(8,128)(2,1)S(1)} %collective-permute-done.22.refs_2_, ...), custom_call_target="tpu_custom_call" | custom-call | tf_op jit(solution)/shard_map/widen/pallas_call | solution.py:489
  (110 shorter events, 18.7 us)
Async XLA Ops:
  10.4 31.3 %all-to-all-start = ((bf16[32,6,16,128]{3,2,1,0:T(8,128)(2,1)}), bf16[32,6,16,128]{3,2,1,0:T(8,128)(2,1)S(1)}, u32[]{:S(2)}, u32[]{:S(2)}) async-start(bf16[32,6,16,128]{3,2,1,0:T(8,128)(2,1)} %bitcast.33), calls=%async_computation | async-start | bytes 1572864 | tf_op jit(solution)/shard_map/all_to_all | solution.py:345
  22.4 62.8 %all-gather.3.cloned.1.call-start = ((), (), s32[]{:S(2)}) async-start(), calls=%async_computation.6 | async-start | bytes 6193152 | tf_op jit(solution)/shard_map/all_gather | solution.py:376
  22.5 8.4 %collective-permute-start.2 = (bf16[2,128,128]{2,1,0:T(8,128)(2,1)}, bf16[2,128,128]{2,1,0:T(8,128)(2,1)S(1)}, u32[]{:S(2)}, u32[]{:S(2)}) collective-permute-start(bf16[2,128,128]{2,1,0:T(8,128)(2,1)} %get-tuple-element.28), channel_id=1, source_target_pairs={{0,24},{1,25},{2,26},{3,27},{4,28},{5,29},{6,30},{7,31},{8,0},{9,1... | collective-permute-start | bytes 196616 | tf_op jit(solution)/shard_map/ppermute | solution.py:353
  25.0 5.9 %collective-permute-start.1 = (bf16[2,128,128]{2,1,0:T(8,128)(2,1)}, bf16[2,128,128]{2,1,0:T(8,128)(2,1)S(1)}, u32[]{:S(2)}, u32[]{:S(2)}) collective-permute-start(bf16[2,128,128]{2,1,0:T(8,128)(2,1)} %get-tuple-element.28), channel_id=1, source_target_pairs={{0,16},{1,17},{2,18},{3,19},{4,20},{5,21},{6,22},{7,23},{8,24},{9,... | collective-permute-start | bytes 196616 | tf_op jit(solution)/shard_map/ppermute | solution.py:353
  25.6 5.4 %collective-permute-start = (bf16[2,128,128]{2,1,0:T(8,128)(2,1)}, bf16[2,128,128]{2,1,0:T(8,128)(2,1)S(1)}, u32[]{:S(2)}, u32[]{:S(2)}) collective-permute-start(bf16[2,128,128]{2,1,0:T(8,128)(2,1)} %get-tuple-element.28), channel_id=1, source_target_pairs={{0,8},{1,9},{2,10},{3,11},{4,12},{5,13},{6,14},{7,15},{8,16},{9,17... | collective-permute-start | bytes 196616 | tf_op jit(solution)/shard_map/ppermute | solution.py:353
  43.7 116.2 %reduce-scatter.3.cloned.1.call-start = ((), (), s32[]{:S(2)}) async-start(), calls=%async_computation.4 | async-start | bytes 2621440 | tf_op jit(solution)/shard_map/reduce_scatter | solution.py:454
  43.7 7.3 %collective-permute-start.6 = (bf16[4,2,128,128]{3,2,1,0:T(8,128)(2,1)S(1)}, bf16[4,2,128,128]{3,2,1,0:T(8,128)(2,1)S(1)}, u32[]{:S(2)}, u32[]{:S(2)}) collective-permute-start(bf16[4,2,128,128]{3,2,1,0:T(8,128)(2,1)S(1)} %pad_maximum_fusion.refs_3_), channel_id=1, source_target_pairs={{0,7},{1,0},{2,1},{3,2},{4,3},{5,4},{6,5},{7,6},{8,15},{9,8},{10,9... | collective-permute-start | bytes 786440 | tf_op jit(solution)/shard_map/ppermute | solution.py:359
  45.8 6.4 %collective-permute-start.3 = (bf16[4,2,128,128]{3,2,1,0:T(8,128)(2,1)S(1)}, bf16[4,2,128,128]{3,2,1,0:T(8,128)(2,1)S(1)}, u32[]{:S(2)}, u32[]{:S(2)}) collective-permute-start(bf16[4,2,128,128]{3,2,1,0:T(8,128)(2,1)S(1)} %pad_maximum_fusion.refs_3_), channel_id=1, source_target_pairs={{0,1},{1,2},{2,3},{3,4},{4,5},{5,6},{6,7},{7,0},{8,9},{9,10},{10,1... | collective-permute-start | bytes 786440 | tf_op jit(solution)/shard_map/ppermute | solution.py:359
  51.0 6.4 %collective-permute-start.7 = (bf16[4,2,128,128]{3,2,1,0:T(8,128)(2,1)S(1)}, bf16[4,2,128,128]{3,2,1,0:T(8,128)(2,1)S(1)}, u32[]{:S(2)}, u32[]{:S(2)}) collective-permute-start(bf16[4,2,128,128]{3,2,1,0:T(8,128)(2,1)S(1)} %collective-permute-done.6.refs_9_), channel_id=1, source_target_pairs={{0,7},{1,0},{2,1},{3,2},{4,3},{5,4},{6,5},{7,6},{8,15},{9,8},{10,9... | collective-permute-start | bytes 786440 | tf_op jit(solution)/shard_map/ppermute | solution.py:359
  52.3 6.7 %collective-permute-start.4 = (bf16[4,2,128,128]{3,2,1,0:T(8,128)(2,1)S(1)}, bf16[4,2,128,128]{3,2,1,0:T(8,128)(2,1)S(1)}, u32[]{:S(2)}, u32[]{:S(2)}) collective-permute-start(bf16[4,2,128,128]{3,2,1,0:T(8,128)(2,1)S(1)} %collective-permute-done.3.refs_4_), channel_id=1, source_target_pairs={{0,1},{1,2},{2,3},{3,4},{4,5},{5,6},{6,7},{7,0},{8,9},{9,10},{10,1... | collective-permute-start | bytes 786440 | tf_op jit(solution)/shard_map/ppermute | solution.py:359
  57.4 7.8 %collective-permute-start.8 = (bf16[4,2,128,128]{3,2,1,0:T(8,128)(2,1)S(1)}, bf16[4,2,128,128]{3,2,1,0:T(8,128)(2,1)S(1)}, u32[]{:S(2)}, u32[]{:S(2)}) collective-permute-start(bf16[4,2,128,128]{3,2,1,0:T(8,128)(2,1)S(1)} %collective-permute-done.7.refs_8_), channel_id=1, source_target_pairs={{0,7},{1,0},{2,1},{3,2},{4,3},{5,4},{6,5},{7,6},{8,15},{9,8},{10,9... | collective-permute-start | bytes 786440 | tf_op jit(solution)/shard_map/ppermute | solution.py:359
  59.0 8.2 %collective-permute-start.5 = (bf16[4,2,128,128]{3,2,1,0:T(8,128)(2,1)S(1)}, bf16[4,2,128,128]{3,2,1,0:T(8,128)(2,1)S(1)}, u32[]{:S(2)}, u32[]{:S(2)}) collective-permute-start(bf16[4,2,128,128]{3,2,1,0:T(8,128)(2,1)S(1)} %collective-permute-done.4.refs_5_), channel_id=1, source_target_pairs={{0,1},{1,2},{2,3},{3,4},{4,5},{5,6},{6,7},{7,0},{8,9},{9,10},{10,1... | collective-permute-start | bytes 786440 | tf_op jit(solution)/shard_map/ppermute | solution.py:359
  65.2 5.9 %collective-permute-start.10 = (bf16[2,2,128,128]{3,2,1,0:T(8,128)(2,1)S(1)}, bf16[2,2,128,128]{3,2,1,0:T(8,128)(2,1)S(1)}, u32[]{:S(2)}, u32[]{:S(2)}) collective-permute-start(bf16[2,2,128,128]{3,2,1,0:T(8,128)(2,1)S(1)} %slice.53), channel_id=1, source_target_pairs={{0,7},{1,0},{2,1},{3,2},{4,3},{5,4},{6,5},{7,6},{8,15},{9,8},{10,9... | collective-permute-start | bytes 393224 | tf_op jit(solution)/shard_map/ppermute | solution.py:359
  67.1 6.9 %collective-permute-start.9 = (bf16[2,2,128,128]{3,2,1,0:T(8,128)(2,1)S(1)}, bf16[2,2,128,128]{3,2,1,0:T(8,128)(2,1)S(1)}, u32[]{:S(2)}, u32[]{:S(2)}) collective-permute-start(bf16[2,2,128,128]{3,2,1,0:T(8,128)(2,1)S(1)} %slice.52), channel_id=1, source_target_pairs={{0,1},{1,2},{2,3},{3,4},{4,5},{5,6},{6,7},{7,0},{8,9},{9,10},{10,1... | collective-permute-start | bytes 393224 | tf_op jit(solution)/shard_map/ppermute | solution.py:359
  98.5 94.5 %reduce-scatter.5.cloned.1.call-start = ((), (), s32[]{:S(2)}) async-start(), calls=%async_computation.5 | async-start | bytes 589824 | tf_op jit(solution)/shard_map/reduce_scatter | solution.py:486
  98.5 3.4 %collective-permute-start.11 = (bf16[4,84,16,128]{3,2,1,0:T(8,128)(2,1)}, bf16[4,84,16,128]{3,2,1,0:T(8,128)(2,1)S(1)}, u32[]{:S(2)}, u32[]{:S(2)}) collective-permute-start(bf16[4,84,16,128]{3,2,1,0:T(8,128)(2,1)} %get-tuple-element.33), channel_id=1, source_target_pairs={{0,32},{32,0},{64,96},{96,64},{128,160},{160,128},{192,224},{224,1... | collective-permute-start | bytes 4128776 | tf_op jit(solution)/shard_map/ppermute | solution.py:437
  98.9 5.9 %collective-permute-start.16 = (bf16[4,84,16,128]{3,2,1,0:T(8,128)(2,1)}, bf16[4,84,16,128]{3,2,1,0:T(8,128)(2,1)S(1)}, u32[]{:S(2)}, u32[]{:S(2)}) collective-permute-start(bf16[4,84,16,128]{3,2,1,0:T(8,128)(2,1)} %get-tuple-element.41), channel_id=1, source_target_pairs={{0,32},{32,0},{64,96},{96,64},{128,160},{160,128},{192,224},{224,1... | collective-permute-start | bytes 4128776 | tf_op jit(solution)/shard_map/ppermute | solution.py:437
  103.2 5.8 %collective-permute-start.13 = (bf16[42,16,128]{2,1,0:T(8,128)(2,1)S(1)}, bf16[42,16,128]{2,1,0:T(8,128)(2,1)S(1)}, u32[]{:S(2)}, u32[]{:S(2)}) collective-permute-start(bf16[42,16,128]{2,1,0:T(8,128)(2,1)S(1)} %get-tuple-element.55), channel_id=1, source_target_pairs={{0,192},{32,224},{64,0},{96,32},{128,64},{160,96},{192,128},{224,1... | collective-permute-start | bytes 516104 | tf_op jit(solution)/shard_map/ppermute | solution.py:417
  103.9 6.6 %collective-permute-start.12 = (bf16[42,16,128]{2,1,0:T(8,128)(2,1)S(1)}, bf16[42,16,128]{2,1,0:T(8,128)(2,1)S(1)}, u32[]{:S(2)}, u32[]{:S(2)}) collective-permute-start(bf16[42,16,128]{2,1,0:T(8,128)(2,1)S(1)} %get-tuple-element.56), channel_id=1, source_target_pairs={{0,64},{32,96},{64,128},{96,160},{128,192},{160,224},{192,0},{224,... | collective-permute-start | bytes 516104 | tf_op jit(solution)/shard_map/ppermute | solution.py:417
  106.1 7.3 %collective-permute-start.18 = (bf16[42,16,128]{2,1,0:T(8,128)(2,1)S(1)}, bf16[42,16,128]{2,1,0:T(8,128)(2,1)S(1)}, u32[]{:S(2)}, u32[]{:S(2)}) collective-permute-start(bf16[42,16,128]{2,1,0:T(8,128)(2,1)S(1)} %get-tuple-element.53), channel_id=1, source_target_pairs={{0,192},{32,224},{64,0},{96,32},{128,64},{160,96},{192,128},{224,1... | collective-permute-start | bytes 516104 | tf_op jit(solution)/shard_map/ppermute | solution.py:417
  107.9 6.1 %collective-permute-start.17 = (bf16[42,16,128]{2,1,0:T(8,128)(2,1)S(1)}, bf16[42,16,128]{2,1,0:T(8,128)(2,1)S(1)}, u32[]{:S(2)}, u32[]{:S(2)}) collective-permute-start(bf16[42,16,128]{2,1,0:T(8,128)(2,1)S(1)} %get-tuple-element.54), channel_id=1, source_target_pairs={{0,64},{32,96},{64,128},{96,160},{128,192},{160,224},{192,0},{224,... | collective-permute-start | bytes 516104 | tf_op jit(solution)/shard_map/ppermute | solution.py:417
  110.6 11.5 %collective-permute-start.14 = (bf16[84,16,128]{2,1,0:T(8,128)(2,1)S(1)}, bf16[84,16,128]{2,1,0:T(8,128)(2,1)S(1)}, u32[]{:S(2)}, u32[]{:S(2)}) collective-permute-start(bf16[84,16,128]{2,1,0:T(8,128)(2,1)S(1)} %get-tuple-element.38), channel_id=1, source_target_pairs={{0,64},{32,96},{64,128},{96,160},{128,192},{160,224},{192,0},{224,... | collective-permute-start | bytes 1032200 | tf_op jit(solution)/shard_map/ppermute | solution.py:417
  110.7 11.4 %collective-permute-start.15 = (bf16[84,16,128]{2,1,0:T(8,128)(2,1)S(1)}, bf16[84,16,128]{2,1,0:T(8,128)(2,1)S(1)}, u32[]{:S(2)}, u32[]{:S(2)}) collective-permute-start(bf16[84,16,128]{2,1,0:T(8,128)(2,1)S(1)} %get-tuple-element.39), channel_id=1, source_target_pairs={{0,192},{32,224},{64,0},{96,32},{128,64},{160,96},{192,128},{224,1... | collective-permute-start | bytes 1032200 | tf_op jit(solution)/shard_map/ppermute | solution.py:417
  114.1 15.2 %collective-permute-start.19 = (bf16[84,16,128]{2,1,0:T(8,128)(2,1)S(1)}, bf16[84,16,128]{2,1,0:T(8,128)(2,1)S(1)}, u32[]{:S(2)}, u32[]{:S(2)}) collective-permute-start(bf16[84,16,128]{2,1,0:T(8,128)(2,1)S(1)} %get-tuple-element.46), channel_id=1, source_target_pairs={{0,64},{32,96},{64,128},{96,160},{128,192},{160,224},{192,0},{224,... | collective-permute-start | bytes 1032200 | tf_op jit(solution)/shard_map/ppermute | solution.py:417
  114.4 15.0 %collective-permute-start.20 = (bf16[84,16,128]{2,1,0:T(8,128)(2,1)S(1)}, bf16[84,16,128]{2,1,0:T(8,128)(2,1)S(1)}, u32[]{:S(2)}, u32[]{:S(2)}) collective-permute-start(bf16[84,16,128]{2,1,0:T(8,128)(2,1)S(1)} %get-tuple-element.47), channel_id=1, source_target_pairs={{0,192},{32,224},{64,0},{96,32},{128,64},{160,96},{192,128},{224,1... | collective-permute-start | bytes 1032200 | tf_op jit(solution)/shard_map/ppermute | solution.py:417
  159.8 7.4 %collective-permute-start.22 = (bf16[84,16,128]{2,1,0:T(8,128)(2,1)S(1)}, bf16[84,16,128]{2,1,0:T(8,128)(2,1)S(1)}, u32[]{:S(2)}, u32[]{:S(2)}) collective-permute-start(bf16[84,16,128]{2,1,0:T(8,128)(2,1)S(1)} %bitcast.26), channel_id=1, source_target_pairs={{0,64},{32,96},{64,128},{96,160},{128,192},{160,224},{192,0},{224,... | collective-permute-start | bytes 1032200 | tf_op jit(solution)/shard_map/ppermute | solution.py:417
  159.9 7.4 %collective-permute-start.25 = (bf16[84,16,128]{2,1,0:T(8,128)(2,1)S(1)}, bf16[84,16,128]{2,1,0:T(8,128)(2,1)S(1)}, u32[]{:S(2)}, u32[]{:S(2)}) collective-permute-start(bf16[84,16,128]{2,1,0:T(8,128)(2,1)S(1)} %bitcast.27), channel_id=1, source_target_pairs={{0,192},{32,224},{64,0},{96,32},{128,64},{160,96},{192,128},{224,1... | collective-permute-start | bytes 1032200 | tf_op jit(solution)/shard_map/ppermute | solution.py:417
  167.2 11.3 %collective-permute-start.24 = (bf16[42,16,128]{2,1,0:T(8,128)(2,1)S(1)}, bf16[42,16,128]{2,1,0:T(8,128)(2,1)S(1)}, u32[]{:S(2)}, u32[]{:S(2)}) collective-permute-start(bf16[42,16,128]{2,1,0:T(8,128)(2,1)S(1)} %slice.54), channel_id=1, source_target_pairs={{0,64},{32,96},{64,128},{96,160},{128,192},{160,224},{192,0},{224,... | collective-permute-start | bytes 516104 | tf_op jit(solution)/shard_map/ppermute | solution.py:417
  167.3 11.2 %collective-permute-start.26 = (bf16[42,16,128]{2,1,0:T(8,128)(2,1)S(1)}, bf16[42,16,128]{2,1,0:T(8,128)(2,1)S(1)}, u32[]{:S(2)}, u32[]{:S(2)}) collective-permute-start(bf16[42,16,128]{2,1,0:T(8,128)(2,1)S(1)} %slice.55), channel_id=1, source_target_pairs={{0,192},{32,224},{64,0},{96,32},{128,64},{160,96},{192,128},{224,1... | collective-permute-start | bytes 516104 | tf_op jit(solution)/shard_map/ppermute | solution.py:417
  170.0 11.1 %collective-permute-start.21 = (bf16[84,16,128]{2,1,0:T(8,128)(2,1)S(1)}, bf16[84,16,128]{2,1,0:T(8,128)(2,1)S(1)}, u32[]{:S(2)}, u32[]{:S(2)}) collective-permute-start(bf16[84,16,128]{2,1,0:T(8,128)(2,1)S(1)} %bitcast.28), channel_id=1, source_target_pairs={{0,32},{32,0},{64,96},{96,64},{128,160},{160,128},{192,224},{224,1... | collective-permute-start | bytes 1032200 | tf_op jit(solution)/shard_map/ppermute | solution.py:437
  177.9 3.1 %collective-permute-start.28 = (bf16[84,16,128]{2,1,0:T(8,128)(2,1)S(1)}, bf16[84,16,128]{2,1,0:T(8,128)(2,1)S(1)}, u32[]{:S(2)}, u32[]{:S(2)}) collective-permute-start(bf16[84,16,128]{2,1,0:T(8,128)(2,1)S(1)} %collective-permute-done.25.refs_6_), channel_id=1, source_target_pairs={{0,32},{32,0},{64,96},{96,64},{128,160},{160,128},{192,224},{224,1... | collective-permute-start | bytes 1032200 | tf_op jit(solution)/shard_map/ppermute | solution.py:437
  178.5 3.8 %collective-permute-start.27 = (bf16[84,16,128]{2,1,0:T(8,128)(2,1)S(1)}, bf16[84,16,128]{2,1,0:T(8,128)(2,1)S(1)}, u32[]{:S(2)}, u32[]{:S(2)}) collective-permute-start(bf16[84,16,128]{2,1,0:T(8,128)(2,1)S(1)} %constant_dynamic-update-slice_fusion.refs_4_), channel_id=1, source_target_pairs={{0,32},{32,0},{64,96},{96,64},{128,160},{160,128},{192,224},{224,1... | collective-permute-start | bytes 1032200 | tf_op jit(solution)/shard_map/ppermute | solution.py:437
  (20 other events, 431.8 us)
Sparse Core Ops, SparseCore 0:
  43.8 41.3 all-gather.2
  98.6 31.0 reduce-scatter.2
  160.0 32.8 reduce-scatter.4
